TPU v7x, 32 devices: a whole 2x2x4 slice. The times are simulated.
32 devices in a mesh: region: 4 (over z), tile: 8 (over y, x, core).
Axes of the slice: x: 2, y: 2, z: 4, core: 2. Of those that a mesh axis runs over, the one named last changes fastest.
Arguments:
- offsets: float32 [2, 131072], P(None, ('region', 'tile')), may hold values from 0 to 1
- design: float32 [2, 131072], P(None, ('region', 'tile')), may hold values from -4 to 4
- target: float32 [131072], P(('region', 'tile')), may hold values from -6 to 6
- beta_second: float32 [131072], P(('region', 'tile')), may hold values from -3 to 3
- counts: int32 [512], P(('region', 'tile')), may hold values from 1 to 256, as said below
- kernel_width: int32 [2, 512], P(None, ('region', 'tile')), may hold values from 2 to 8
- reach: int32 [2, 512, 9], P(None, ('region', 'tile')), may hold values 0 or 1
- assignment: int32 [4, 128], P('region', 'tile'), may hold values from 0 to 127, each once within a row
Outputs:
- betas: float32 [2, 131072], P(None, ('region', 'tile'))
- hats: float32 [2, 131072], P(None, ('region', 'tile'))
- residual: float32 [131072], P(('region', 'tile'))
Inputs may be any that keep to these rules, and one draw needn't show every extreme that they name: `counts`: some tile holds 256 live records in every draw.
All inputs are finite; a program needn't handle non-finite values. No bound on the sum of `reach` on one device may be relied on, other than what follows from the above.
Results may differ from a plain program's by a relative error of at most 0.0003.
Values sent between devices are 32-bit elements; how exact they have to be, the bound alone decides.
No kernel may reach another device: no remote copies, remote signals or barrier semaphores. Data moves between devices by JAX's collectives and lax.ppermute only.
A program may use at most 64 MiB of HBM per device.

v0:
```python
import functools

import jax
import jax.numpy as jnp
from jax import lax
from jax.experimental import pallas as pl
from jax.experimental.pallas import tpu as pltpu
from jax.sharding import PartitionSpec as P

TILE = 256
TX = 4
LANES = 128
TWO, EAST, NORTH, ONE, PART, PRICE, INFO = range(7)
SLOTS = 16
BASE = 32.0 * 1.4426950408889634
LABEL, COUNT, WIDTH, REACH = 0, 1, 2, 3
NEAR = [(a, b) for a in (-1, 0, 1) for b in (-1, 0, 1)]
F32, I32 = jnp.float32, jnp.int32
ANY = pl.BlockSpec(memory_space=pl.ANY)
SMEM = pl.BlockSpec(memory_space=pltpu.SMEM)
VMEM = pl.BlockSpec(memory_space=pltpu.VMEM)


def prepare_kernel(*refs):
    given, (out, mine), held, sem = refs[:8], refs[8:10], refs[10:18], refs[18]
    copies = [pltpu.make_async_copy(a, b, sem) for a, b in zip(given, held)]
    for copy in copies:
        copy.start()
    for copy in copies:
        copy.wait()
    off, des, tgt, sec, counts, widths, reach, cells = held
    lane = lax.broadcasted_iota(I32, (1, LANES), 1)
    packed = []
    for t in range(counts.shape[0]):
        row = jnp.zeros((1, LANES), F32)
        facts = [cells[0, t], counts[t], widths[0, t]] + [reach[e, 0, t] for e in range(9)]
        for k, fact in enumerate(facts):
            row = jnp.where(lane == k, fact.astype(F32), row)
        out[INFO, 0, t : t + 1, :] = row
        facts[WIDTH:] = [widths[1, t]] + [reach[e, 1, t] for e in range(9)]
        for k, fact in enumerate(facts + [jnp.int32(0)] * 4):
            mine[t * SLOTS + k] = fact
        packed.append(row)
        for h in range(2):
            at = slice(t * TILE + h * LANES, t * TILE + (h + 1) * LANES)
            live = lane + h * LANES < counts[t]
            one = jnp.where(live, des[0:1, at], 0.0)
            two = jnp.where(live, des[1:2, at], 0.0)
            price = tgt[0:1, at]
            out[EAST, h, t : t + 1, :] = off[0:1, at] - 0.5
            out[NORTH, h, t : t + 1, :] = off[1:2, at] - 0.5
            out[ONE, h, t : t + 1, :] = one
            out[PART, h, t : t + 1, :] = one * (price - two * sec[0:1, at])
            out[TWO, h, t : t + 1, :] = two
            out[PRICE, h, t : t + 1, :] = price
    for t in range(8):
        out[INFO, 1, t : t + 1, :] = packed[t] + pltpu.roll(packed[t + 8], LANES // 2, 1)
    out[INFO, 1, 8:16, :] = jnp.zeros((8, LANES), F32)


def split(number, size):
    return number >> (size.bit_length() - 1), number & (size - 1)


def fact(facts, number, k):
    block, slot = split(number, SLOTS)
    return facts[block, slot & 7, ((slot >> 3) << 6) + k]


def fetch(same, other, table, fields, sem):
    half = same.shape[0]
    return [
        pltpu.make_async_copy(
            held.at[:, pl.ds(0, fields)], table.at[pl.ds(side * half, half)], sem
        )
        for side, held in enumerate((same, other))
    ]


def fetch_facts(same, other, facts, sem):
    half = same.shape[0]
    return [
        pltpu.make_async_copy(held.at[:, INFO, 1, pl.ds(0, 8)], facts.at[pl.ds(side * half, half)], sem)
        for side, held in enumerate((same, other))
    ]


def invert(facts, inverse, number, cells):
    def step(s, carry):
        cell = fact(facts, s, LABEL).astype(I32)
        inverse[cell] = s
        number[cell] = fact(facts, s, COUNT).astype(I32)
        return carry

    lax.fori_loop(0, cells, step, 0, unroll=8)


def border_kernel(same, other, out, inverse, number, table, facts, sem, fact_sem):
    copies = fetch(same, other, table, 7, sem)
    fact_copies = fetch_facts(same, other, facts, fact_sem)
    for copy in fact_copies + copies:
        copy.start()
    for copy in fact_copies:
        copy.wait()
    cells = inverse.shape[0]
    rows = cells // TX
    per_pair = 8
    invert(facts, inverse, number, cells)
    for copy in copies:
        copy.wait()
    me = lax.axis_index("tile")
    odd = me & 1
    first = (me >> 1) * per_pair
    order = [(0, r) for r in range(1, 9)] + [(1, r) for r in range(1, 9)]
    order += [(0, 0), (0, 9), (1, 0), (1, 9)]
    for i, (away, r) in enumerate(order):
        column = jnp.where(odd == 1, away, TX - 1 - away)
        row = jnp.clip(first + r - 1, 0, rows - 1)
        source = inverse[column * rows + row]
        source = split(source, SLOTS)
        for f, field in enumerate((EAST, NORTH, ONE, PART, INFO)):
            out[:, f * 24 + i : f * 24 + i + 1, :] = row_of(table, field, source)
        if i < 8:
            for f, field in enumerate((TWO, PRICE)):
                out[:, 120 + 8 * f + i : 121 + 8 * f + i, :] = row_of(table, field, source)
    for f in range(5):
        out[:, f * 24 + 20 : f * 24 + 24, :] = jnp.zeros((2, 4, LANES), F32)


def row_of(table, field, source):
    return table[source[0], field, :, pl.ds(source[1], 1), :]


def records(tiles):
    shape = (2, tiles, LANES)
    number = lax.broadcasted_iota(I32, shape, 2) + LANES * lax.broadcasted_iota(I32, shape, 0)
    return number.astype(F32)


def columns_of(rows):
    pad = jnp.zeros((64 - rows.shape[1], LANES), F32)
    return jnp.concatenate([rows[0], pad, rows[1], pad], axis=0).T


def rows_of(columns, tiles):
    flat = columns.T
    return jnp.stack([flat[:tiles], flat[64 : 64 + tiles]])


def blocks_in(number):
    return (number + 63) >> 6


def spread_columns(tiles, number_of, east, north, columns):
    def lay(t, nb, values):
        i = (nb >> 1) * 64 + t
        for k, value in enumerate(values):
            wide = jnp.broadcast_to(value[:, i : i + 1], (64, LANES))
            columns[t, k, nb * 64 : nb * 64 + 64, :] = wide

    low = (east[0:64, :], north[0:64, :])
    for t in range(tiles):
        lay(t, 0, low)
    for t in range(tiles):
        number = number_of(t)

        @pl.when(number > 64)
        def _():
            lay(t, 1, (east[64:128, :], north[64:128, :]))

        @pl.when(number > 128)
        def _():
            lay(t, 2, (east[0:64, :], north[0:64, :]))
            lay(t, 3, (east[64:128, :], north[64:128, :]))


def collect_sums(tiles, number_of, sums, den_ref, num_ref):
    lane = lax.broadcasted_iota(I32, (64, LANES), 1)
    ones = jnp.ones((LANES, LANES), jnp.bfloat16)

    def total(values):
        high = values.astype(jnp.bfloat16)
        low = (values - high.astype(F32)).astype(jnp.bfloat16)
        return jnp.dot(high, ones, preferred_element_type=F32) + jnp.dot(
            low, ones, preferred_element_type=F32
        )

    zero = jnp.zeros((64, LANES), F32)
    for k, held in enumerate((den_ref, num_ref)):
        for nb in range(2):
            result = zero
            for t in range(tiles):
                x = total(sums[t, k, nb * 64 : nb * 64 + 64, :])
                result = jnp.where(lane == t, x, result)
            held[nb * 64 : nb * 64 + 64, :] = result

    def rest(t, carry):
        @pl.when(number_of(t) > 128)
        def _():
            for k, held in enumerate((den_ref, num_ref)):
                x = total(sums[t, k, 128:256, :])
                mine = lax.broadcasted_iota(I32, (128, LANES), 1) == 64 + t
                held[...] = jnp.where(mine, x, held[...])

        return carry

    lax.fori_loop(0, tiles, rest, 0)


STEP = 4


def sweep_tile(t, number, used, scale, columns, sums, table, part, cov, lists):
    words, steps = lists
    scale = jnp.broadcast_to(scale, (8, LANES))

    def block(nb, carry):
        at = pl.ds(pl.multiple_of(nb * 64, 64), 64)
        x = columns[t, 0, at, :].reshape(8, 8, LANES)
        y = columns[t, 1, at, :].reshape(8, 8, LANES)

        def some(p, sums_now):
            den, num = sums_now
            for k in range(STEP):
                i = STEP * p + k
                word = words[i]
                n, slot = split(word & 0xFFFF, SLOTS)
                row = pl.ds(slot, 1)
                h = (word >> 16) & 1
                e = word >> 20

                def wide(values):
                    return jnp.broadcast_to(values, (8, LANES))

                u = wide(table[n, EAST, h, row, :]) + steps[e]
                v = wide(table[n, NORTH, h, row, :]) + steps[9 + e]
                c = wide(table[n, cov, h, row, :])
                d = wide(part(i, n, h, row))
                q = scale * (u * u + v * v)
                w = jnp.exp2(x * u + y * v - q)
                den = den + w * (c * c)
                num = num + w * d
            return den, num

        zero = jnp.zeros((8, 8, LANES), F32)
        den, num = lax.fori_loop(0, (used + STEP - 1) // STEP, some, (zero, zero))
        sums[t, 0, at, :] = den.reshape(64, LANES)
        sums[t, 1, at, :] = num.reshape(64, LANES)
        return carry

    lax.fori_loop(0, blocks_in(number), block, 0)


def set_steps(steps):
    for e, (a, b) in enumerate(NEAR):
        steps[e] = jnp.float32(a)
        steps[9 + e] = jnp.float32(b)


def chunks_in(number):
    return (number > 0).astype(I32) + (number > LANES).astype(I32)


def first_kernel(
    inverse, number, same, other, border, out,
    table, own, scales, numbers, east, north, dens, nums, columns, sums,
    facts, border_facts, window, live, chunks, words, steps, sem, fact_sem,
):
    copies = fetch(same, other, table, 6, sem)
    fact_copies = fetch_facts(same, other, facts, fact_sem)
    cells = inverse.shape[0]
    rows = cells // TX
    blocks = cells // SLOTS
    empty = cells + 20
    for f, field in enumerate((EAST, NORTH, ONE, PART, INFO)):
        for k, size in enumerate((16, 8)):
            held = pl.ds(f * 24 + 16 * k, size)
            if field == INFO:
                to = border_facts.at[pl.ds(16 * k, size)]
                fact_copies.append(pltpu.make_async_copy(border.at[0, held], to, fact_sem))
            else:
                to = table.at[blocks + k, field, :, pl.ds(0, size)]
                copies.append(pltpu.make_async_copy(border.at[:, held], to, sem))
    for f, field in enumerate((TWO, PRICE)):
        to = table.at[blocks, field, :, pl.ds(0, 8)]
        copies.append(pltpu.make_async_copy(border.at[:, pl.ds(120 + 8 * f, 8)], to, sem))
    for copy in fact_copies + copies:
        copy.start()
    for copy in fact_copies:
        copy.wait()
    me = lax.axis_index("tile")
    odd = me & 1
    first = (me >> 1) * 8
    toward = 1 - 2 * odd
    order = [(0, r) for r in range(1, 9)] + [(1, r) for r in range(1, 9)]
    order += [(0, 0), (0, 9), (1, 0), (1, 9)]
    for u in range(5):
        for r in range(10):
            row = first + r - 1
            if u < 2:
                i = order.index((1 - u, r))
                source = cells + i
                held = border_facts[i, COUNT].astype(I32)
            else:
                column = jnp.where(odd == 1, 5 - u, u - 2)
                cell = column * rows + jnp.clip(row, 0, rows - 1)
                source = inverse[cell]
                held = number[cell]
            if r in (0, 9):
                held = jnp.where((row >= 0) & (row < rows), held, 0)
            window[u * 10 + r] = source
            live[u * 10 + r] = held
            chunks[u * 10 + r] = chunks_in(held)
    for copy in copies:
        copy.wait()
    tiles = 24

    def target_fact(t, target, k):
        inner = fact(facts, jnp.minimum(target, cells - 1), k)
        return jnp.where(t < 8, border_facts[jnp.minimum(t, 7), k], inner)

    def gather(t, carry):
        place = ((t >> 3) + 1) * 10 + (t & 7) + 1
        target = window[place]
        at = split(target, SLOTS)
        width = jnp.full((1, LANES), target_fact(t, target, WIDTH), F32)
        scales[pl.ds(t, 1), :] = BASE / (width * width)
        numbers[pl.ds(t, 1), :] = jnp.full((1, LANES), live[place].astype(F32), F32)
        for field in range(6):
            own[field, :, pl.ds(t, 1), :] = row_of(table, field, at)
        return carry

    lax.fori_loop(0, tiles, gather, 0, unroll=2)
    set_steps(steps)
    present = records(tiles) < numbers[...][None]
    scale_rows = scales[...][None]
    x, y = own[EAST], own[NORTH]
    east[...] = columns_of(2.0 * scale_rows * x)
    north[...] = columns_of(2.0 * scale_rows * y)
    dens[...] = jnp.zeros_like(dens)
    nums[...] = jnp.zeros_like(nums)

    def number_of(t):
        return live[((t >> 3) + 1) * 10 + (t & 7) + 1]

    spread_columns(tiles, number_of, east, north, columns)

    def each(t, carry):
        u = (t >> 3) + 1
        r = (t & 7) + 1
        target = window[u * 10 + r]
        number = live[u * 10 + r]
        used = jnp.int32(0)
        for e, (a, b) in enumerate(NEAR):
            place = (u + toward * a) * 10 + r + b
            word = window[place] + (e << 20)
            more = chunks[place]
            if e != 4:
                more = jnp.where(target_fact(t, target, REACH + e) > 0.5, more, 0)
            words[used] = word
            words[used + 1] = word + (1 << 16)
            used = used + more
        for k in range(STEP - 1):
            words[used + k] = jnp.int32(empty)
        lists = (words, steps)
        sweep_tile(
            t, number, used, scales[pl.ds(t, 1), :], columns, sums, table,
            lambda i, n, h, row: table[n, PART, h, row, :], ONE, lists,
        )
        return carry

    lax.fori_loop(0, tiles, each, 0)
    collect_sums(tiles, number_of, sums, dens, nums)
    shrink = jnp.exp2(-scale_rows * (x * x + y * y))
    inv = 1.0 / (1.0 + shrink * rows_of(dens[...], tiles))
    beta = jnp.where(present, shrink * rows_of(nums[...], tiles) * inv, 0.0)
    one, two = own[ONE], own[TWO]
    out[:, 0:24, :] = two * (own[PRICE] - one * beta)
    out[:, 24:40, :] = beta[:, 8:24]
    out[:, 40:56, :] = (one * one * inv)[:, 8:24]
    out[:, 56:64, :] = two[:, 0:8]
    out[:, 64:72, :] = x[:, 0:8]
    out[:, 72:80, :] = y[:, 0:8]
    out[:, 80:88, :] = jnp.broadcast_to(numbers[0:8, :][None], (2, 8, LANES))


def second_kernel(
    inverse, number, own_block, same, other, same_b, other_b, mine,
    betas, hats, residual,
    table, results, own, scales, numbers, east, north, dens, nums, columns, sums,
    border_facts, words, steps, spots, sem, fact_sem,
):
    copies = fetch(same, other, table, 3, sem)
    fact_copies = []
    half, _, _, tiles, _ = same.shape
    cells = inverse.shape[0]
    rows = cells // TX
    blocks = cells // SLOTS
    empty = cells + 2 * half * 8
    for side, held in enumerate((same_b, other_b)):
        at = pl.ds(side * half, half)
        copies.append(pltpu.make_async_copy(held, results.at[at, :, pl.ds(0, 88)], sem))
        fact_copies.append(
            pltpu.make_async_copy(held.at[:, 0, pl.ds(80, 8)], border_facts.at[at], fact_sem)
        )
    for copy in fact_copies + copies:
        copy.start()
    for t in range(tiles):
        width = jnp.full((1, LANES), mine[t * SLOTS + WIDTH].astype(F32), F32)
        scales[t : t + 1, :] = BASE / (width * width)
        numbers[t : t + 1, :] = jnp.full((1, LANES), mine[t * SLOTS + COUNT].astype(F32), F32)
    present = records(tiles) < numbers[...][None]
    scale_rows = scales[...][None]
    x, y = own_block[EAST], own_block[NORTH]
    east[...] = columns_of(2.0 * scale_rows * x)
    north[...] = columns_of(2.0 * scale_rows * y)
    dens[...] = jnp.zeros_like(dens)
    nums[...] = jnp.zeros_like(nums)

    def number_of(t):
        return mine[t * SLOTS + COUNT]

    spread_columns(tiles, number_of, east, north, columns)
    for copy in fact_copies:
        copy.wait()
    me = lax.axis_index("tile")
    for copy in copies:
        copy.wait()

    def lay(n, carry):
        at = pl.ds(pl.multiple_of((n & 1) * 8, 8), 8)
        for field in range(3):
            held = results[n, :, 56 + 8 * field : 64 + 8 * field, :]
            table[blocks + (n >> 1), field, :, at, :] = held
        return carry

    lax.fori_loop(0, 2 * half, lay, 0)
    for field in range(3):
        table[blocks + half, field, :, 0:8, :] = jnp.zeros((2, 8, LANES), F32)
    results[0, :, 88:96, :] = jnp.zeros((2, 8, LANES), F32)

    set_steps(steps)

    def place(low, depth, upper, r):
        k = (upper + 1 - low) ^ me
        n = (k & 1) * half + (k >> 1)
        return n, depth * 8 + r

    def side(column):
        low = (column < TX // 2).astype(I32)
        return low, jnp.where(low == 1, column + 1, TX - column)

    def each(t, carry):
        column, across = split(mine[t * SLOTS + LABEL], rows)
        used = jnp.int32(0)
        sides = [(column + a, *side(column + a)) for a in (-1, 0, 1)]
        lines = []
        for b in (-1, 0, 1):
            row = jnp.clip(across + b, 0, rows - 1)
            lines.append((row, row == across + b, (row >> 3) * 2, row & 7))
        for e, (a, b) in enumerate(NEAR):
            col, low, depth = sides[a + 1]
            row, inside, upper, r = lines[b + 1]
            n, at = place(low, depth, upper, r)
            in_strip = (col >= 0) & (col < TX)
            near = jnp.clip(col, 0, TX - 1) * rows + row
            source = jnp.where(in_strip, inverse[near], cells + n * 8 + r)
            live = jnp.where(in_strip, number[near], border_facts[n, r, 0].astype(I32))
            more = chunks_in(live)
            if e != 4:
                more = jnp.where(inside, more * mine[t * SLOTS + REACH + e], 0)
            word = source + (e << 20)
            words[used] = word
            words[used + 1] = word + (1 << 16)
            spots[used] = (n << 8) + at
            spots[used + 1] = (n << 8) + at
            used = used + more
        for k in range(STEP - 1):
            words[used + k] = jnp.int32(empty)
            spots[used + k] = jnp.int32(88)
        lists = (words, steps)
        n, at = place(*sides[1][1:], *lines[1][2:])
        own[0, :, pl.ds(t, 1), :] = results[n, :, pl.ds(16 + at, 1), :]
        own[1, :, pl.ds(t, 1), :] = results[n, :, pl.ds(32 + at, 1), :]

        def part(i, n, h, row):
            n, at = split(spots[i], 256)
            return results[n, h, pl.ds(at, 1), :]

        sweep_tile(
            t, mine[t * SLOTS + COUNT], used, scales[pl.ds(t, 1), :], columns, sums, table,
            part, TWO, lists,
        )
        return carry

    lax.fori_loop(0, tiles, each, 0)
    collect_sums(tiles, number_of, sums, dens, nums)
    shrink = jnp.exp2(-scale_rows * (x * x + y * y))
    inv = 1.0 / (1.0 + shrink * rows_of(dens[...], tiles))
    beta_two = jnp.where(present, shrink * rows_of(nums[...], tiles) * inv, 0.0)
    beta_one = own[0]
    one, two = own_block[ONE], own_block[TWO]
    left = jnp.where(present, own_block[PRICE] - one * beta_one - two * beta_two, 0.0)
    hat_two = two * two * inv
    for t in range(tiles):
        for h in range(2):
            at = slice(t * TILE + h * LANES, t * TILE + (h + 1) * LANES)
            betas[0:1, at] = beta_one[h, t : t + 1]
            betas[1:2, at] = beta_two[h, t : t + 1]
            hats[0:1, at] = own[1, h, t : t + 1, :]
            hats[1:2, at] = hat_two[h, t : t + 1]
            residual[0:1, at] = left[h, t : t + 1]


def swap(x, k):
    count = lax.axis_size("tile")
    return lax.ppermute(x, "tile", [(i, i ^ k) for i in range(count)])


def spread(block):
    count = lax.axis_size("tile")
    same = jnp.stack([block] + [swap(block, k) for k in range(2, count, 2)])
    return same, swap(same, 1)


def body(offsets, design, target, beta_second, counts, kernel_width, reach, assignment):
    tiles = counts.shape[0]
    count = lax.axis_size("tile")
    regions = lax.axis_size("region")
    cells = tiles * count
    limit = pltpu.CompilerParams(vmem_limit_bytes=48 * 1024 * 1024)
    price = target.reshape(1, -1)
    wide = tiles * TILE
    given = (
        offsets, design, price, beta_second.reshape(1, -1),
        counts, kernel_width, reach.transpose(2, 0, 1), assignment,
    )
    block, mine = pl.pallas_call(
        prepare_kernel,
        out_shape=(
            pltpu.VMEM((7, 2, tiles, LANES), F32),
            jax.ShapeDtypeStruct((tiles * SLOTS,), I32),
        ),
        in_specs=[pl.BlockSpec(memory_space=pltpu.HBM)] * 8,
        out_specs=(VMEM, SMEM),
        scratch_shapes=[pltpu.VMEM((2, wide), F32)] * 2
        + [pltpu.VMEM((1, wide), F32)] * 2
        + [
            pltpu.SMEM((tiles,), I32),
            pltpu.SMEM((2, tiles), I32),
            pltpu.SMEM((9, 2, tiles), I32),
            pltpu.SMEM((1, tiles), I32),
            pltpu.SemaphoreType.DMA,
        ],
        compiler_params=limit,
    )(*[pltpu.with_memory_space_constraint(x, pltpu.HBM) for x in given])
    same, other = spread(block)
    dma = pltpu.SemaphoreType.DMA
    edge, inverse, number = pl.pallas_call(
        border_kernel,
        out_shape=(
            jax.ShapeDtypeStruct((2, 136, LANES), F32),
            jax.ShapeDtypeStruct((cells,), I32),
            jax.ShapeDtypeStruct((cells,), I32),
        ),
        in_specs=[ANY, ANY],
        out_specs=(VMEM, SMEM, SMEM),
        scratch_shapes=[
            pltpu.VMEM((count, 7, 2, tiles, LANES), F32),
            pltpu.SMEM((count, 8, LANES), F32),
            dma,
            dma,
        ],
        compiler_params=limit,
    )(same, other)
    moves = []
    for r in range(regions):
        for t in range(count):
            to = r + 1 - 2 * (t % 2)
            if 0 <= to < regions:
                moves.append((r * count + t, to * count + t))
    border = lax.ppermute(edge, ("region", "tile"), moves)
    square = pltpu.VMEM((LANES, LANES), F32)
    lists = [pltpu.SMEM((24,), I32), pltpu.SMEM((18,), F32)]
    first = pl.pallas_call(
        first_kernel,
        out_shape=jax.ShapeDtypeStruct((2, 88, LANES), F32),
        in_specs=[SMEM, SMEM, ANY, ANY, ANY],
        out_specs=VMEM,
        scratch_shapes=[
            pltpu.VMEM((count + 2, 6, 2, tiles, LANES), F32),
            pltpu.VMEM((6, 2, 24, LANES), F32),
            pltpu.VMEM((24, LANES), F32),
            pltpu.VMEM((24, LANES), F32),
            square,
            square,
            square,
            square,
            pltpu.VMEM((24, 2, TILE, LANES), F32),
            pltpu.VMEM((24, 2, TILE, LANES), F32),
            pltpu.SMEM((count, 8, LANES), F32),
            pltpu.SMEM((24, LANES), F32),
            *[pltpu.SMEM((56,), I32)] * 3,
            *lists,
            dma,
            dma,
        ],
        compiler_params=limit,
    )(inverse, number, same, other, border)
    same_b, other_b = spread(first)
    betas, hats, residual = pl.pallas_call(
        second_kernel,
        out_shape=(
            jax.ShapeDtypeStruct((2, wide), F32),
            jax.ShapeDtypeStruct((2, wide), F32),
            jax.ShapeDtypeStruct((1, wide), F32),
        ),
        in_specs=[SMEM, SMEM, VMEM, ANY, ANY, ANY, ANY, SMEM],
        out_specs=(VMEM, VMEM, VMEM),
        scratch_shapes=[
            pltpu.VMEM((count + count // 2 + 1, 3, 2, tiles, LANES), F32),
            pltpu.VMEM((count, 2, 96, LANES), F32),
            pltpu.VMEM((2, 2, tiles, LANES), F32),
            pltpu.VMEM((tiles, LANES), F32),
            pltpu.VMEM((tiles, LANES), F32),
            square,
            square,
            square,
            square,
            pltpu.VMEM((tiles, 2, TILE, LANES), F32),
            pltpu.VMEM((tiles, 2, TILE, LANES), F32),
            pltpu.SMEM((count, 8, LANES), F32),
            *lists,
            pltpu.SMEM((24,), I32),
            dma,
            dma,
        ],
        compiler_params=limit,
    )(inverse, number, block, same, other, same_b, other_b, mine)
    return (betas, hats, residual.reshape(-1))


def solution(mesh):
    in_specs = (
        P(None, ("region", "tile")),
        P(None, ("region", "tile")),
        P(("region", "tile")),
        P(("region", "tile")),
        P(("region", "tile")),
        P(None, ("region", "tile")),
        P(None, ("region", "tile"), None),
        P("region", "tile"),
    )
    out_specs = (P(None, ("region", "tile")), P(None, ("region", "tile")), P(("region", "tile")))
    return jax.shard_map(body, mesh=mesh, in_specs=in_specs, out_specs=out_specs, check_vma=False)
```

profile of v0, /device:TPU:25, one launch (start us, length us, event | category | flops | bytes accessed | tf_op | source)
XLA Modules:
  0.0 61.7 jit_solution(8646346321187436551)
XLA Ops:
  0.6 1.8 %shard_map.103 = (f32[7,2,16,128]{3,2,1,0:T(8,128)S(1)}, s32[256]{0:T(256)S(1)}) custom-call(f32[2,4096]{1,0:T(2,128)} %refs_0_.1, f32[2,4096]{1,0:T(2,128)} %refs_1_.1, f32[1,4096]{1,0:T(1,128)} %bitcast.20, f32[1,4096]{1,0:T(1,128)} %bitcast.21, s32[16]{0:T(128)} %refs_4_.1, s32[2,16]{1,0:T(2,128)} %refs_5_.1, s32[9,2,16]{2,1,0:T(2,128)} %bitcast.22, ...), custom_call_target="tpu_custom_call" | custom-call | tf_op jit(solution)/shard_map/pallas_call | solution.py:538
  2.5 2.2 %collective-permute-start.2 = (f32[7,2,16,128]{3,2,1,0:T(8,128)S(1)}, f32[7,2,16,128]{3,2,1,0:T(8,128)S(1)}, u32[]{:S(2)}, u32[]{:S(2)}) collective-permute-start(f32[7,2,16,128]{3,2,1,0:T(8,128)S(1)} %get-tuple-element.11.own_block), channel_id=1, source_target_pairs={{0,6},{1,7},{2,4},{3,5},{4,2},{5,3},{6,0},{7,1},{8,14},{9,15},{10,... | collective-permute-start | bytes 344072 | tf_op jit(solution)/shard_map/ppermute | solution.py:517
  4.7 0.2 collective-permute-start.1
  4.9 0.3 collective-permute-start
  5.2 2.3 %collective-permute-done.2 = f32[7,2,16,128]{3,2,1,0:T(8,128)S(1)} collective-permute-done((f32[7,2,16,128]{3,2,1,0:T(8,128)S(1)}, f32[7,2,16,128]{3,2,1,0:T(8,128)S(1)}, u32[]{:S(2)}, u32[]{:S(2)}) %collective-permute-start.2) | collective-permute-done | bytes 114720 | tf_op jit(solution)/shard_map/ppermute | solution.py:517
  7.4 3.4 %collective-permute-done.1 = f32[7,2,16,128]{3,2,1,0:T(8,128)S(1)} collective-permute-done((f32[7,2,16,128]{3,2,1,0:T(8,128)S(1)}, f32[7,2,16,128]{3,2,1,0:T(8,128)S(1)}, u32[]{:S(2)}, u32[]{:S(2)}) %collective-permute-start.1) | collective-permute-done | bytes 114720 | tf_op jit(solution)/shard_map/ppermute | solution.py:517
  10.8 0.0 collective-permute-done
  10.9 0.7 %collective-permute-start.3 = (f32[4,7,2,16,128]{4,3,2,1,0:T(8,128)S(1)}, f32[4,7,2,16,128]{4,3,2,1,0:T(8,128)S(1)}, u32[]{:S(2)}, u32[]{:S(2)}) collective-permute-start(f32[4,7,2,16,128]{4,3,2,1,0:T(8,128)S(1)} %pad_maximum_fusion.same), channel_id=1, source_target_pairs={{0,1},{1,0},{2,3},{3,2},{4,5},{5,4},{6,7},{7,6},{8,9},{9,8},{10,11... | collective-permute-start | bytes 1376264 | tf_op jit(solution)/shard_map/ppermute | solution.py:517
  11.6 1.4 %collective-permute-done.3.other = f32[4,7,2,16,128]{4,3,2,1,0:T(8,128)S(1)} collective-permute-done((f32[4,7,2,16,128]{4,3,2,1,0:T(8,128)S(1)}, f32[4,7,2,16,128]{4,3,2,1,0:T(8,128)S(1)}, u32[]{:S(2)}, u32[]{:S(2)}) %collective-permute-start.3) | collective-permute-done | bytes 458784 | tf_op jit(solution)/shard_map/ppermute | solution.py:517
  13.0 3.0 %shard_map.104 = (f32[2,136,128]{2,1,0:T(8,128)S(1)}, s32[128]{0:T(128)S(1)}, s32[128]{0:T(128)S(1)}) custom-call(f32[4,7,2,16,128]{4,3,2,1,0:T(8,128)S(1)} %pad_maximum_fusion.same, f32[4,7,2,16,128]{4,3,2,1,0:T(8,128)S(1)} %collective-permute-done.3.other), custom_call_target="tpu_custom_call" | custom-call | tf_op jit(solution)/shard_map/pallas_call | solution.py:559
  16.1 2.1 %collective-permute-start.4 = (f32[2,136,128]{2,1,0:T(8,128)S(1)}, f32[2,136,128]{2,1,0:T(8,128)S(1)}, u32[]{:S(2)}, u32[]{:S(2)}) collective-permute-start(f32[2,136,128]{2,1,0:T(8,128)S(1)} %get-tuple-element.14), channel_id=1, source_target_pairs={{0,8},{2,10},{4,12},{6,14},{8,16},{9,1},{10,18},{11,3},{12,20},{13... | collective-permute-start | bytes 417800 | tf_op jit(solution)/shard_map/ppermute | solution.py:582
  18.2 2.0 %collective-permute-done.4.border = f32[2,136,128]{2,1,0:T(8,128)S(1)} collective-permute-done((f32[2,136,128]{2,1,0:T(8,128)S(1)}, f32[2,136,128]{2,1,0:T(8,128)S(1)}, u32[]{:S(2)}, u32[]{:S(2)}) %collective-permute-start.4) | collective-permute-done | bytes 139296 | tf_op jit(solution)/shard_map/ppermute | solution.py:582
  20.2 14.3 %shard_map.105 = f32[2,88,128]{2,1,0:T(8,128)S(1)} custom-call(s32[128]{0:T(128)S(1)} %get-tuple-element.12.inverse, s32[128]{0:T(128)S(1)} %get-tuple-element.13.number, f32[4,7,2,16,128]{4,3,2,1,0:T(8,128)S(1)} %pad_maximum_fusion.same, f32[4,7,2,16,128]{4,3,2,1,0:T(8,128)S(1)} %collective-permute-done.3.other, ...), custom_call_target="tpu_custom_call" | custom-call | tf_op jit(solution)/shard_map/pallas_call | solution.py:585
  34.5 0.1 collective-permute-start.7
  34.6 0.3 collective-permute-start.6
  34.9 2.3 %collective-permute-start.5 = (f32[2,88,128]{2,1,0:T(8,128)S(1)}, f32[2,88,128]{2,1,0:T(8,128)S(1)}, u32[]{:S(2)}, u32[]{:S(2)}) collective-permute-start(f32[2,88,128]{2,1,0:T(8,128)S(1)} %shard_map.105), channel_id=1, source_target_pairs={{0,2},{1,3},{2,0},{3,1},{4,6},{5,7},{6,4},{7,5},{8,10},{9,11},{10,... | collective-permute-start | bytes 270344 | tf_op jit(solution)/shard_map/ppermute | solution.py:517
  37.2 1.7 %collective-permute-done.7 = f32[2,88,128]{2,1,0:T(8,128)S(1)} collective-permute-done((f32[2,88,128]{2,1,0:T(8,128)S(1)}, f32[2,88,128]{2,1,0:T(8,128)S(1)}, u32[]{:S(2)}, u32[]{:S(2)}) %collective-permute-start.7) | collective-permute-done | bytes 90144 | tf_op jit(solution)/shard_map/ppermute | solution.py:517
  38.9 0.0 collective-permute-done.6
  39.0 0.1 collective-permute-done.5
  39.2 7.3 %collective-permute-start.8 = (f32[4,2,88,128]{3,2,1,0:T(8,128)S(1)}, f32[4,2,88,128]{3,2,1,0:T(8,128)S(1)}, u32[]{:S(2)}, u32[]{:S(2)}) collective-permute-start(f32[4,2,88,128]{3,2,1,0:T(8,128)S(1)} %pad_maximum_fusion.1.same_b), channel_id=1, source_target_pairs={{0,1},{1,0},{2,3},{3,2},{4,5},{5,4},{6,7},{7,6},{8,9},{9,8},{10,11... | collective-permute-start | bytes 1081352 | tf_op jit(solution)/shard_map/ppermute | solution.py:517
  46.4 1.3 %collective-permute-done.8.other_b = f32[4,2,88,128]{3,2,1,0:T(8,128)S(1)} collective-permute-done((f32[4,2,88,128]{3,2,1,0:T(8,128)S(1)}, f32[4,2,88,128]{3,2,1,0:T(8,128)S(1)}, u32[]{:S(2)}, u32[]{:S(2)}) %collective-permute-start.8) | collective-permute-done | bytes 360480 | tf_op jit(solution)/shard_map/ppermute | solution.py:517
  47.7 13.9 %shard_map.106 = (f32[2,4096]{1,0:T(2,128)}, f32[2,4096]{1,0:T(2,128)}, f32[1,4096]{1,0:T(1,128)}) custom-call(s32[128]{0:T(128)S(1)} %get-tuple-element.12.inverse, s32[128]{0:T(128)S(1)} %get-tuple-element.13.number, f32[7,2,16,128]{3,2,1,0:T(8,128)S(1)} %get-tuple-element.11.own_block, f32[4,7,2,16,128]{4,3,2,1,0:T(8,128)S(1)} %pad_maximum_fusion.same, ...), custom_call_target="tpu_custom_call" | custom-call | tf_op jit(solution)/shard_map/pallas_call | solution.py:611
  (2 shorter events, 0.1 us)
Async XLA Ops:
  2.5 5.0 %collective-permute-start.2 = (f32[7,2,16,128]{3,2,1,0:T(8,128)S(1)}, f32[7,2,16,128]{3,2,1,0:T(8,128)S(1)}, u32[]{:S(2)}, u32[]{:S(2)}) collective-permute-start(f32[7,2,16,128]{3,2,1,0:T(8,128)S(1)} %get-tuple-element.11.own_block), channel_id=1, source_target_pairs={{0,6},{1,7},{2,4},{3,5},{4,2},{5,3},{6,0},{7,1},{8,14},{9,15},{10,... | collective-permute-start | bytes 344072 | tf_op jit(solution)/shard_map/ppermute | solution.py:517
  4.7 6.1 %collective-permute-start.1 = (f32[7,2,16,128]{3,2,1,0:T(8,128)S(1)}, f32[7,2,16,128]{3,2,1,0:T(8,128)S(1)}, u32[]{:S(2)}, u32[]{:S(2)}) collective-permute-start(f32[7,2,16,128]{3,2,1,0:T(8,128)S(1)} %get-tuple-element.11.own_block), channel_id=1, source_target_pairs={{0,4},{1,5},{2,6},{3,7},{4,0},{5,1},{6,2},{7,3},{8,12},{9,13},{10,... | collective-permute-start | bytes 344072 | tf_op jit(solution)/shard_map/ppermute | solution.py:517
  4.9 5.9 %collective-permute-start = (f32[7,2,16,128]{3,2,1,0:T(8,128)S(1)}, f32[7,2,16,128]{3,2,1,0:T(8,128)S(1)}, u32[]{:S(2)}, u32[]{:S(2)}) collective-permute-start(f32[7,2,16,128]{3,2,1,0:T(8,128)S(1)} %get-tuple-element.11.own_block), channel_id=1, source_target_pairs={{0,2},{1,3},{2,0},{3,1},{4,6},{5,7},{6,4},{7,5},{8,10},{9,11},{10,... | collective-permute-start | bytes 344072 | tf_op jit(solution)/shard_map/ppermute | solution.py:517
  10.9 2.2 %collective-permute-start.3 = (f32[4,7,2,16,128]{4,3,2,1,0:T(8,128)S(1)}, f32[4,7,2,16,128]{4,3,2,1,0:T(8,128)S(1)}, u32[]{:S(2)}, u32[]{:S(2)}) collective-permute-start(f32[4,7,2,16,128]{4,3,2,1,0:T(8,128)S(1)} %pad_maximum_fusion.same), channel_id=1, source_target_pairs={{0,1},{1,0},{2,3},{3,2},{4,5},{5,4},{6,7},{7,6},{8,9},{9,8},{10,11... | collective-permute-start | bytes 1376264 | tf_op jit(solution)/shard_map/ppermute | solution.py:517
  16.1 4.1 %collective-permute-start.4 = (f32[2,136,128]{2,1,0:T(8,128)S(1)}, f32[2,136,128]{2,1,0:T(8,128)S(1)}, u32[]{:S(2)}, u32[]{:S(2)}) collective-permute-start(f32[2,136,128]{2,1,0:T(8,128)S(1)} %get-tuple-element.14), channel_id=1, source_target_pairs={{0,8},{2,10},{4,12},{6,14},{8,16},{9,1},{10,18},{11,3},{12,20},{13... | collective-permute-start | bytes 417800 | tf_op jit(solution)/shard_map/ppermute | solution.py:582
  34.5 4.5 %collective-permute-start.7 = (f32[2,88,128]{2,1,0:T(8,128)S(1)}, f32[2,88,128]{2,1,0:T(8,128)S(1)}, u32[]{:S(2)}, u32[]{:S(2)}) collective-permute-start(f32[2,88,128]{2,1,0:T(8,128)S(1)} %shard_map.105), channel_id=1, source_target_pairs={{0,6},{1,7},{2,4},{3,5},{4,2},{5,3},{6,0},{7,1},{8,14},{9,15},{10,... | collective-permute-start | bytes 270344 | tf_op jit(solution)/shard_map/ppermute | solution.py:517
  34.6 4.4 %collective-permute-start.6 = (f32[2,88,128]{2,1,0:T(8,128)S(1)}, f32[2,88,128]{2,1,0:T(8,128)S(1)}, u32[]{:S(2)}, u32[]{:S(2)}) collective-permute-start(f32[2,88,128]{2,1,0:T(8,128)S(1)} %shard_map.105), channel_id=1, source_target_pairs={{0,4},{1,5},{2,6},{3,7},{4,0},{5,1},{6,2},{7,3},{8,12},{9,13},{10,... | collective-permute-start | bytes 270344 | tf_op jit(solution)/shard_map/ppermute | solution.py:517
  34.9 4.2 %collective-permute-start.5 = (f32[2,88,128]{2,1,0:T(8,128)S(1)}, f32[2,88,128]{2,1,0:T(8,128)S(1)}, u32[]{:S(2)}, u32[]{:S(2)}) collective-permute-start(f32[2,88,128]{2,1,0:T(8,128)S(1)} %shard_map.105), channel_id=1, source_target_pairs={{0,2},{1,3},{2,0},{3,1},{4,6},{5,7},{6,4},{7,5},{8,10},{9,11},{10,... | collective-permute-start | bytes 270344 | tf_op jit(solution)/shard_map/ppermute | solution.py:517
  39.2 8.6 %collective-permute-start.8 = (f32[4,2,88,128]{3,2,1,0:T(8,128)S(1)}, f32[4,2,88,128]{3,2,1,0:T(8,128)S(1)}, u32[]{:S(2)}, u32[]{:S(2)}) collective-permute-start(f32[4,2,88,128]{3,2,1,0:T(8,128)S(1)} %pad_maximum_fusion.1.same_b), channel_id=1, source_target_pairs={{0,1},{1,0},{2,3},{3,2},{4,5},{5,4},{6,7},{7,6},{8,9},{9,8},{10,11... | collective-permute-start | bytes 1081352 | tf_op jit(solution)/shard_map/ppermute | solution.py:517
where the time goes:
time: 62.5 us; the launch traced here: 61.7 us
  Pallas kernels  33.1 us (53%)
  starting transfers between devices  15.5 us (25%)
  waiting for transfers between devices  12.3 us (20%)
  between operations  0.69 us (1%)
    pallas_call x1, Pallas kernels, body(): pl.pallas_call(first_kernel, out_shape=jax.ShapeDtypeStruct((2, 88, LANES...  14.3 us
    pallas_call x1, Pallas kernels, body(): pl.pallas_call(second_kernel, out_shape=(jax.ShapeDtypeStruct((2, wide),...  13.9 us
    ppermute x8, starting transfers between devices, swap(): return lax.ppermute(x, 'tile', [(i, i ^ k) for i in range(count)])  13.4 us
    ppermute x8, waiting for transfers between devices, swap(): return lax.ppermute(x, 'tile', [(i, i ^ k) for i in range(count)])  10.3 us
    pallas_call x1, Pallas kernels, body(): pl.pallas_call(border_kernel, out_shape=(jax.ShapeDtypeStruct((2, 136, LA...  3.05 us
    ppermute x1, starting transfers between devices, body(): border = lax.ppermute(edge, ('region', 'tile'), moves)  2.08 us
    ppermute x1, waiting for transfers between devices, body(): border = lax.ppermute(edge, ('region', 'tile'), moves)  2 us
    pallas_call x1, Pallas kernels, body(): pl.pallas_call(prepare_kernel, out_shape=(pltpu.VMEM((7, 2, tiles, LANES)...  1.81 us
  transfers between devices with their start and end apart: 9, of which 7 were waited for; matrix products, arithmetic and copies ran while one was open for 0% of the time, Pallas kernels for 0%

commit v1 on v0

--- a/solution.py
+++ b/solution.py
@@ -95,40 +95,87 @@
     lax.fori_loop(0, cells, step, 0, unroll=8)
 
 
-def border_kernel(same, other, out, inverse, number, table, facts, sem, fact_sem):
-    copies = fetch(same, other, table, 7, sem)
+ORDER = [(0, r) for r in range(1, 9)] + [(1, r) for r in range(1, 9)]
+ORDER += [(0, 0), (0, 9), (1, 0), (1, 9)]
+NEAR_ROWS, EDGE_ROWS, SPARE = 32, 24, 30
+
+
+def border_kernel(same, other, out, inverse, number, facts, fact_sem):
     fact_copies = fetch_facts(same, other, facts, fact_sem)
-    for copy in fact_copies + copies:
+    for copy in fact_copies:
         copy.start()
     for copy in fact_copies:
         copy.wait()
     cells = inverse.shape[0]
     rows = cells // TX
-    per_pair = 8
     invert(facts, inverse, number, cells)
-    for copy in copies:
-        copy.wait()
     me = lax.axis_index("tile")
     odd = me & 1
-    first = (me >> 1) * per_pair
-    order = [(0, r) for r in range(1, 9)] + [(1, r) for r in range(1, 9)]
-    order += [(0, 0), (0, 9), (1, 0), (1, 9)]
-    for i, (away, r) in enumerate(order):
+    first = (me >> 1) * 8
+    for i, (away, r) in enumerate(ORDER):
         column = jnp.where(odd == 1, away, TX - 1 - away)
         row = jnp.clip(first + r - 1, 0, rows - 1)
-        source = inverse[column * rows + row]
-        source = split(source, SLOTS)
+        held = rows_at(same, other, inverse[column * rows + row])
         for f, field in enumerate((EAST, NORTH, ONE, PART, INFO)):
-            out[:, f * 24 + i : f * 24 + i + 1, :] = row_of(table, field, source)
+            out[:, f * 24 + i : f * 24 + i + 1, :] = held[field]
         if i < 8:
             for f, field in enumerate((TWO, PRICE)):
-                out[:, 120 + 8 * f + i : 121 + 8 * f + i, :] = row_of(table, field, source)
+                out[:, 120 + 8 * f + i : 121 + 8 * f + i, :] = held[field]
     for f in range(5):
         out[:, f * 24 + 20 : f * 24 + 24, :] = jnp.zeros((2, 4, LANES), F32)
 
 
-def row_of(table, field, source):
-    return table[source[0], field, :, pl.ds(source[1], 1), :]
+def rows_at(same, other, source):
+    half = same.shape[0]
+    block, slot = split(source, SLOTS)
+    at = (block & (half - 1), slice(None), slice(None), pl.ds(slot, 1), slice(None))
+    return jnp.where(block >= half, other[at], same[at])
+
+
+def near_kernel(inverse, number, same, other, near, columns, east, north):
+    me = lax.axis_index("tile")
+    odd = me & 1
+    first = (me >> 1) * 8
+    rows = inverse.shape[0] // TX
+    for u in range(3):
+        column = jnp.where(odd == 1, TX - 1 - u, u)
+
+        def gather(r, carry):
+            row = jnp.clip(first + r - 1, 0, rows - 1)
+            held = rows_at(same, other, inverse[column * rows + row])
+            near[:, :, pl.ds(u * 10 + r, 1), :] = held
+            return carry
+
+        lax.fori_loop(0, 10, gather, 0, unroll=2)
+    near[:, :, SPARE:NEAR_ROWS, :] = jnp.zeros((7, 2, NEAR_ROWS - SPARE, LANES), F32)
+
+    def targets(field):
+        return jnp.concatenate([near[field, :, 1:9, :], near[field, :, 11:19, :]], axis=1)
+
+    info = targets(INFO)[0]
+    scale = scale_of(info[:, WIDTH : WIDTH + 1])[None]
+    east[...] = columns_of(2.0 * scale * targets(EAST))
+    north[...] = columns_of(2.0 * scale * targets(NORTH))
+
+    def number_of(t):
+        return number[jnp.where(odd == 1, TX - 1 - t // 8, t // 8) * rows + first + t % 8]
+
+    spread_columns(16, number_of, east, north, columns)
+
+
+def scale_of(width):
+    return jnp.broadcast_to(BASE / (width * width), (width.shape[0], LANES))
+
+
+def own_columns_kernel(block, mine, columns, scales, east, north):
+    tiles = block.shape[2]
+    for t in range(tiles):
+        width = jnp.full((1, LANES), mine[t * SLOTS + WIDTH].astype(F32), F32)
+        scales[t : t + 1, :] = BASE / (width * width)
+    scale = scales[...][None]
+    east[...] = columns_of(2.0 * scale * block[EAST])
+    north[...] = columns_of(2.0 * scale * block[NORTH])
+    spread_columns(tiles, lambda t: mine[t * SLOTS + COUNT], east, north, columns)
 
 
 def records(tiles):
@@ -142,9 +189,9 @@
     return jnp.concatenate([rows[0], pad, rows[1], pad], axis=0).T
 
 
-def rows_of(columns, tiles):
-    flat = columns.T
-    return jnp.stack([flat[:tiles], flat[64 : 64 + tiles]])
+def rows_of(low, high, tiles):
+    low, high = low.T, high.T
+    return [jnp.stack([low[k : k + tiles], high[k : k + tiles]]) for k in (0, 64)]
 
 
 def blocks_in(number):
@@ -174,9 +221,11 @@
             lay(t, 3, (east[64:128, :], north[64:128, :]))
 
 
-def collect_sums(tiles, number_of, sums, den_ref, num_ref):
-    lane = lax.broadcasted_iota(I32, (64, LANES), 1)
-    ones = jnp.ones((LANES, LANES), jnp.bfloat16)
+def collect_sums(tiles, number_of, sums, low_ref, high_ref):
+    split_at = lax.broadcasted_iota(I32, (2 * LANES, LANES), 0) // LANES
+    sides = lax.broadcasted_iota(I32, (2 * LANES, LANES), 1) // 64
+    ones = (split_at == sides).astype(F32).astype(jnp.bfloat16)
+    lane = lax.broadcasted_iota(I32, (64, LANES), 1) & 63
 
     def total(values):
         high = values.astype(jnp.bfloat16)
@@ -185,22 +234,20 @@
             low, ones, preferred_element_type=F32
         )
 
-    zero = jnp.zeros((64, LANES), F32)
-    for k, held in enumerate((den_ref, num_ref)):
-        for nb in range(2):
-            result = zero
-            for t in range(tiles):
-                x = total(sums[t, k, nb * 64 : nb * 64 + 64, :])
-                result = jnp.where(lane == t, x, result)
-            held[nb * 64 : nb * 64 + 64, :] = result
+    for nb in range(2):
+        result = jnp.zeros((64, LANES), F32)
+        for t in range(tiles):
+            x = total(sums[t, nb * 64 : nb * 64 + 64, :])
+            result = jnp.where(lane == t, x, result)
+        low_ref[nb * 64 : nb * 64 + 64, :] = result
+    high_ref[...] = jnp.zeros_like(high_ref)
 
     def rest(t, carry):
         @pl.when(number_of(t) > 128)
         def _():
-            for k, held in enumerate((den_ref, num_ref)):
-                x = total(sums[t, k, 128:256, :])
-                mine = lax.broadcasted_iota(I32, (128, LANES), 1) == 64 + t
-                held[...] = jnp.where(mine, x, held[...])
+            x = total(sums[t, 128:256, :])
+            mine = lax.broadcasted_iota(I32, (128, LANES), 1) & 63
+            high_ref[...] = jnp.where(mine == t, x, high_ref[...])
 
         return carry
 
@@ -210,42 +257,36 @@
 STEP = 4
 
 
-def sweep_tile(t, number, used, scale, columns, sums, table, part, cov, lists):
+def sweep_tile(t, at_column, number, used, scale, columns, sums, rows_for, lists):
     words, steps = lists
     scale = jnp.broadcast_to(scale, (8, LANES))
 
     def block(nb, carry):
         at = pl.ds(pl.multiple_of(nb * 64, 64), 64)
-        x = columns[t, 0, at, :].reshape(8, 8, LANES)
-        y = columns[t, 1, at, :].reshape(8, 8, LANES)
+        x = columns[at_column, 0, at, :].reshape(8, 8, LANES)
+        y = columns[at_column, 1, at, :].reshape(8, 8, LANES)
 
         def some(p, sums_now):
             den, num = sums_now
             for k in range(STEP):
                 i = STEP * p + k
                 word = words[i]
-                n, slot = split(word & 0xFFFF, SLOTS)
-                row = pl.ds(slot, 1)
-                h = (word >> 16) & 1
                 e = word >> 20
-
-                def wide(values):
-                    return jnp.broadcast_to(values, (8, LANES))
-
-                u = wide(table[n, EAST, h, row, :]) + steps[e]
-                v = wide(table[n, NORTH, h, row, :]) + steps[9 + e]
-                c = wide(table[n, cov, h, row, :])
-                d = wide(part(i, n, h, row))
-                q = scale * (u * u + v * v)
-                w = jnp.exp2(x * u + y * v - q)
-                den = den + w * (c * c)
-                num = num + w * d
+                u, v, c, d = rows_for(i, word & 0xFFFF, (word >> 16) & 1)
+                u = jnp.broadcast_to(u, (8, LANES)) + steps[e]
+                v = jnp.broadcast_to(v, (8, LANES)) + steps[9 + e]
+                c = jnp.broadcast_to(c, (8, LANES))
+                d = jnp.broadcast_to(d, (8, LANES))
+                fade = jnp.exp2(-scale * (u * u + v * v))
+                w = jnp.exp2(x * u + y * v)
+                den = den + w * (c * c * fade)
+                num = num + w * (d * fade)
             return den, num
 
         zero = jnp.zeros((8, 8, LANES), F32)
         den, num = lax.fori_loop(0, (used + STEP - 1) // STEP, some, (zero, zero))
-        sums[t, 0, at, :] = den.reshape(64, LANES)
-        sums[t, 1, at, :] = num.reshape(64, LANES)
+        sums[t, at, 0:LANES] = den.reshape(64, LANES)
+        sums[t, at, LANES : 2 * LANES] = num.reshape(64, LANES)
         return carry
 
     lax.fori_loop(0, blocks_in(number), block, 0)
@@ -262,28 +303,24 @@
 
 
 def first_kernel(
-    inverse, number, same, other, border, out,
-    table, own, scales, numbers, east, north, dens, nums, columns, sums,
-    facts, border_facts, window, live, chunks, words, steps, sem, fact_sem,
+    number, near, near_columns, border, out,
+    table, own, east, north, low, high, columns, sums,
+    facts, window, live, chunks, words, steps, sem, fact_sem,
 ):
-    copies = fetch(same, other, table, 6, sem)
-    fact_copies = fetch_facts(same, other, facts, fact_sem)
-    cells = inverse.shape[0]
+    cells = number.shape[0]
     rows = cells // TX
-    blocks = cells // SLOTS
-    empty = cells + 20
-    for f, field in enumerate((EAST, NORTH, ONE, PART, INFO)):
-        for k, size in enumerate((16, 8)):
-            held = pl.ds(f * 24 + 16 * k, size)
-            if field == INFO:
-                to = border_facts.at[pl.ds(16 * k, size)]
-                fact_copies.append(pltpu.make_async_copy(border.at[0, held], to, fact_sem))
-            else:
-                to = table.at[blocks + k, field, :, pl.ds(0, size)]
-                copies.append(pltpu.make_async_copy(border.at[:, held], to, sem))
+    near_at, edge_at = pl.ds(0, NEAR_ROWS), pl.ds(NEAR_ROWS, EDGE_ROWS)
+    copies = [pltpu.make_async_copy(near.at[pl.ds(0, 6)], table.at[:, :, near_at], sem)]
+    fact_copies = [
+        pltpu.make_async_copy(near.at[INFO, 0], facts.at[near_at], fact_sem),
+        pltpu.make_async_copy(border.at[0, pl.ds(4 * 24, 24)], facts.at[edge_at], fact_sem),
+    ]
+    for f, field in enumerate((EAST, NORTH, ONE, PART)):
+        held = border.at[:, pl.ds(f * 24, 24)]
+        copies.append(pltpu.make_async_copy(held, table.at[field, :, edge_at], sem))
     for f, field in enumerate((TWO, PRICE)):
-        to = table.at[blocks, field, :, pl.ds(0, 8)]
-        copies.append(pltpu.make_async_copy(border.at[:, pl.ds(120 + 8 * f, 8)], to, sem))
+        held = border.at[:, pl.ds(120 + 8 * f, 8)]
+        copies.append(pltpu.make_async_copy(held, table.at[field, :, pl.ds(NEAR_ROWS, 8)], sem))
     for copy in fact_copies + copies:
         copy.start()
     for copy in fact_copies:
@@ -292,102 +329,93 @@
     odd = me & 1
     first = (me >> 1) * 8
     toward = 1 - 2 * odd
-    order = [(0, r) for r in range(1, 9)] + [(1, r) for r in range(1, 9)]
-    order += [(0, 0), (0, 9), (1, 0), (1, 9)]
     for u in range(5):
         for r in range(10):
             row = first + r - 1
             if u < 2:
-                i = order.index((1 - u, r))
-                source = cells + i
-                held = border_facts[i, COUNT].astype(I32)
+                source = NEAR_ROWS + ORDER.index((1 - u, r))
+                held = facts[source, COUNT].astype(I32)
             else:
+                source = (u - 2) * 10 + r
                 column = jnp.where(odd == 1, 5 - u, u - 2)
-                cell = column * rows + jnp.clip(row, 0, rows - 1)
-                source = inverse[cell]
-                held = number[cell]
+                held = number[column * rows + jnp.clip(row, 0, rows - 1)]
             if r in (0, 9):
                 held = jnp.where((row >= 0) & (row < rows), held, 0)
-            window[u * 10 + r] = source
+            window[u * 10 + r] = jnp.int32(source)
             live[u * 10 + r] = held
             chunks[u * 10 + r] = chunks_in(held)
+    set_steps(steps)
     for copy in copies:
         copy.wait()
     tiles = 24
-
-    def target_fact(t, target, k):
-        inner = fact(facts, jnp.minimum(target, cells - 1), k)
-        return jnp.where(t < 8, border_facts[jnp.minimum(t, 7), k], inner)
-
-    def gather(t, carry):
-        place = ((t >> 3) + 1) * 10 + (t & 7) + 1
-        target = window[place]
-        at = split(target, SLOTS)
-        width = jnp.full((1, LANES), target_fact(t, target, WIDTH), F32)
-        scales[pl.ds(t, 1), :] = BASE / (width * width)
-        numbers[pl.ds(t, 1), :] = jnp.full((1, LANES), live[place].astype(F32), F32)
-        for field in range(6):
-            own[field, :, pl.ds(t, 1), :] = row_of(table, field, at)
-        return carry
-
-    lax.fori_loop(0, tiles, gather, 0, unroll=2)
-    set_steps(steps)
-    present = records(tiles) < numbers[...][None]
-    scale_rows = scales[...][None]
-    x, y = own[EAST], own[NORTH]
-    east[...] = columns_of(2.0 * scale_rows * x)
-    north[...] = columns_of(2.0 * scale_rows * y)
-    dens[...] = jnp.zeros_like(dens)
-    nums[...] = jnp.zeros_like(nums)
+    edge_info = border[0, 4 * 24 : 4 * 24 + 8, :]
+    info = jnp.concatenate([edge_info, near[INFO, 0, 1:9, :], near[INFO, 0, 11:19, :]], axis=0)
+    scales = scale_of(info[:, WIDTH : WIDTH + 1])
+    counts = jnp.broadcast_to(info[:, COUNT : COUNT + 1], (tiles, LANES))
+
+    def of_targets(field):
+        parts = [table[field, :, 32:40, :], table[field, :, 1:9, :], table[field, :, 11:19, :]]
+        return jnp.concatenate(parts, axis=1)
+
+    present = records(tiles) < counts[None]
+    scale_rows = scales[None]
+    own[...] = scales
+    x, y = of_targets(EAST), of_targets(NORTH)
+    east[...] = columns_of(2.0 * scale_rows[:, 0:8] * x[:, 0:8])
+    north[...] = columns_of(2.0 * scale_rows[:, 0:8] * y[:, 0:8])
 
     def number_of(t):
         return live[((t >> 3) + 1) * 10 + (t & 7) + 1]
 
-    spread_columns(tiles, number_of, east, north, columns)
-
-    def each(t, carry):
+    spread_columns(8, number_of, east, north, columns)
+
+    def rows_for(i, source, h):
+        at = pl.ds(source, 1)
+        return [table[field, h, at, :] for field in (EAST, NORTH, ONE, PART)]
+
+    def each(t, carry, held, skip):
         u = (t >> 3) + 1
         r = (t & 7) + 1
         target = window[u * 10 + r]
-        number = live[u * 10 + r]
         used = jnp.int32(0)
         for e, (a, b) in enumerate(NEAR):
             place = (u + toward * a) * 10 + r + b
             word = window[place] + (e << 20)
             more = chunks[place]
             if e != 4:
-                more = jnp.where(target_fact(t, target, REACH + e) > 0.5, more, 0)
+                more = jnp.where(facts[target, REACH + e] > 0.5, more, 0)
             words[used] = word
             words[used + 1] = word + (1 << 16)
             used = used + more
         for k in range(STEP - 1):
-            words[used + k] = jnp.int32(empty)
-        lists = (words, steps)
+            words[used + k] = jnp.int32(SPARE)
         sweep_tile(
-            t, number, used, scales[pl.ds(t, 1), :], columns, sums, table,
-            lambda i, n, h, row: table[n, PART, h, row, :], ONE, lists,
+            t, t - skip, number_of(t), used, own[pl.ds(t, 1), :], held, sums,
+            rows_for, (words, steps),
         )
         return carry
 
-    lax.fori_loop(0, tiles, each, 0)
-    collect_sums(tiles, number_of, sums, dens, nums)
+    lax.fori_loop(0, 8, lambda t, c: each(t, c, columns, 0), 0)
+    lax.fori_loop(8, tiles, lambda t, c: each(t, c, near_columns, 8), 0)
+    collect_sums(tiles, number_of, sums, low, high)
     shrink = jnp.exp2(-scale_rows * (x * x + y * y))
-    inv = 1.0 / (1.0 + shrink * rows_of(dens[...], tiles))
-    beta = jnp.where(present, shrink * rows_of(nums[...], tiles) * inv, 0.0)
-    one, two = own[ONE], own[TWO]
-    out[:, 0:24, :] = two * (own[PRICE] - one * beta)
+    den, num = rows_of(low[...], high[...], tiles)
+    inv = 1.0 / (1.0 + shrink * den)
+    beta = jnp.where(present, shrink * num * inv, 0.0)
+    one, two = of_targets(ONE), of_targets(TWO)
+    out[:, 0:24, :] = two * (of_targets(PRICE) - one * beta)
     out[:, 24:40, :] = beta[:, 8:24]
-    out[:, 40:56, :] = (one * one * inv)[:, 8:24]
+    out[:, 40:56, :] = jnp.where(present, one * one * inv, 0.0)[:, 8:24]
     out[:, 56:64, :] = two[:, 0:8]
     out[:, 64:72, :] = x[:, 0:8]
     out[:, 72:80, :] = y[:, 0:8]
-    out[:, 80:88, :] = jnp.broadcast_to(numbers[0:8, :][None], (2, 8, LANES))
+    out[:, 80:88, :] = jnp.broadcast_to(counts[0:8][None], (2, 8, LANES))
 
 
 def second_kernel(
-    inverse, number, own_block, same, other, same_b, other_b, mine,
+    inverse, number, own_block, columns, same, other, same_b, other_b, mine,
     betas, hats, residual,
-    table, results, own, scales, numbers, east, north, dens, nums, columns, sums,
+    table, results, own, scales, numbers, low, high, sums,
     border_facts, words, steps, spots, sem, fact_sem,
 ):
     copies = fetch(same, other, table, 3, sem)
@@ -412,15 +440,10 @@
     present = records(tiles) < numbers[...][None]
     scale_rows = scales[...][None]
     x, y = own_block[EAST], own_block[NORTH]
-    east[...] = columns_of(2.0 * scale_rows * x)
-    north[...] = columns_of(2.0 * scale_rows * y)
-    dens[...] = jnp.zeros_like(dens)
-    nums[...] = jnp.zeros_like(nums)
 
     def number_of(t):
         return mine[t * SLOTS + COUNT]
 
-    spread_columns(tiles, number_of, east, north, columns)
     for copy in fact_copies:
         copy.wait()
     me = lax.axis_index("tile")
@@ -449,6 +472,12 @@
     def side(column):
         low = (column < TX // 2).astype(I32)
         return low, jnp.where(low == 1, column + 1, TX - column)
+
+    def rows_for(i, source, h):
+        n, slot = split(source, SLOTS)
+        m, at = split(spots[i], 256)
+        held = [table[n, field, h, pl.ds(slot, 1), :] for field in (EAST, NORTH, TWO)]
+        return [*held, results[m, h, pl.ds(at, 1), :]]
 
     def each(t, carry):
         column, across = split(mine[t * SLOTS + LABEL], rows)
@@ -478,30 +507,26 @@
         for k in range(STEP - 1):
             words[used + k] = jnp.int32(empty)
             spots[used + k] = jnp.int32(88)
-        lists = (words, steps)
         n, at = place(*sides[1][1:], *lines[1][2:])
         own[0, :, pl.ds(t, 1), :] = results[n, :, pl.ds(16 + at, 1), :]
         own[1, :, pl.ds(t, 1), :] = results[n, :, pl.ds(32 + at, 1), :]
 
-        def part(i, n, h, row):
-            n, at = split(spots[i], 256)
-            return results[n, h, pl.ds(at, 1), :]
-
         sweep_tile(
-            t, mine[t * SLOTS + COUNT], used, scales[pl.ds(t, 1), :], columns, sums, table,
-            part, TWO, lists,
+            t, t, number_of(t), used, scales[pl.ds(t, 1), :], columns, sums,
+            rows_for, (words, steps),
         )
         return carry
 
     lax.fori_loop(0, tiles, each, 0)
-    collect_sums(tiles, number_of, sums, dens, nums)
+    collect_sums(tiles, number_of, sums, low, high)
     shrink = jnp.exp2(-scale_rows * (x * x + y * y))
-    inv = 1.0 / (1.0 + shrink * rows_of(dens[...], tiles))
-    beta_two = jnp.where(present, shrink * rows_of(nums[...], tiles) * inv, 0.0)
+    den, num = rows_of(low[...], high[...], tiles)
+    inv = 1.0 / (1.0 + shrink * den)
+    beta_two = jnp.where(present, shrink * num * inv, 0.0)
     beta_one = own[0]
     one, two = own_block[ONE], own_block[TWO]
     left = jnp.where(present, own_block[PRICE] - one * beta_one - two * beta_two, 0.0)
-    hat_two = two * two * inv
+    hat_two = jnp.where(present, two * two * inv, 0.0)
     for t in range(tiles):
         for h in range(2):
             at = slice(t * TILE + h * LANES, t * TILE + (h + 1) * LANES)
@@ -528,7 +553,7 @@
     count = lax.axis_size("tile")
     regions = lax.axis_size("region")
     cells = tiles * count
-    limit = pltpu.CompilerParams(vmem_limit_bytes=48 * 1024 * 1024)
+    limit = pltpu.CompilerParams(vmem_limit_bytes=24 * 1024 * 1024)
     price = target.reshape(1, -1)
     wide = tiles * TILE
     given = (
@@ -554,6 +579,16 @@
         ],
         compiler_params=limit,
     )(*[pltpu.with_memory_space_constraint(x, pltpu.HBM) for x in given])
+    square = pltpu.VMEM((LANES, LANES), F32)
+    own_columns = pl.pallas_call(
+        own_columns_kernel,
+        out_shape=pltpu.VMEM((tiles, 2, TILE, LANES), F32),
+        in_specs=[VMEM, SMEM],
+        out_specs=VMEM,
+        scratch_shapes=[pltpu.VMEM((tiles, LANES), F32), square, square],
+        compiler_params=limit,
+        cost_estimate=pl.CostEstimate(flops=4000000, bytes_accessed=4000000, transcendentals=0),
+    )(block, mine)
     same, other = spread(block)
     dma = pltpu.SemaphoreType.DMA
     edge, inverse, number = pl.pallas_call(
@@ -563,16 +598,23 @@
             jax.ShapeDtypeStruct((cells,), I32),
             jax.ShapeDtypeStruct((cells,), I32),
         ),
-        in_specs=[ANY, ANY],
+        in_specs=[VMEM, VMEM],
         out_specs=(VMEM, SMEM, SMEM),
-        scratch_shapes=[
-            pltpu.VMEM((count, 7, 2, tiles, LANES), F32),
-            pltpu.SMEM((count, 8, LANES), F32),
-            dma,
-            dma,
-        ],
+        scratch_shapes=[pltpu.SMEM((count, 8, LANES), F32), dma],
         compiler_params=limit,
     )(same, other)
+    near, near_columns = pl.pallas_call(
+        near_kernel,
+        out_shape=(
+            pltpu.VMEM((7, 2, NEAR_ROWS, LANES), F32),
+            pltpu.VMEM((16, 2, TILE, LANES), F32),
+        ),
+        in_specs=[SMEM, SMEM, VMEM, VMEM],
+        out_specs=(VMEM, VMEM),
+        scratch_shapes=[square, square],
+        compiler_params=limit,
+        cost_estimate=pl.CostEstimate(flops=4000000, bytes_accessed=4000000, transcendentals=0),
+    )(inverse, number, same, other)
     moves = []
     for r in range(regions):
         for t in range(count):
@@ -580,33 +622,29 @@
             if 0 <= to < regions:
                 moves.append((r * count + t, to * count + t))
     border = lax.ppermute(edge, ("region", "tile"), moves)
-    square = pltpu.VMEM((LANES, LANES), F32)
     lists = [pltpu.SMEM((24,), I32), pltpu.SMEM((18,), F32)]
     first = pl.pallas_call(
         first_kernel,
         out_shape=jax.ShapeDtypeStruct((2, 88, LANES), F32),
-        in_specs=[SMEM, SMEM, ANY, ANY, ANY],
+        in_specs=[SMEM, VMEM, VMEM, VMEM],
         out_specs=VMEM,
         scratch_shapes=[
-            pltpu.VMEM((count + 2, 6, 2, tiles, LANES), F32),
-            pltpu.VMEM((6, 2, 24, LANES), F32),
-            pltpu.VMEM((24, LANES), F32),
+            pltpu.VMEM((6, 2, NEAR_ROWS + EDGE_ROWS, LANES), F32),
             pltpu.VMEM((24, LANES), F32),
             square,
             square,
             square,
             square,
-            pltpu.VMEM((24, 2, TILE, LANES), F32),
-            pltpu.VMEM((24, 2, TILE, LANES), F32),
-            pltpu.SMEM((count, 8, LANES), F32),
-            pltpu.SMEM((24, LANES), F32),
+            pltpu.VMEM((8, 2, TILE, LANES), F32),
+            pltpu.VMEM((24, TILE, 2 * LANES), F32),
+            pltpu.SMEM((NEAR_ROWS + EDGE_ROWS, LANES), F32),
             *[pltpu.SMEM((56,), I32)] * 3,
             *lists,
             dma,
             dma,
         ],
         compiler_params=limit,
-    )(inverse, number, same, other, border)
+    )(number, near, near_columns, border)
     same_b, other_b = spread(first)
     betas, hats, residual = pl.pallas_call(
         second_kernel,
@@ -615,7 +653,7 @@
             jax.ShapeDtypeStruct((2, wide), F32),
             jax.ShapeDtypeStruct((1, wide), F32),
         ),
-        in_specs=[SMEM, SMEM, VMEM, ANY, ANY, ANY, ANY, SMEM],
+        in_specs=[SMEM, SMEM, VMEM, VMEM, ANY, ANY, ANY, ANY, SMEM],
         out_specs=(VMEM, VMEM, VMEM),
         scratch_shapes=[
             pltpu.VMEM((count + count // 2 + 1, 3, 2, tiles, LANES), F32),
@@ -625,10 +663,7 @@
             pltpu.VMEM((tiles, LANES), F32),
             square,
             square,
-            square,
-            square,
-            pltpu.VMEM((tiles, 2, TILE, LANES), F32),
-            pltpu.VMEM((tiles, 2, TILE, LANES), F32),
+            pltpu.VMEM((tiles, TILE, 2 * LANES), F32),
             pltpu.SMEM((count, 8, LANES), F32),
             *lists,
             pltpu.SMEM((24,), I32),
@@ -636,7 +671,7 @@
             dma,
         ],
         compiler_params=limit,
-    )(inverse, number, block, same, other, same_b, other_b, mine)
+    )(inverse, number, block, own_columns, same, other, same_b, other_b, mine)
     return (betas, hats, residual.reshape(-1))
 
 

time: 62.5 us -> 58 us (0.928)
  the two profiles are of different devices: /device:TPU:25 before, /device:TPU:13 now
where the time goes in v1:
time: 58 us; the launch traced here: 57 us
  Pallas kernels  31.1 us (54%)
  starting transfers between devices  15.9 us (27%)
  waiting for transfers between devices  9.22 us (16%)
  between operations  0.7 us (1%)
    ppermute x8, starting transfers between devices, swap(): return lax.ppermute(x, 'tile', [(i, i ^ k) for i in range(count)])  13.9 us
    pallas_call x1, Pallas kernels, body(): pl.pallas_call(second_kernel, out_shape=(jax.ShapeDtypeStruct((2, wide),...  11.1 us
    pallas_call x1, Pallas kernels, body(): pl.pallas_call(first_kernel, out_shape=jax.ShapeDtypeStruct((2, 88, LANES...  10.8 us
    ppermute x8, waiting for transfers between devices, swap(): return lax.ppermute(x, 'tile', [(i, i ^ k) for i in range(count)])  7.54 us
    pallas_call x1, Pallas kernels, body(): pl.pallas_call(border_kernel, out_shape=(jax.ShapeDtypeStruct((2, 136, LA...  3.08 us
    pallas_call x1, Pallas kernels, body(): pl.pallas_call(near_kernel, out_shape=(pltpu.VMEM((7, 2, NEAR_ROWS, LANES...  2.32 us
    ppermute x1, starting transfers between devices, body(): border = lax.ppermute(edge, ('region', 'tile'), moves)  2.08 us
    pallas_call x1, Pallas kernels, body(): pl.pallas_call(own_columns_kernel, out_shape=pltpu.VMEM((tiles, 2, TILE,...  1.98 us
  transfers between devices with their start and end apart: 9, of which 7 were waited for; matrix products, arithmetic and copies ran while one was open for 0% of the time, Pallas kernels for 8%

profile of v1, /device:TPU:13, one launch (start us, length us, event | category | flops | bytes accessed | tf_op | source)
XLA Modules:
  0.0 57.0 jit_solution(3703590482362491489)
XLA Ops:
  0.6 1.8 %shard_map.103 = (f32[7,2,16,128]{3,2,1,0:T(8,128)S(1)}, s32[256]{0:T(256)S(1)}) custom-call(f32[2,4096]{1,0:T(2,128)} %refs_0_.1, f32[2,4096]{1,0:T(2,128)} %refs_1_.1, f32[1,4096]{1,0:T(1,128)} %bitcast.20, f32[1,4096]{1,0:T(1,128)} %bitcast.21, s32[16]{0:T(128)} %refs_4_.1, s32[2,16]{1,0:T(2,128)} %refs_5_.1, s32[9,2,16]{2,1,0:T(2,128)} %bitcast.22, ...), custom_call_target="tpu_custom_call" | custom-call | tf_op jit(solution)/shard_map/pallas_call | solution.py:563
  2.5 1.3 %collective-permute-start = (f32[7,2,16,128]{3,2,1,0:T(8,128)S(1)}, f32[7,2,16,128]{3,2,1,0:T(8,128)S(1)}, u32[]{:S(2)}, u32[]{:S(2)}) collective-permute-start(f32[7,2,16,128]{3,2,1,0:T(8,128)S(1)} %get-tuple-element.13.block.own_block), channel_id=1, source_target_pairs={{0,2},{1,3},{2,0},{3,1},{4,6},{5,7},{6,4},{7,5},{8,10},{9,11},{10,... | collective-permute-start | bytes 344072 | tf_op jit(solution)/shard_map/ppermute | solution.py:542
  3.7 0.2 collective-permute-start.1
  4.0 1.2 %collective-permute-start.2 = (f32[7,2,16,128]{3,2,1,0:T(8,128)S(1)}, f32[7,2,16,128]{3,2,1,0:T(8,128)S(1)}, u32[]{:S(2)}, u32[]{:S(2)}) collective-permute-start(f32[7,2,16,128]{3,2,1,0:T(8,128)S(1)} %get-tuple-element.13.block.own_block), channel_id=1, source_target_pairs={{0,6},{1,7},{2,4},{3,5},{4,2},{5,3},{6,0},{7,1},{8,14},{9,15},{10,... | collective-permute-start | bytes 344072 | tf_op jit(solution)/shard_map/ppermute | solution.py:542
  5.2 1.4 %collective-permute-done = f32[7,2,16,128]{3,2,1,0:T(8,128)S(1)} collective-permute-done((f32[7,2,16,128]{3,2,1,0:T(8,128)S(1)}, f32[7,2,16,128]{3,2,1,0:T(8,128)S(1)}, u32[]{:S(2)}, u32[]{:S(2)}) %collective-permute-start) | collective-permute-done | bytes 114720 | tf_op jit(solution)/shard_map/ppermute | solution.py:542
  6.5 1.2 %collective-permute-done.1 = f32[7,2,16,128]{3,2,1,0:T(8,128)S(1)} collective-permute-done((f32[7,2,16,128]{3,2,1,0:T(8,128)S(1)}, f32[7,2,16,128]{3,2,1,0:T(8,128)S(1)}, u32[]{:S(2)}, u32[]{:S(2)}) %collective-permute-start.1) | collective-permute-done | bytes 114720 | tf_op jit(solution)/shard_map/ppermute | solution.py:542
  7.7 1.0 %collective-permute-done.2 = f32[7,2,16,128]{3,2,1,0:T(8,128)S(1)} collective-permute-done((f32[7,2,16,128]{3,2,1,0:T(8,128)S(1)}, f32[7,2,16,128]{3,2,1,0:T(8,128)S(1)}, u32[]{:S(2)}, u32[]{:S(2)}) %collective-permute-start.2) | collective-permute-done | bytes 114720 | tf_op jit(solution)/shard_map/ppermute | solution.py:542
  8.7 3.2 %collective-permute-start.3 = (f32[4,7,2,16,128]{4,3,2,1,0:T(8,128)S(1)}, f32[4,7,2,16,128]{4,3,2,1,0:T(8,128)S(1)}, u32[]{:S(2)}, u32[]{:S(2)}) collective-permute-start(f32[4,7,2,16,128]{4,3,2,1,0:T(8,128)S(1)} %pad_maximum_fusion.same), channel_id=1, source_target_pairs={{0,1},{1,0},{2,3},{3,2},{4,5},{5,4},{6,7},{7,6},{8,9},{9,8},{10,11... | collective-permute-start | bytes 1376264 | tf_op jit(solution)/shard_map/ppermute | solution.py:542
  11.9 1.4 %collective-permute-done.3.other = f32[4,7,2,16,128]{4,3,2,1,0:T(8,128)S(1)} collective-permute-done((f32[4,7,2,16,128]{4,3,2,1,0:T(8,128)S(1)}, f32[4,7,2,16,128]{4,3,2,1,0:T(8,128)S(1)}, u32[]{:S(2)}, u32[]{:S(2)}) %collective-permute-start.3) | collective-permute-done | bytes 458784 | tf_op jit(solution)/shard_map/ppermute | solution.py:542
  13.3 3.1 %shard_map.104 = (f32[2,136,128]{2,1,0:T(8,128)S(1)}, s32[128]{0:T(128)S(1)}, s32[128]{0:T(128)S(1)}) custom-call(f32[4,7,2,16,128]{4,3,2,1,0:T(8,128)S(1)} %pad_maximum_fusion.same, f32[4,7,2,16,128]{4,3,2,1,0:T(8,128)S(1)} %collective-permute-done.3.other), custom_call_target="tpu_custom_call" | custom-call | tf_op jit(solution)/shard_map/pallas_call | solution.py:594
  16.4 2.1 %collective-permute-start.4 = (f32[2,136,128]{2,1,0:T(8,128)S(1)}, f32[2,136,128]{2,1,0:T(8,128)S(1)}, u32[]{:S(2)}, u32[]{:S(2)}) collective-permute-start(f32[2,136,128]{2,1,0:T(8,128)S(1)} %get-tuple-element.19), channel_id=1, source_target_pairs={{0,8},{2,10},{4,12},{6,14},{8,16},{9,1},{10,18},{11,3},{12,20},{13... | collective-permute-start | bytes 417800 | tf_op jit(solution)/shard_map/ppermute | solution.py:624
  18.5 2.3 %shard_map.106 = (f32[7,2,32,128]{3,2,1,0:T(8,128)S(1)}, f32[16,2,256,128]{3,2,1,0:T(8,128)S(1)}) custom-call(s32[128]{0:T(128)S(1)} %get-tuple-element.14.inverse, s32[128]{0:T(128)S(1)} %get-tuple-element.15.number, f32[4,7,2,16,128]{4,3,2,1,0:T(8,128)S(1)} %pad_maximum_fusion.same, f32[4,7,2,16,128]{4,3,2,1,0:T(8,128)S(1)} %collective-permute-done.3.other), custom_call_target="tpu_custom_call" | custom-call | flops 4000000 | bytes 4000000 | tf_op jit(solution)/shard_map/pallas_call | solution.py:606
  20.8 1.7 %collective-permute-done.4.border = f32[2,136,128]{2,1,0:T(8,128)S(1)} collective-permute-done((f32[2,136,128]{2,1,0:T(8,128)S(1)}, f32[2,136,128]{2,1,0:T(8,128)S(1)}, u32[]{:S(2)}, u32[]{:S(2)}) %collective-permute-start.4) | collective-permute-done | bytes 139296 | tf_op jit(solution)/shard_map/ppermute | solution.py:624
  22.5 10.8 %shard_map.107 = f32[2,88,128]{2,1,0:T(8,128)S(1)} custom-call(s32[128]{0:T(128)S(1)} %get-tuple-element.15.number, f32[7,2,32,128]{3,2,1,0:T(8,128)S(1)} %get-tuple-element.17.near, f32[16,2,256,128]{3,2,1,0:T(8,128)S(1)} %get-tuple-element.18.near_columns, f32[2,136,128]{2,1,0:T(8,128)S(1)} %collective-permute-done.4.border), custom_call_target="tpu_custom_call" | custom-call | tf_op jit(solution)/shard_map/pallas_call | solution.py:626
  33.3 0.1 collective-permute-start.7
  33.3 0.9 %collective-permute-start.5 = (f32[2,88,128]{2,1,0:T(8,128)S(1)}, f32[2,88,128]{2,1,0:T(8,128)S(1)}, u32[]{:S(2)}, u32[]{:S(2)}) collective-permute-start(f32[2,88,128]{2,1,0:T(8,128)S(1)} %shard_map.107), channel_id=1, source_target_pairs={{0,2},{1,3},{2,0},{3,1},{4,6},{5,7},{6,4},{7,5},{8,10},{9,11},{10,... | collective-permute-start | bytes 270344 | tf_op jit(solution)/shard_map/ppermute | solution.py:542
  34.2 1.8 %collective-permute-start.6 = (f32[2,88,128]{2,1,0:T(8,128)S(1)}, f32[2,88,128]{2,1,0:T(8,128)S(1)}, u32[]{:S(2)}, u32[]{:S(2)}) collective-permute-start(f32[2,88,128]{2,1,0:T(8,128)S(1)} %shard_map.107), channel_id=1, source_target_pairs={{0,4},{1,5},{2,6},{3,7},{4,0},{5,1},{6,2},{7,3},{8,12},{9,13},{10,... | collective-permute-start | bytes 270344 | tf_op jit(solution)/shard_map/ppermute | solution.py:542
  36.0 1.7 %collective-permute-done.7 = f32[2,88,128]{2,1,0:T(8,128)S(1)} collective-permute-done((f32[2,88,128]{2,1,0:T(8,128)S(1)}, f32[2,88,128]{2,1,0:T(8,128)S(1)}, u32[]{:S(2)}, u32[]{:S(2)}) %collective-permute-start.7) | collective-permute-done | bytes 90144 | tf_op jit(solution)/shard_map/ppermute | solution.py:542
  37.7 0.0 collective-permute-done.5
  37.7 0.9 %collective-permute-done.6 = f32[2,88,128]{2,1,0:T(8,128)S(1)} collective-permute-done((f32[2,88,128]{2,1,0:T(8,128)S(1)}, f32[2,88,128]{2,1,0:T(8,128)S(1)}, u32[]{:S(2)}, u32[]{:S(2)}) %collective-permute-start.6) | collective-permute-done | bytes 90144 | tf_op jit(solution)/shard_map/ppermute | solution.py:542
  38.6 5.3 %collective-permute-start.8 = (f32[4,2,88,128]{3,2,1,0:T(8,128)S(1)}, f32[4,2,88,128]{3,2,1,0:T(8,128)S(1)}, u32[]{:S(2)}, u32[]{:S(2)}) collective-permute-start(f32[4,2,88,128]{3,2,1,0:T(8,128)S(1)} %pad_maximum_fusion.1.same_b), channel_id=1, source_target_pairs={{0,1},{1,0},{2,3},{3,2},{4,5},{5,4},{6,7},{7,6},{8,9},{9,8},{10,11... | collective-permute-start | bytes 1081352 | tf_op jit(solution)/shard_map/ppermute | solution.py:542
  43.9 2.0 %shard_map.105.columns = f32[16,2,256,128]{3,2,1,0:T(8,128)S(1)} custom-call(f32[7,2,16,128]{3,2,1,0:T(8,128)S(1)} %get-tuple-element.13.block.own_block, s32[256]{0:T(256)S(1)} %get-tuple-element.16.mine), custom_call_target="tpu_custom_call" | custom-call | flops 4000000 | bytes 4000000 | tf_op jit(solution)/shard_map/pallas_call | solution.py:583
  45.9 0.0 collective-permute-done.8.other_b
  45.9 11.1 %shard_map.108 = (f32[2,4096]{1,0:T(2,128)}, f32[2,4096]{1,0:T(2,128)}, f32[1,4096]{1,0:T(1,128)}) custom-call(s32[128]{0:T(128)S(1)} %get-tuple-element.14.inverse, s32[128]{0:T(128)S(1)} %get-tuple-element.15.number, f32[7,2,16,128]{3,2,1,0:T(8,128)S(1)} %get-tuple-element.13.block.own_block, f32[16,2,256,128]{3,2,1,0:T(8,128)S(1)} %shard_map.105.columns, ...), custom_call_target="tpu_custom_call" | custom-call | tf_op jit(solution)/shard_map/pallas_call | solution.py:649
  (2 shorter events, 0.1 us)
Async XLA Ops:
  2.5 4.1 %collective-permute-start = (f32[7,2,16,128]{3,2,1,0:T(8,128)S(1)}, f32[7,2,16,128]{3,2,1,0:T(8,128)S(1)}, u32[]{:S(2)}, u32[]{:S(2)}) collective-permute-start(f32[7,2,16,128]{3,2,1,0:T(8,128)S(1)} %get-tuple-element.13.block.own_block), channel_id=1, source_target_pairs={{0,2},{1,3},{2,0},{3,1},{4,6},{5,7},{6,4},{7,5},{8,10},{9,11},{10,... | collective-permute-start | bytes 344072 | tf_op jit(solution)/shard_map/ppermute | solution.py:542
  3.7 4.0 %collective-permute-start.1 = (f32[7,2,16,128]{3,2,1,0:T(8,128)S(1)}, f32[7,2,16,128]{3,2,1,0:T(8,128)S(1)}, u32[]{:S(2)}, u32[]{:S(2)}) collective-permute-start(f32[7,2,16,128]{3,2,1,0:T(8,128)S(1)} %get-tuple-element.13.block.own_block), channel_id=1, source_target_pairs={{0,4},{1,5},{2,6},{3,7},{4,0},{5,1},{6,2},{7,3},{8,12},{9,13},{10,... | collective-permute-start | bytes 344072 | tf_op jit(solution)/shard_map/ppermute | solution.py:542
  4.0 4.7 %collective-permute-start.2 = (f32[7,2,16,128]{3,2,1,0:T(8,128)S(1)}, f32[7,2,16,128]{3,2,1,0:T(8,128)S(1)}, u32[]{:S(2)}, u32[]{:S(2)}) collective-permute-start(f32[7,2,16,128]{3,2,1,0:T(8,128)S(1)} %get-tuple-element.13.block.own_block), channel_id=1, source_target_pairs={{0,6},{1,7},{2,4},{3,5},{4,2},{5,3},{6,0},{7,1},{8,14},{9,15},{10,... | collective-permute-start | bytes 344072 | tf_op jit(solution)/shard_map/ppermute | solution.py:542
  8.7 4.6 %collective-permute-start.3 = (f32[4,7,2,16,128]{4,3,2,1,0:T(8,128)S(1)}, f32[4,7,2,16,128]{4,3,2,1,0:T(8,128)S(1)}, u32[]{:S(2)}, u32[]{:S(2)}) collective-permute-start(f32[4,7,2,16,128]{4,3,2,1,0:T(8,128)S(1)} %pad_maximum_fusion.same), channel_id=1, source_target_pairs={{0,1},{1,0},{2,3},{3,2},{4,5},{5,4},{6,7},{7,6},{8,9},{9,8},{10,11... | collective-permute-start | bytes 1376264 | tf_op jit(solution)/shard_map/ppermute | solution.py:542
  16.4 6.1 %collective-permute-start.4 = (f32[2,136,128]{2,1,0:T(8,128)S(1)}, f32[2,136,128]{2,1,0:T(8,128)S(1)}, u32[]{:S(2)}, u32[]{:S(2)}) collective-permute-start(f32[2,136,128]{2,1,0:T(8,128)S(1)} %get-tuple-element.19), channel_id=1, source_target_pairs={{0,8},{2,10},{4,12},{6,14},{8,16},{9,1},{10,18},{11,3},{12,20},{13... | collective-permute-start | bytes 417800 | tf_op jit(solution)/shard_map/ppermute | solution.py:624
  33.3 4.4 %collective-permute-start.7 = (f32[2,88,128]{2,1,0:T(8,128)S(1)}, f32[2,88,128]{2,1,0:T(8,128)S(1)}, u32[]{:S(2)}, u32[]{:S(2)}) collective-permute-start(f32[2,88,128]{2,1,0:T(8,128)S(1)} %shard_map.107), channel_id=1, source_target_pairs={{0,6},{1,7},{2,4},{3,5},{4,2},{5,3},{6,0},{7,1},{8,14},{9,15},{10,... | collective-permute-start | bytes 270344 | tf_op jit(solution)/shard_map/ppermute | solution.py:542
  33.3 4.3 %collective-permute-start.5 = (f32[2,88,128]{2,1,0:T(8,128)S(1)}, f32[2,88,128]{2,1,0:T(8,128)S(1)}, u32[]{:S(2)}, u32[]{:S(2)}) collective-permute-start(f32[2,88,128]{2,1,0:T(8,128)S(1)} %shard_map.107), channel_id=1, source_target_pairs={{0,2},{1,3},{2,0},{3,1},{4,6},{5,7},{6,4},{7,5},{8,10},{9,11},{10,... | collective-permute-start | bytes 270344 | tf_op jit(solution)/shard_map/ppermute | solution.py:542
  34.2 4.4 %collective-permute-start.6 = (f32[2,88,128]{2,1,0:T(8,128)S(1)}, f32[2,88,128]{2,1,0:T(8,128)S(1)}, u32[]{:S(2)}, u32[]{:S(2)}) collective-permute-start(f32[2,88,128]{2,1,0:T(8,128)S(1)} %shard_map.107), channel_id=1, source_target_pairs={{0,4},{1,5},{2,6},{3,7},{4,0},{5,1},{6,2},{7,3},{8,12},{9,13},{10,... | collective-permute-start | bytes 270344 | tf_op jit(solution)/shard_map/ppermute | solution.py:542
  38.6 7.3 %collective-permute-start.8 = (f32[4,2,88,128]{3,2,1,0:T(8,128)S(1)}, f32[4,2,88,128]{3,2,1,0:T(8,128)S(1)}, u32[]{:S(2)}, u32[]{:S(2)}) collective-permute-start(f32[4,2,88,128]{3,2,1,0:T(8,128)S(1)} %pad_maximum_fusion.1.same_b), channel_id=1, source_target_pairs={{0,1},{1,0},{2,3},{3,2},{4,5},{5,4},{6,7},{7,6},{8,9},{9,8},{10,11... | collective-permute-start | bytes 1081352 | tf_op jit(solution)/shard_map/ppermute | solution.py:542

commit v2 on v1

v2 whole, which is shorter than its diff:
```python
import functools

import jax
import jax.numpy as jnp
from jax import lax
from jax.experimental import pallas as pl
from jax.experimental.pallas import tpu as pltpu
from jax.sharding import PartitionSpec as P

TILE = 256
TX = 4
LANES = 128
TWO, EAST, NORTH, ONE, PART, PRICE, INFO = range(7)
SLOTS = 16
BASE = 32.0 * 1.4426950408889634
LABEL, COUNT, WIDTH, REACH = 0, 1, 2, 3
NEAR = [(a, b) for a in (-1, 0, 1) for b in (-1, 0, 1)]
F32, I32 = jnp.float32, jnp.int32
ANY = pl.BlockSpec(memory_space=pl.ANY)
SMEM = pl.BlockSpec(memory_space=pltpu.SMEM)
VMEM = pl.BlockSpec(memory_space=pltpu.VMEM)


def prepare_kernel(*refs):
    given, (out, mine), held, sem = refs[:8], refs[8:10], refs[10:18], refs[18]
    copies = [pltpu.make_async_copy(a, b, sem) for a, b in zip(given, held)]
    for copy in copies:
        copy.start()
    for copy in copies:
        copy.wait()
    off, des, tgt, sec, counts, widths, reach, cells = held
    lane = lax.broadcasted_iota(I32, (1, LANES), 1)
    for t in range(counts.shape[0]):
        row = jnp.zeros((1, LANES), F32)
        facts = [cells[0, t], counts[t], widths[0, t]] + [reach[e, 0, t] for e in range(9)]
        for k, fact in enumerate(facts):
            row = jnp.where(lane == k, fact.astype(F32), row)
        out[INFO, 0, t : t + 1, :] = row
        for k, value in enumerate([widths[1, t]] + [reach[e, 1, t] for e in range(9)]):
            row = jnp.where(lane == WIDTH + k, value.astype(F32), row)
        mine[t : t + 1, :] = row
        for h in range(2):
            at = slice(t * TILE + h * LANES, t * TILE + (h + 1) * LANES)
            live = lane + h * LANES < counts[t]
            one = jnp.where(live, des[0:1, at], 0.0)
            two = jnp.where(live, des[1:2, at], 0.0)
            price = tgt[0:1, at]
            out[EAST, h, t : t + 1, :] = off[0:1, at] - 0.5
            out[NORTH, h, t : t + 1, :] = off[1:2, at] - 0.5
            out[ONE, h, t : t + 1, :] = one
            out[PART, h, t : t + 1, :] = one * (price - two * sec[0:1, at])
            out[TWO, h, t : t + 1, :] = two
            out[PRICE, h, t : t + 1, :] = price
    out[INFO, 1] = jnp.zeros_like(out[INFO, 1])


def split(number, size):
    return number >> (size.bit_length() - 1), number & (size - 1)


def fetch(same, other, table, fields, sem):
    half = same.shape[0]
    return [
        pltpu.make_async_copy(
            held.at[:, pl.ds(0, fields)], table.at[pl.ds(side * half, half)], sem
        )
        for side, held in enumerate((same, other))
    ]


ORDER = [(0, r) for r in range(1, 9)] + [(1, r) for r in range(1, 9)]
ORDER += [(0, 0), (0, 9), (1, 0), (1, 9)]
NEAR_ROWS, EDGE_ROWS, SPARE = 32, 24, 30


def wanted_cells(rows):
    me = lax.axis_index("tile")
    odd = me & 1
    first = (me >> 1) * 8
    i = lax.broadcasted_iota(I32, (64, LANES), 0)
    u = (i >= 10).astype(I32) + (i >= 20).astype(I32)
    j = i - NEAR_ROWS
    away = jnp.where(j < 16, j >> 3, (j >> 1) & 1)
    own = i < NEAR_ROWS
    r = jnp.where(own, i - 10 * u, jnp.where(j < 16, (j & 7) + 1, (j & 1) * 9))
    low = jnp.where(own, u, TX - 1 - away)
    column = jnp.where(odd == 1, TX - 1 - low, low)
    cell = column * rows + jnp.clip(first + r - 1, 0, rows - 1)
    none = (i == SPARE) | (i == SPARE + 1) | (j >= len(ORDER))
    return jnp.where(none, -1, cell).astype(F32)


def border_kernel(same, other, out, near):
    half = same.shape[0]
    cells = 2 * half * SLOTS

    def plane(field, h):
        parts = [x[:, field, h].reshape(half * SLOTS, LANES) for x in (same, other)]
        return jnp.concatenate(parts, axis=0)

    info = plane(INFO, 0)
    wanted = wanted_cells(cells // TX)
    hot = []
    for k in range(0, cells, LANES):
        labels = info[k : k + LANES].T[LABEL : LABEL + 1]
        hot.append((jnp.broadcast_to(labels, wanted.shape) == wanted).astype(F32))
    hot = jnp.concatenate(hot, axis=1).astype(jnp.bfloat16)

    def pick(values, pieces):
        total = jnp.zeros((64, LANES), F32)
        for _ in range(pieces):
            piece = values.astype(jnp.bfloat16)
            values = values - piece.astype(F32)
            total = total + jnp.dot(hot, piece, preferred_element_type=F32)
        return total

    for field in (EAST, NORTH, ONE, PART, INFO, TWO, PRICE):
        for h in range(2):
            if field != INFO:
                got = pick(plane(field, h), 3)
            elif h == 0:
                got = pick(info, 1)
            near[field, h] = got[0:NEAR_ROWS]
            edge = got[NEAR_ROWS : NEAR_ROWS + EDGE_ROWS]
            if field in (TWO, PRICE):
                f = (TWO, PRICE).index(field)
                out[h, 120 + 8 * f : 128 + 8 * f, :] = edge[0:8]
            else:
                f = (EAST, NORTH, ONE, PART, INFO).index(field)
                out[h, f * 24 : f * 24 + 24, :] = edge


def targets_of(near, field):
    return jnp.concatenate([near[field, :, 1:9, :], near[field, :, 11:19, :]], axis=1)


def near_kernel(near, columns, east, north, facts, sem):
    copy = pltpu.make_async_copy(near.at[INFO, 0], facts, sem)
    copy.start()
    info = targets_of(near, INFO)[0]
    scale = scale_of(info[:, WIDTH : WIDTH + 1])[None]
    east[...] = columns_of(2.0 * scale * targets_of(near, EAST))
    north[...] = columns_of(2.0 * scale * targets_of(near, NORTH))

    def number_of(t):
        return facts[(t >> 3) * 10 + (t & 7) + 1, COUNT].astype(I32)

    spread_columns(16, number_of, east, north, columns, copy.wait)


USED, LIVE, HOLDER, HELD_AT = 100, 101, 102, 103


def column_of(info, k):
    return jnp.broadcast_to(info[:, k : k + 1], (info.shape[0], LANES))


def chunks_in(number):
    return (number > 0.0).astype(I32) + (number > LANES).astype(I32)


def list_chunks(entries, number, spare):
    lane = lax.broadcasted_iota(I32, number.shape, 1)
    words = jnp.full(number.shape, spare, I32)
    used = jnp.zeros(number.shape, I32)
    for word, chunks in entries:
        words = jnp.where((lane == used) & (chunks > 0), word, words)
        words = jnp.where((lane == used + 1) & (chunks > 1), word + (1 << 10), words)
        used = used + chunks
    words = jnp.where(lane == USED, used, words)
    return jnp.where(lane == LIVE, number.astype(I32), words)


def place_of(column, row, me, half):
    low = (column < TX // 2).astype(I32)
    depth = jnp.where(low == 1, column + 1, TX - column)
    k = ((row >> 3) * 2 + 1 - low) ^ me
    return (k & 1) * half + (k >> 1), depth * 8 + (row & 7)


def scale_of(width):
    return jnp.broadcast_to(BASE / (width * width), (width.shape[0], LANES))


def own_columns_kernel(block, mine, columns, east, north, facts, sem):
    copy = pltpu.make_async_copy(mine, facts, sem)
    copy.start()
    scale = scale_of(mine[:, WIDTH : WIDTH + 1])[None]
    east[...] = columns_of(2.0 * scale * block[EAST])
    north[...] = columns_of(2.0 * scale * block[NORTH])

    def number_of(t):
        return facts[t, COUNT].astype(I32)

    spread_columns(block.shape[2], number_of, east, north, columns, copy.wait)


def records(tiles):
    shape = (2, tiles, LANES)
    number = lax.broadcasted_iota(I32, shape, 2) + LANES * lax.broadcasted_iota(I32, shape, 0)
    return number.astype(F32)


def columns_of(rows):
    pad = jnp.zeros((64 - rows.shape[1], LANES), F32)
    return jnp.concatenate([rows[0], pad, rows[1], pad], axis=0).T


def rows_of(low, high, tiles):
    low, high = low.T, high.T
    return [jnp.stack([low[k : k + tiles], high[k : k + tiles]]) for k in (0, 64)]


def blocks_in(number):
    return (number + 63) >> 6


def spread_columns(tiles, number_of, east, north, columns, ready=None):
    def lay(t, nb, values):
        i = (nb >> 1) * 64 + t
        for k, value in enumerate(values):
            wide = jnp.broadcast_to(value[:, i : i + 1], (64, LANES))
            columns[t, k, nb * 64 : nb * 64 + 64, :] = wide

    low = (east[0:64, :], north[0:64, :])
    for t in range(tiles):
        lay(t, 0, low)
    if ready is not None:
        ready()
    for t in range(tiles):
        number = number_of(t)

        @pl.when(number > 64)
        def _():
            lay(t, 1, (east[64:128, :], north[64:128, :]))

        @pl.when(number > 128)
        def _():
            lay(t, 2, (east[0:64, :], north[0:64, :]))
            lay(t, 3, (east[64:128, :], north[64:128, :]))


def collect_sums(tiles, number_of, sums, low_ref, high_ref):
    split_at = lax.broadcasted_iota(I32, (2 * LANES, LANES), 0) // LANES
    sides = lax.broadcasted_iota(I32, (2 * LANES, LANES), 1) // 64
    ones = (split_at == sides).astype(F32).astype(jnp.bfloat16)
    lane = lax.broadcasted_iota(I32, (64, LANES), 1) & 63

    def total(values):
        high = values.astype(jnp.bfloat16)
        low = (values - high.astype(F32)).astype(jnp.bfloat16)
        return jnp.dot(high, ones, preferred_element_type=F32) + jnp.dot(
            low, ones, preferred_element_type=F32
        )

    for nb in range(2):
        result = jnp.zeros((64, LANES), F32)
        for t in range(tiles):
            x = total(sums[t, nb * 64 : nb * 64 + 64, :])
            result = jnp.where(lane == t, x, result)
        low_ref[nb * 64 : nb * 64 + 64, :] = result
    high_ref[...] = jnp.zeros_like(high_ref)

    def rest(t, carry):
        @pl.when(number_of(t) > 128)
        def _():
            x = total(sums[t, 128:256, :])
            mine = lax.broadcasted_iota(I32, (128, LANES), 1) & 63
            high_ref[...] = jnp.where(mine == t, x, high_ref[...])

        return carry

    lax.fori_loop(0, tiles, rest, 0)


STEP = 2


def sweep_tile(t, at_column, scale, columns, sums, words, rows_for, steps):
    scale = jnp.broadcast_to(scale, (8, LANES))

    def block(nb, carry):
        at = pl.ds(pl.multiple_of(nb * 64, 64), 64)
        x = columns[at_column, 0, at, :].reshape(8, 8, LANES)
        y = columns[at_column, 1, at, :].reshape(8, 8, LANES)

        def some(p, sums_now):
            den, num = sums_now
            for k in range(STEP):
                word = words[t, STEP * p + k]
                e = (word >> 11) & 15
                u, v, c, d = rows_for(word)
                u = jnp.broadcast_to(u, (8, LANES)) + steps[e]
                v = jnp.broadcast_to(v, (8, LANES)) + steps[9 + e]
                c = jnp.broadcast_to(c, (8, LANES))
                d = jnp.broadcast_to(d, (8, LANES))
                fade = jnp.exp2(-scale * (u * u + v * v))
                w = jnp.exp2(x * u + y * v)
                den = den + w * (c * c * fade)
                num = num + w * (d * fade)
            return den, num

        zero = jnp.zeros((8, 8, LANES), F32)
        steps_used = (words[t, USED] + STEP - 1) // STEP
        den, num = lax.fori_loop(0, steps_used, some, (zero, zero))
        sums[t, at, 0:LANES] = den.reshape(64, LANES)
        sums[t, at, LANES : 2 * LANES] = num.reshape(64, LANES)
        return carry

    lax.fori_loop(0, blocks_in(words[t, LIVE]), block, 0)


def set_steps(steps):
    for e, (a, b) in enumerate(NEAR):
        steps[e] = jnp.float32(a)
        steps[9 + e] = jnp.float32(b)


def first_lists(near_info, edge_info, rows):
    me = lax.axis_index("tile")
    odd = me & 1
    first = (me >> 1) * 8
    near_live, edge_live = column_of(near_info, COUNT), column_of(edge_info, COUNT)
    step = lax.broadcasted_iota(I32, (8, LANES), 0)
    on_map = [(first > 0).astype(F32), (first + 8 < rows).astype(F32)]
    lines = []
    for u in range(5):
        if u < 2:
            away = 1 - u
            parts = [edge_live[i : i + n] for i, n in ((16 + 2 * away, 1), (8 * away, 8), (17 + 2 * away, 1))]
        else:
            parts = [near_live[10 * (u - 2) + i : 10 * (u - 2) + i + n] for i, n in ((0, 1), (1, 8), (9, 1))]
        lines.append(jnp.concatenate([parts[0] * on_map[0], parts[1], parts[2] * on_map[1]], axis=0))

    def source(u, b):
        if u >= 2:
            return (u - 2) * 10 + 1 + b + step
        start = NEAR_ROWS + 8 * (1 - u)
        at = start + b + step
        if b == 0:
            return at
        corner = NEAR_ROWS + 16 + 2 * (1 - u) + (b + 1) // 2
        return jnp.where(step == (0 if b < 0 else 7), corner, at)

    result = []
    for j, info in enumerate((edge_info[0:8], near_info[1:9], near_info[11:19])):
        entries = []
        for du in (-1, 0, 1):
            for b in (-1, 0, 1):
                here, there = 3 * (du + 1) + b + 1, 3 * (1 - du) + b + 1
                e = jnp.where(odd == 1, there, here)
                chunks = chunks_in(lines[j + 1 + du][1 + b : 9 + b])
                if here != 4:
                    taken = jnp.where(odd == 1, column_of(info, REACH + there), column_of(info, REACH + here))
                    chunks = jnp.where(taken > 0.5, chunks, 0)
                entries.append((source(j + 1 + du, b) + (e << 11), chunks))
        result.append(list_chunks(entries, column_of(info, COUNT), SPARE))
    return jnp.concatenate(result, axis=0)


def first_kernel(
    near, near_columns, border, out,
    table, own, east, north, low, high, columns, sums, listed,
    words, steps, sem, word_sem,
):
    rows = lax.axis_size("tile") * SLOTS // TX
    near_at, edge_at = pl.ds(0, NEAR_ROWS), pl.ds(NEAR_ROWS, EDGE_ROWS)
    copies = [pltpu.make_async_copy(near.at[pl.ds(0, 6)], table.at[:, :, near_at], sem)]
    for f, field in enumerate((EAST, NORTH, ONE, PART)):
        held = border.at[:, pl.ds(f * 24, 24)]
        copies.append(pltpu.make_async_copy(held, table.at[field, :, edge_at], sem))
    for f, field in enumerate((TWO, PRICE)):
        held = border.at[:, pl.ds(120 + 8 * f, 8)]
        copies.append(pltpu.make_async_copy(held, table.at[field, :, pl.ds(NEAR_ROWS, 8)], sem))
    for copy in copies:
        copy.start()
    near_info, edge_info = near[INFO, 0], border[0, 4 * 24 : 5 * 24, :]
    listed[...] = first_lists(near_info, edge_info, rows)
    word_copy = pltpu.make_async_copy(listed, words, word_sem)
    word_copy.start()
    set_steps(steps)
    tiles = 24
    info = jnp.concatenate([edge_info[0:8], near_info[1:9], near_info[11:19]], axis=0)
    scales = scale_of(info[:, WIDTH : WIDTH + 1])
    counts = column_of(info, COUNT)
    for copy in copies:
        copy.wait()

    def of_targets(field):
        parts = [table[field, :, 32:40, :], table[field, :, 1:9, :], table[field, :, 11:19, :]]
        return jnp.concatenate(parts, axis=1)

    present = records(tiles) < counts[None]
    scale_rows = scales[None]
    own[...] = scales
    x, y = of_targets(EAST), of_targets(NORTH)
    east[...] = columns_of(2.0 * scale_rows[:, 0:8] * x[:, 0:8])
    north[...] = columns_of(2.0 * scale_rows[:, 0:8] * y[:, 0:8])

    def number_of(t):
        return words[t, LIVE]

    spread_columns(8, number_of, east, north, columns, word_copy.wait)

    def rows_for(word):
        at, h = pl.ds(word & 1023, 1), (word >> 10) & 1
        return [table[field, h, at, :] for field in (EAST, NORTH, ONE, PART)]

    def each(t, carry, held, skip):
        sweep_tile(t, t - skip, own[pl.ds(t, 1), :], held, sums, words, rows_for, steps)
        return carry

    lax.fori_loop(0, 8, lambda t, c: each(t, c, columns, 0), 0)
    lax.fori_loop(8, tiles, lambda t, c: each(t, c, near_columns, 8), 0)
    collect_sums(tiles, number_of, sums, low, high)
    shrink = jnp.exp2(-scale_rows * (x * x + y * y))
    den, num = rows_of(low[...], high[...], tiles)
    inv = 1.0 / (1.0 + shrink * den)
    beta = jnp.where(present, shrink * num * inv, 0.0)
    one, two = of_targets(ONE), of_targets(TWO)
    out[:, 0:24, :] = two * (of_targets(PRICE) - one * beta)
    out[:, 24:40, :] = beta[:, 8:24]
    out[:, 40:56, :] = jnp.where(present, one * one * inv, 0.0)[:, 8:24]
    out[:, 56:64, :] = two[:, 0:8]
    out[:, 64:72, :] = x[:, 0:8]
    out[:, 72:80, :] = y[:, 0:8]
    out[:, 80:88, :] = jnp.broadcast_to(counts[0:8][None], (2, 8, LANES))


def second_lists(mine, same, other, same_b, other_b):
    half = same.shape[0]
    cells = 2 * half * SLOTS
    rows = cells // TX
    edge = 2 * half * 8
    padded = -(-edge // LANES) * LANES
    me = lax.axis_index("tile")
    info = jnp.concatenate([x[:, INFO, 0].reshape(half * SLOTS, LANES) for x in (same, other)], axis=0)
    keys = [info[k : k + LANES].T[LABEL : LABEL + 1] + rows for k in range(0, cells, LANES)]
    at = lax.broadcasted_iota(I32, (1, padded), 1)
    n = at >> 3
    device = (((n & (half - 1)) << 1) | (n >= half).astype(I32)) ^ me
    row = (device >> 1) * 8 + (at & 7)
    key = jnp.where((device & 1) == 1, (TX + 1) * rows + row, row)
    keys.append(jnp.where(at < edge, key, -1).astype(F32))
    keys = jnp.concatenate(keys, axis=1)
    total = cells + padded
    edge_live = [x[k, 0, 80:88, :] for x in (same_b, other_b) for k in range(half)]
    if padded > edge:
        edge_live.append(jnp.zeros((padded - edge, LANES), F32))
    live = jnp.concatenate([column_of(info, COUNT), *edge_live], axis=0)
    index = lax.broadcasted_iota(I32, (total, LANES), 0)
    cell = column_of(mine, LABEL).astype(I32)
    column, across = split(cell, rows)
    hot = []
    for a, b in NEAR:
        row = across + b
        wanted = jnp.where((row >= 0) & (row < rows), (column + a + 1) * rows + row, -2).astype(F32)
        parts = [keys[:, k : k + LANES] == wanted for k in range(0, total, LANES)]
        hot.append(jnp.concatenate([p.astype(F32) for p in parts], axis=1))
    hot = jnp.concatenate(hot, axis=0).astype(jnp.bfloat16)

    def look_up(values):
        return jnp.dot(hot, values.astype(F32).astype(jnp.bfloat16), preferred_element_type=F32)

    blocks, slots = look_up(index >> 4), look_up(index & 15)
    lives = look_up(live)
    tiles = mine.shape[0]
    entries = []
    for e, (a, b) in enumerate(NEAR):
        at = slice(e * tiles, (e + 1) * tiles)
        chunks = chunks_in(lives[at])
        if e != 4:
            chunks = jnp.where(column_of(mine, REACH + e) > 0.5, chunks, 0)
        source = blocks[at].astype(I32) * SLOTS + slots[at].astype(I32)
        n, spot = place_of(column + a, across + b, me, half)
        entries.append((source + (e << 11) + (n << 15) + (spot << 20), chunks))
    spare = cells + edge + (88 << 20)
    words = list_chunks(entries, column_of(mine, COUNT), spare)
    lane = lax.broadcasted_iota(I32, words.shape, 1)
    n, spot = place_of(column, across, me, half)
    words = jnp.where(lane == HOLDER, n, words)
    return jnp.where(lane == HELD_AT, spot, words)


def second_kernel(
    own_block, mine, columns, same, other, same_b, other_b,
    betas, hats, residual,
    table, results, own, scales, low, high, sums, listed,
    words, steps, sem, word_sem,
):
    copies = fetch(same, other, table, 3, sem)
    half, _, _, tiles, _ = same.shape
    blocks = 2 * half
    for side, held in enumerate((same_b, other_b)):
        at = pl.ds(side * half, half)
        copies.append(pltpu.make_async_copy(held, results.at[at, :, pl.ds(0, 88)], sem))
    for copy in copies:
        copy.start()
    listed[...] = second_lists(mine, same, other, same_b, other_b)
    word_copy = pltpu.make_async_copy(listed, words, word_sem)
    word_copy.start()
    set_steps(steps)
    scales[...] = scale_of(mine[:, WIDTH : WIDTH + 1])
    present = records(tiles) < column_of(mine, COUNT)[None]
    scale_rows = scales[...][None]
    x, y = own_block[EAST], own_block[NORTH]

    def number_of(t):
        return words[t, LIVE]

    for n in range(2 * half):
        held = (same_b if n < half else other_b).at[n % half]
        for field in range(3):
            table[blocks + n // 2, field, :, n % 2 * 8 : n % 2 * 8 + 8, :] = held[
                :, 56 + 8 * field : 64 + 8 * field, :
            ]
    for field in range(3):
        table[blocks + half, field, :, 0:8, :] = jnp.zeros((2, 8, LANES), F32)
    results[0, :, 88:96, :] = jnp.zeros((2, 8, LANES), F32)
    for copy in copies:
        copy.wait()
    word_copy.wait()

    def rows_for(word):
        n, slot = split(word & 1023, SLOTS)
        h = (word >> 10) & 1
        held = [table[n, field, h, pl.ds(slot, 1), :] for field in (EAST, NORTH, TWO)]
        return [*held, results[(word >> 15) & 31, h, pl.ds(word >> 20, 1), :]]

    def each(t, carry):
        n, at = words[t, HOLDER], words[t, HELD_AT]
        own[0, :, pl.ds(t, 1), :] = results[n, :, pl.ds(16 + at, 1), :]
        own[1, :, pl.ds(t, 1), :] = results[n, :, pl.ds(32 + at, 1), :]
        sweep_tile(t, t, scales[pl.ds(t, 1), :], columns, sums, words, rows_for, steps)
        return carry

    lax.fori_loop(0, tiles, each, 0)
    collect_sums(tiles, number_of, sums, low, high)
    shrink = jnp.exp2(-scale_rows * (x * x + y * y))
    den, num = rows_of(low[...], high[...], tiles)
    inv = 1.0 / (1.0 + shrink * den)
    beta_two = jnp.where(present, shrink * num * inv, 0.0)
    beta_one = own[0]
    one, two = own_block[ONE], own_block[TWO]
    left = jnp.where(present, own_block[PRICE] - one * beta_one - two * beta_two, 0.0)
    hat_two = jnp.where(present, two * two * inv, 0.0)
    for t in range(tiles):
        for h in range(2):
            at = slice(t * TILE + h * LANES, t * TILE + (h + 1) * LANES)
            betas[0:1, at] = beta_one[h, t : t + 1]
            betas[1:2, at] = beta_two[h, t : t + 1]
            hats[0:1, at] = own[1, h, t : t + 1, :]
            hats[1:2, at] = hat_two[h, t : t + 1]
            residual[0:1, at] = left[h, t : t + 1]


def swap(x, k):
    count = lax.axis_size("tile")
    return lax.ppermute(x, "tile", [(i, i ^ k) for i in range(count)])


def spread(block):
    count = lax.axis_size("tile")
    same = jnp.stack([block] + [swap(block, k) for k in range(2, count, 2)])
    return same, swap(same, 1)


def body(offsets, design, target, beta_second, counts, kernel_width, reach, assignment):
    tiles = counts.shape[0]
    count = lax.axis_size("tile")
    regions = lax.axis_size("region")
    cells = tiles * count
    limit = pltpu.CompilerParams(vmem_limit_bytes=24 * 1024 * 1024)
    price = target.reshape(1, -1)
    wide = tiles * TILE
    given = (
        offsets, design, price, beta_second.reshape(1, -1),
        counts, kernel_width, reach.transpose(2, 0, 1), assignment,
    )
    block, mine = pl.pallas_call(
        prepare_kernel,
        out_shape=(
            pltpu.VMEM((7, 2, tiles, LANES), F32),
            pltpu.VMEM((tiles, LANES), F32),
        ),
        in_specs=[pl.BlockSpec(memory_space=pltpu.HBM)] * 8,
        out_specs=(VMEM, VMEM),
        scratch_shapes=[pltpu.VMEM((2, wide), F32)] * 2
        + [pltpu.VMEM((1, wide), F32)] * 2
        + [
            pltpu.SMEM((tiles,), I32),
            pltpu.SMEM((2, tiles), I32),
            pltpu.SMEM((9, 2, tiles), I32),
            pltpu.SMEM((1, tiles), I32),
            pltpu.SemaphoreType.DMA,
        ],
        compiler_params=limit,
    )(*[pltpu.with_memory_space_constraint(x, pltpu.HBM) for x in given])
    square = pltpu.VMEM((LANES, LANES), F32)
    dma = pltpu.SemaphoreType.DMA
    own_columns = pl.pallas_call(
        own_columns_kernel,
        out_shape=pltpu.VMEM((tiles, 2, TILE, LANES), F32),
        in_specs=[VMEM, VMEM],
        out_specs=VMEM,
        scratch_shapes=[square, square, pltpu.SMEM((tiles, LANES), F32), dma],
        compiler_params=limit,
        cost_estimate=pl.CostEstimate(flops=4000000, bytes_accessed=4000000, transcendentals=0),
    )(block, mine)
    same, other = spread(block)
    edge, near = pl.pallas_call(
        border_kernel,
        out_shape=(
            jax.ShapeDtypeStruct((2, 136, LANES), F32),
            pltpu.VMEM((7, 2, NEAR_ROWS, LANES), F32),
        ),
        in_specs=[VMEM, VMEM],
        out_specs=(VMEM, VMEM),
        compiler_params=limit,
    )(same, other)
    near_columns = pl.pallas_call(
        near_kernel,
        out_shape=pltpu.VMEM((16, 2, TILE, LANES), F32),
        in_specs=[VMEM],
        out_specs=VMEM,
        scratch_shapes=[square, square, pltpu.SMEM((NEAR_ROWS, LANES), F32), dma],
        compiler_params=limit,
        cost_estimate=pl.CostEstimate(flops=4000000, bytes_accessed=4000000, transcendentals=0),
    )(near)
    moves = []
    for r in range(regions):
        for t in range(count):
            to = r + 1 - 2 * (t % 2)
            if 0 <= to < regions:
                moves.append((r * count + t, to * count + t))
    border = lax.ppermute(edge, ("region", "tile"), moves)
    first = pl.pallas_call(
        first_kernel,
        out_shape=jax.ShapeDtypeStruct((2, 88, LANES), F32),
        in_specs=[VMEM, VMEM, VMEM],
        out_specs=VMEM,
        scratch_shapes=[
            pltpu.VMEM((6, 2, NEAR_ROWS + EDGE_ROWS, LANES), F32),
            pltpu.VMEM((24, LANES), F32),
            square,
            square,
            square,
            square,
            pltpu.VMEM((8, 2, TILE, LANES), F32),
            pltpu.VMEM((24, TILE, 2 * LANES), F32),
            pltpu.VMEM((24, LANES), I32),
            pltpu.SMEM((24, LANES), I32),
            pltpu.SMEM((18,), F32),
            dma,
            dma,
        ],
        compiler_params=limit,
    )(near, near_columns, border)
    same_b, other_b = spread(first)
    betas, hats, residual = pl.pallas_call(
        second_kernel,
        out_shape=(
            jax.ShapeDtypeStruct((2, wide), F32),
            jax.ShapeDtypeStruct((2, wide), F32),
            jax.ShapeDtypeStruct((1, wide), F32),
        ),
        in_specs=[VMEM] * 7,
        out_specs=(VMEM, VMEM, VMEM),
        scratch_shapes=[
            pltpu.VMEM((count + count // 2 + 1, 3, 2, tiles, LANES), F32),
            pltpu.VMEM((count, 2, 96, LANES), F32),
            pltpu.VMEM((2, 2, tiles, LANES), F32),
            pltpu.VMEM((tiles, LANES), F32),
            square,
            square,
            pltpu.VMEM((tiles, TILE, 2 * LANES), F32),
            pltpu.VMEM((tiles, LANES), I32),
            pltpu.SMEM((tiles, LANES), I32),
            pltpu.SMEM((18,), F32),
            dma,
            dma,
        ],
        compiler_params=limit,
    )(block, mine, own_columns, same, other, same_b, other_b)
    return (betas, hats, residual.reshape(-1))


def solution(mesh):
    in_specs = (
        P(None, ("region", "tile")),
        P(None, ("region", "tile")),
        P(("region", "tile")),
        P(("region", "tile")),
        P(("region", "tile")),
        P(None, ("region", "tile")),
        P(None, ("region", "tile"), None),
        P("region", "tile"),
    )
    out_specs = (P(None, ("region", "tile")), P(None, ("region", "tile")), P(("region", "tile")))
    return jax.shard_map(body, mesh=mesh, in_specs=in_specs, out_specs=out_specs, check_vma=False)
```

time: 58 us -> 53 us (0.914)
  the two profiles are of different devices: /device:TPU:13 before, /device:TPU:16 now
where the time goes in v2:
time: 53 us; the launch traced here: 53.1 us
  Pallas kernels  29.9 us (56%)
  waiting for transfers between devices  11.7 us (22%)
  starting transfers between devices  10.7 us (20%)
  between operations  0.72 us (1%)
    pallas_call x1, Pallas kernels, body(): pl.pallas_call(first_kernel, out_shape=jax.ShapeDtypeStruct((2, 88, LANES...  12.5 us
    pallas_call x1, Pallas kernels, body(): pl.pallas_call(second_kernel, out_shape=(jax.ShapeDtypeStruct((2, wide),...  11.3 us
    ppermute x8, waiting for transfers between devices, swap(): return lax.ppermute(x, 'tile', [(i, i ^ k) for i in range(count)])  10.4 us
    ppermute x8, starting transfers between devices, swap(): return lax.ppermute(x, 'tile', [(i, i ^ k) for i in range(count)])  7.24 us
    ppermute x1, starting transfers between devices, body(): border = lax.ppermute(edge, ('region', 'tile'), moves)  3.48 us
    pallas_call x1, Pallas kernels, body(): pl.pallas_call(own_columns_kernel, out_shape=pltpu.VMEM((tiles, 2, TILE,...  2.27 us
    pallas_call x1, Pallas kernels, body(): pl.pallas_call(near_kernel, out_shape=pltpu.VMEM((16, 2, TILE, LANES), F3...  2.11 us
    ppermute x1, waiting for transfers between devices, body(): border = lax.ppermute(edge, ('region', 'tile'), moves)  1.34 us
  transfers between devices with their start and end apart: 9, of which 8 were waited for; matrix products, arithmetic and copies ran while one was open for 0% of the time, Pallas kernels for 8%

profile of v2, /device:TPU:16, one launch (start us, length us, event | category | flops | bytes accessed | tf_op | source)
XLA Modules:
  0.0 53.1 jit_solution(12313014345945589971)
XLA Ops:
  0.6 1.2 %shard_map.103 = (f32[7,2,16,128]{3,2,1,0:T(8,128)S(1)}, f32[16,128]{1,0:T(8,128)S(1)}) custom-call(f32[2,4096]{1,0:T(2,128)} %refs_0_.1, f32[2,4096]{1,0:T(2,128)} %refs_1_.1, f32[1,4096]{1,0:T(1,128)} %bitcast.20, f32[1,4096]{1,0:T(1,128)} %bitcast.21, s32[16]{0:T(128)} %refs_4_.1, s32[2,16]{1,0:T(2,128)} %refs_5_.1, s32[9,2,16]{2,1,0:T(2,128)} %bitcast.22, ...), custom_call_target="tpu_custom_call" | custom-call | tf_op jit(solution)/shard_map/pallas_call | solution.py:580
  1.8 2.5 %collective-permute-start.2 = (f32[7,2,16,128]{3,2,1,0:T(8,128)S(1)}, f32[7,2,16,128]{3,2,1,0:T(8,128)S(1)}, u32[]{:S(2)}, u32[]{:S(2)}) collective-permute-start(f32[7,2,16,128]{3,2,1,0:T(8,128)S(1)} %get-tuple-element.10.block.own_block), channel_id=1, source_target_pairs={{0,6},{1,7},{2,4},{3,5},{4,2},{5,3},{6,0},{7,1},{8,14},{9,15},{10,... | collective-permute-start | bytes 344072 | tf_op jit(solution)/shard_map/ppermute | solution.py:559
  4.3 0.5 collective-permute-start.1
  4.8 0.5 %collective-permute-start = (f32[7,2,16,128]{3,2,1,0:T(8,128)S(1)}, f32[7,2,16,128]{3,2,1,0:T(8,128)S(1)}, u32[]{:S(2)}, u32[]{:S(2)}) collective-permute-start(f32[7,2,16,128]{3,2,1,0:T(8,128)S(1)} %get-tuple-element.10.block.own_block), channel_id=1, source_target_pairs={{0,2},{1,3},{2,0},{3,1},{4,6},{5,7},{6,4},{7,5},{8,10},{9,11},{10,... | collective-permute-start | bytes 344072 | tf_op jit(solution)/shard_map/ppermute | solution.py:559
  5.4 2.5 %collective-permute-done.2 = f32[7,2,16,128]{3,2,1,0:T(8,128)S(1)} collective-permute-done((f32[7,2,16,128]{3,2,1,0:T(8,128)S(1)}, f32[7,2,16,128]{3,2,1,0:T(8,128)S(1)}, u32[]{:S(2)}, u32[]{:S(2)}) %collective-permute-start.2) | collective-permute-done | bytes 114720 | tf_op jit(solution)/shard_map/ppermute | solution.py:559
  7.9 2.2 %collective-permute-done.1 = f32[7,2,16,128]{3,2,1,0:T(8,128)S(1)} collective-permute-done((f32[7,2,16,128]{3,2,1,0:T(8,128)S(1)}, f32[7,2,16,128]{3,2,1,0:T(8,128)S(1)}, u32[]{:S(2)}, u32[]{:S(2)}) %collective-permute-start.1) | collective-permute-done | bytes 114720 | tf_op jit(solution)/shard_map/ppermute | solution.py:559
  10.1 0.1 collective-permute-done
  10.2 0.1 collective-permute-start.3
  10.3 1.8 %collective-permute-done.3.other = f32[4,7,2,16,128]{4,3,2,1,0:T(8,128)S(1)} collective-permute-done((f32[4,7,2,16,128]{4,3,2,1,0:T(8,128)S(1)}, f32[4,7,2,16,128]{4,3,2,1,0:T(8,128)S(1)}, u32[]{:S(2)}, u32[]{:S(2)}) %collective-permute-start.3) | collective-permute-done | bytes 458784 | tf_op jit(solution)/shard_map/ppermute | solution.py:559
  12.1 0.5 shard_map.105
  12.6 3.5 %collective-permute-start.4 = (f32[2,136,128]{2,1,0:T(8,128)S(1)}, f32[2,136,128]{2,1,0:T(8,128)S(1)}, u32[]{:S(2)}, u32[]{:S(2)}) collective-permute-start(f32[2,136,128]{2,1,0:T(8,128)S(1)} %get-tuple-element.13), channel_id=1, source_target_pairs={{0,8},{2,10},{4,12},{6,14},{8,16},{9,1},{10,18},{11,3},{12,20},{13... | collective-permute-start | bytes 417800 | tf_op jit(solution)/shard_map/ppermute | solution.py:636
  16.1 2.1 %shard_map.106.near_columns = f32[16,2,256,128]{3,2,1,0:T(8,128)S(1)} custom-call(f32[7,2,32,128]{3,2,1,0:T(8,128)S(1)} %get-tuple-element.12.near), custom_call_target="tpu_custom_call" | custom-call | flops 4000000 | bytes 4000000 | tf_op jit(solution)/shard_map/pallas_call | solution.py:621
  18.2 1.3 %collective-permute-done.4.border = f32[2,136,128]{2,1,0:T(8,128)S(1)} collective-permute-done((f32[2,136,128]{2,1,0:T(8,128)S(1)}, f32[2,136,128]{2,1,0:T(8,128)S(1)}, u32[]{:S(2)}, u32[]{:S(2)}) %collective-permute-start.4) | collective-permute-done | bytes 139296 | tf_op jit(solution)/shard_map/ppermute | solution.py:636
  19.6 12.5 %shard_map.107 = f32[2,88,128]{2,1,0:T(8,128)S(1)} custom-call(f32[7,2,32,128]{3,2,1,0:T(8,128)S(1)} %get-tuple-element.12.near, f32[16,2,256,128]{3,2,1,0:T(8,128)S(1)} %shard_map.106.near_columns, f32[2,136,128]{2,1,0:T(8,128)S(1)} %collective-permute-done.4.border), custom_call_target="tpu_custom_call" | custom-call | tf_op jit(solution)/shard_map/pallas_call | solution.py:637
  32.1 0.1 collective-permute-start.7
  32.1 2.7 %collective-permute-start.6 = (f32[2,88,128]{2,1,0:T(8,128)S(1)}, f32[2,88,128]{2,1,0:T(8,128)S(1)}, u32[]{:S(2)}, u32[]{:S(2)}) collective-permute-start(f32[2,88,128]{2,1,0:T(8,128)S(1)} %shard_map.107), channel_id=1, source_target_pairs={{0,4},{1,5},{2,6},{3,7},{4,0},{5,1},{6,2},{7,3},{8,12},{9,13},{10,... | collective-permute-start | bytes 270344 | tf_op jit(solution)/shard_map/ppermute | solution.py:559
  34.8 0.8 %collective-permute-start.5 = (f32[2,88,128]{2,1,0:T(8,128)S(1)}, f32[2,88,128]{2,1,0:T(8,128)S(1)}, u32[]{:S(2)}, u32[]{:S(2)}) collective-permute-start(f32[2,88,128]{2,1,0:T(8,128)S(1)} %shard_map.107), channel_id=1, source_target_pairs={{0,2},{1,3},{2,0},{3,1},{4,6},{5,7},{6,4},{7,5},{8,10},{9,11},{10,... | collective-permute-start | bytes 270344 | tf_op jit(solution)/shard_map/ppermute | solution.py:559
  35.6 2.0 %collective-permute-done.7 = f32[2,88,128]{2,1,0:T(8,128)S(1)} collective-permute-done((f32[2,88,128]{2,1,0:T(8,128)S(1)}, f32[2,88,128]{2,1,0:T(8,128)S(1)}, u32[]{:S(2)}, u32[]{:S(2)}) %collective-permute-start.7) | collective-permute-done | bytes 90144 | tf_op jit(solution)/shard_map/ppermute | solution.py:559
  37.7 0.6 %collective-permute-done.6 = f32[2,88,128]{2,1,0:T(8,128)S(1)} collective-permute-done((f32[2,88,128]{2,1,0:T(8,128)S(1)}, f32[2,88,128]{2,1,0:T(8,128)S(1)}, u32[]{:S(2)}, u32[]{:S(2)}) %collective-permute-start.6) | collective-permute-done | bytes 90144 | tf_op jit(solution)/shard_map/ppermute | solution.py:559
  38.3 1.1 %collective-permute-done.5 = f32[2,88,128]{2,1,0:T(8,128)S(1)} collective-permute-done((f32[2,88,128]{2,1,0:T(8,128)S(1)}, f32[2,88,128]{2,1,0:T(8,128)S(1)}, u32[]{:S(2)}, u32[]{:S(2)}) %collective-permute-start.5) | collective-permute-done | bytes 90144 | tf_op jit(solution)/shard_map/ppermute | solution.py:559
  39.4 0.1 collective-permute-start.8
  39.5 2.3 %shard_map.104.columns = f32[16,2,256,128]{3,2,1,0:T(8,128)S(1)} custom-call(f32[7,2,16,128]{3,2,1,0:T(8,128)S(1)} %get-tuple-element.10.block.own_block, f32[16,128]{1,0:T(8,128)S(1)} %get-tuple-element.11.mine), custom_call_target="tpu_custom_call" | custom-call | flops 4000000 | bytes 4000000 | tf_op jit(solution)/shard_map/pallas_call | solution.py:601
  41.8 0.0 collective-permute-done.8.other_b
  41.8 11.3 %shard_map.108 = (f32[2,4096]{1,0:T(2,128)}, f32[2,4096]{1,0:T(2,128)}, f32[1,4096]{1,0:T(1,128)}) custom-call(f32[7,2,16,128]{3,2,1,0:T(8,128)S(1)} %get-tuple-element.10.block.own_block, f32[16,128]{1,0:T(8,128)S(1)} %get-tuple-element.11.mine, f32[16,2,256,128]{3,2,1,0:T(8,128)S(1)} %shard_map.104.columns, ...), custom_call_target="tpu_custom_call" | custom-call | tf_op jit(solution)/shard_map/pallas_call | solution.py:660
  (2 shorter events, 0.1 us)
Async XLA Ops:
  1.8 6.1 %collective-permute-start.2 = (f32[7,2,16,128]{3,2,1,0:T(8,128)S(1)}, f32[7,2,16,128]{3,2,1,0:T(8,128)S(1)}, u32[]{:S(2)}, u32[]{:S(2)}) collective-permute-start(f32[7,2,16,128]{3,2,1,0:T(8,128)S(1)} %get-tuple-element.10.block.own_block), channel_id=1, source_target_pairs={{0,6},{1,7},{2,4},{3,5},{4,2},{5,3},{6,0},{7,1},{8,14},{9,15},{10,... | collective-permute-start | bytes 344072 | tf_op jit(solution)/shard_map/ppermute | solution.py:559
  4.3 5.8 %collective-permute-start.1 = (f32[7,2,16,128]{3,2,1,0:T(8,128)S(1)}, f32[7,2,16,128]{3,2,1,0:T(8,128)S(1)}, u32[]{:S(2)}, u32[]{:S(2)}) collective-permute-start(f32[7,2,16,128]{3,2,1,0:T(8,128)S(1)} %get-tuple-element.10.block.own_block), channel_id=1, source_target_pairs={{0,4},{1,5},{2,6},{3,7},{4,0},{5,1},{6,2},{7,3},{8,12},{9,13},{10,... | collective-permute-start | bytes 344072 | tf_op jit(solution)/shard_map/ppermute | solution.py:559
  4.8 5.3 %collective-permute-start = (f32[7,2,16,128]{3,2,1,0:T(8,128)S(1)}, f32[7,2,16,128]{3,2,1,0:T(8,128)S(1)}, u32[]{:S(2)}, u32[]{:S(2)}) collective-permute-start(f32[7,2,16,128]{3,2,1,0:T(8,128)S(1)} %get-tuple-element.10.block.own_block), channel_id=1, source_target_pairs={{0,2},{1,3},{2,0},{3,1},{4,6},{5,7},{6,4},{7,5},{8,10},{9,11},{10,... | collective-permute-start | bytes 344072 | tf_op jit(solution)/shard_map/ppermute | solution.py:559
  10.2 1.9 %collective-permute-start.3 = (f32[4,7,2,16,128]{4,3,2,1,0:T(8,128)S(1)}, f32[4,7,2,16,128]{4,3,2,1,0:T(8,128)S(1)}, u32[]{:S(2)}, u32[]{:S(2)}) collective-permute-start(f32[4,7,2,16,128]{4,3,2,1,0:T(8,128)S(1)} %pad_maximum_fusion.same), channel_id=1, source_target_pairs={{0,1},{1,0},{2,3},{3,2},{4,5},{5,4},{6,7},{7,6},{8,9},{9,8},{10,11... | collective-permute-start | bytes 1376264 | tf_op jit(solution)/shard_map/ppermute | solution.py:559
  12.6 6.9 %collective-permute-start.4 = (f32[2,136,128]{2,1,0:T(8,128)S(1)}, f32[2,136,128]{2,1,0:T(8,128)S(1)}, u32[]{:S(2)}, u32[]{:S(2)}) collective-permute-start(f32[2,136,128]{2,1,0:T(8,128)S(1)} %get-tuple-element.13), channel_id=1, source_target_pairs={{0,8},{2,10},{4,12},{6,14},{8,16},{9,1},{10,18},{11,3},{12,20},{13... | collective-permute-start | bytes 417800 | tf_op jit(solution)/shard_map/ppermute | solution.py:636
  32.1 5.6 %collective-permute-start.7 = (f32[2,88,128]{2,1,0:T(8,128)S(1)}, f32[2,88,128]{2,1,0:T(8,128)S(1)}, u32[]{:S(2)}, u32[]{:S(2)}) collective-permute-start(f32[2,88,128]{2,1,0:T(8,128)S(1)} %shard_map.107), channel_id=1, source_target_pairs={{0,6},{1,7},{2,4},{3,5},{4,2},{5,3},{6,0},{7,1},{8,14},{9,15},{10,... | collective-permute-start | bytes 270344 | tf_op jit(solution)/shard_map/ppermute | solution.py:559
  32.1 6.2 %collective-permute-start.6 = (f32[2,88,128]{2,1,0:T(8,128)S(1)}, f32[2,88,128]{2,1,0:T(8,128)S(1)}, u32[]{:S(2)}, u32[]{:S(2)}) collective-permute-start(f32[2,88,128]{2,1,0:T(8,128)S(1)} %shard_map.107), channel_id=1, source_target_pairs={{0,4},{1,5},{2,6},{3,7},{4,0},{5,1},{6,2},{7,3},{8,12},{9,13},{10,... | collective-permute-start | bytes 270344 | tf_op jit(solution)/shard_map/ppermute | solution.py:559
  34.8 4.5 %collective-permute-start.5 = (f32[2,88,128]{2,1,0:T(8,128)S(1)}, f32[2,88,128]{2,1,0:T(8,128)S(1)}, u32[]{:S(2)}, u32[]{:S(2)}) collective-permute-start(f32[2,88,128]{2,1,0:T(8,128)S(1)} %shard_map.107), channel_id=1, source_target_pairs={{0,2},{1,3},{2,0},{3,1},{4,6},{5,7},{6,4},{7,5},{8,10},{9,11},{10,... | collective-permute-start | bytes 270344 | tf_op jit(solution)/shard_map/ppermute | solution.py:559
  39.4 2.4 %collective-permute-start.8 = (f32[4,2,88,128]{3,2,1,0:T(8,128)S(1)}, f32[4,2,88,128]{3,2,1,0:T(8,128)S(1)}, u32[]{:S(2)}, u32[]{:S(2)}) collective-permute-start(f32[4,2,88,128]{3,2,1,0:T(8,128)S(1)} %pad_maximum_fusion.1.same_b), channel_id=1, source_target_pairs={{0,1},{1,0},{2,3},{3,2},{4,5},{5,4},{6,7},{7,6},{8,9},{9,8},{10,11... | collective-permute-start | bytes 1081352 | tf_op jit(solution)/shard_map/ppermute | solution.py:559

commit v3 on v2

--- a/solution.py
+++ b/solution.py
@@ -62,7 +62,7 @@
     half = same.shape[0]
     return [
         pltpu.make_async_copy(
-            held.at[:, pl.ds(0, fields)], table.at[pl.ds(side * half, half)], sem
+            held.at[:, pl.ds(0, fields)], table.at[pl.ds(side * half, half), pl.ds(0, fields)], sem
         )
         for side, held in enumerate((same, other))
     ]
@@ -155,20 +155,36 @@
     return jnp.broadcast_to(info[:, k : k + 1], (info.shape[0], LANES))
 
 
-def chunks_in(number):
-    return (number > 0.0).astype(I32) + (number > LANES).astype(I32)
-
-
-def list_chunks(entries, number, spare):
+def halves_in(number):
+    return sum((number > 64.0 * q).astype(I32) for q in range(4))
+
+
+def list_halves(entries, number, spare, other, half_at, spare_given=0, given_at=(0, 0)):
     lane = lax.broadcasted_iota(I32, number.shape, 1)
-    words = jnp.full(number.shape, spare, I32)
+    rows = jnp.full(number.shape, spare, I32)
+    givens = jnp.full(number.shape, spare_given, I32)
+    east, north = jnp.zeros(number.shape, F32), jnp.zeros(number.shape, F32)
     used = jnp.zeros(number.shape, I32)
-    for word, chunks in entries:
-        words = jnp.where((lane == used) & (chunks > 0), word, words)
-        words = jnp.where((lane == used + 1) & (chunks > 1), word + (1 << 10), words)
-        used = used + chunks
-    words = jnp.where(lane == USED, used, words)
-    return jnp.where(lane == LIVE, number.astype(I32), words)
+    for row, given, a, b, halves in entries:
+        moved = used & 1
+        row = row + moved * other
+        given = given + moved * given_at[0]
+        for q in range(4):
+            here = (lane == used + q) & (halves > q)
+            rows = jnp.where(here, row + (q >> 1) * half_at, rows)
+            givens = jnp.where(here, given + (q >> 1) * given_at[1], givens)
+        here = (lane >= used) & (lane < used + halves)
+        east = jnp.where(here, a, east)
+        north = jnp.where(here, b, north)
+        used = used + halves
+    rows = jnp.where(lane == USED, used, rows)
+    rows = jnp.where(lane == LIVE, number.astype(I32), rows)
+    return rows, givens, east, north
+
+
+def turned(values):
+    flat = pltpu.roll(values.reshape(-1, LANES), LANES // 2, 1)
+    return flat.reshape(values.shape)
 
 
 def place_of(column, row, me, half):
@@ -209,10 +225,6 @@
 def rows_of(low, high, tiles):
     low, high = low.T, high.T
     return [jnp.stack([low[k : k + tiles], high[k : k + tiles]]) for k in (0, 64)]
-
-
-def blocks_in(number):
-    return (number + 63) >> 6
 
 
 def spread_columns(tiles, number_of, east, north, columns, ready=None):
@@ -273,47 +285,51 @@
     lax.fori_loop(0, tiles, rest, 0)
 
 
-STEP = 2
-
-
-def sweep_tile(t, at_column, scale, columns, sums, words, rows_for, steps):
+def sweep_tile(t, at_column, scale, columns, sums, words, steps, rows_for):
     scale = jnp.broadcast_to(scale, (8, LANES))
-
-    def block(nb, carry):
-        at = pl.ds(pl.multiple_of(nb * 64, 64), 64)
-        x = columns[at_column, 0, at, :].reshape(8, 8, LANES)
-        y = columns[at_column, 1, at, :].reshape(8, 8, LANES)
+    left = lax.broadcasted_iota(I32, (8, LANES), 1) < LANES // 2
+
+    def chunk(i):
+        sides = []
+        for k in range(2):
+            u, v, c, d = [jnp.broadcast_to(row, (8, LANES)) for row in rows_for(t, i + k)]
+            sides.append((u + steps[0, t, i + k], v + steps[1, t, i + k], c, d))
+        u, v, c, d = [jnp.where(left, *pair) for pair in zip(*sides)]
+        fade = jnp.exp2(-scale * (u * u + v * v))
+        return u, v, c * c * fade, d * fade
+
+    def block(nb, size, step):
+        at = pl.ds(pl.multiple_of(nb * 64, 64), size)
+        x = columns[at_column, 0, at, :].reshape(size // 8, 8, LANES)
+        y = columns[at_column, 1, at, :].reshape(size // 8, 8, LANES)
 
         def some(p, sums_now):
             den, num = sums_now
-            for k in range(STEP):
-                word = words[t, STEP * p + k]
-                e = (word >> 11) & 15
-                u, v, c, d = rows_for(word)
-                u = jnp.broadcast_to(u, (8, LANES)) + steps[e]
-                v = jnp.broadcast_to(v, (8, LANES)) + steps[9 + e]
-                c = jnp.broadcast_to(c, (8, LANES))
-                d = jnp.broadcast_to(d, (8, LANES))
-                fade = jnp.exp2(-scale * (u * u + v * v))
+            for k in range(step):
+                u, v, c, d = chunk(2 * (step * p + k))
                 w = jnp.exp2(x * u + y * v)
-                den = den + w * (c * c * fade)
-                num = num + w * (d * fade)
+                den = den + w * c
+                num = num + w * d
             return den, num
 
-        zero = jnp.zeros((8, 8, LANES), F32)
-        steps_used = (words[t, USED] + STEP - 1) // STEP
-        den, num = lax.fori_loop(0, steps_used, some, (zero, zero))
-        sums[t, at, 0:LANES] = den.reshape(64, LANES)
-        sums[t, at, LANES : 2 * LANES] = num.reshape(64, LANES)
+        zero = jnp.zeros((size // 8, 8, LANES), F32)
+        trips = (words[0, t, USED] + 2 * step - 1) // (2 * step)
+        den, num = lax.fori_loop(0, trips, some, (zero, zero))
+        sums[t, at, 0:LANES] = den.reshape(size, LANES)
+        sums[t, at, LANES : 2 * LANES] = num.reshape(size, LANES)
+
+    number = words[0, t, LIVE]
+    whole = (number + 31) >> 6
+
+    def full(nb, carry):
+        block(nb, 64, 2)
         return carry
 
-    lax.fori_loop(0, blocks_in(words[t, LIVE]), block, 0)
-
-
-def set_steps(steps):
-    for e, (a, b) in enumerate(NEAR):
-        steps[e] = jnp.float32(a)
-        steps[9 + e] = jnp.float32(b)
+    lax.fori_loop(0, whole, full, 0)
+
+    @pl.when(number > whole * 64)
+    def _():
+        block(whole, 32, 4)
 
 
 def first_lists(near_info, edge_info, rows):
@@ -348,24 +364,27 @@
         for du in (-1, 0, 1):
             for b in (-1, 0, 1):
                 here, there = 3 * (du + 1) + b + 1, 3 * (1 - du) + b + 1
-                e = jnp.where(odd == 1, there, here)
-                chunks = chunks_in(lines[j + 1 + du][1 + b : 9 + b])
+                a = jnp.where(odd == 1, -du, du).astype(F32)
+                chunks = halves_in(lines[j + 1 + du][1 + b : 9 + b])
                 if here != 4:
                     taken = jnp.where(odd == 1, column_of(info, REACH + there), column_of(info, REACH + here))
                     chunks = jnp.where(taken > 0.5, chunks, 0)
-                entries.append((source(j + 1 + du, b) + (e << 11), chunks))
-        result.append(list_chunks(entries, column_of(info, COUNT), SPARE))
-    return jnp.concatenate(result, axis=0)
+                entries.append((source(j + 1 + du, b), 0, a, jnp.float32(b), chunks))
+        plane = NEAR_ROWS + EDGE_ROWS
+        result.append(list_halves(entries, column_of(info, COUNT), SPARE, 10 * plane, plane))
+    return [jnp.concatenate(parts, axis=0) for parts in zip(*result)]
 
 
 def first_kernel(
     near, near_columns, border, out,
-    table, own, east, north, low, high, columns, sums, listed,
+    table, own, east, north, low, high, columns, sums, listed, stepped,
     words, steps, sem, word_sem,
 ):
     rows = lax.axis_size("tile") * SLOTS // TX
     near_at, edge_at = pl.ds(0, NEAR_ROWS), pl.ds(NEAR_ROWS, EDGE_ROWS)
-    copies = [pltpu.make_async_copy(near.at[pl.ds(0, 6)], table.at[:, :, near_at], sem)]
+    copies = [
+        pltpu.make_async_copy(near.at[pl.ds(0, 6)], table.at[pl.ds(0, 6), :, near_at], sem)
+    ]
     for f, field in enumerate((EAST, NORTH, ONE, PART)):
         held = border.at[:, pl.ds(f * 24, 24)]
         copies.append(pltpu.make_async_copy(held, table.at[field, :, edge_at], sem))
@@ -375,10 +394,13 @@
     for copy in copies:
         copy.start()
     near_info, edge_info = near[INFO, 0], border[0, 4 * 24 : 5 * 24, :]
-    listed[...] = first_lists(near_info, edge_info, rows)
-    word_copy = pltpu.make_async_copy(listed, words, word_sem)
-    word_copy.start()
-    set_steps(steps)
+    listed[0], _, stepped[0], stepped[1] = first_lists(near_info, edge_info, rows)
+    word_copies = [
+        pltpu.make_async_copy(listed, words, word_sem),
+        pltpu.make_async_copy(stepped, steps, word_sem),
+    ]
+    for copy in word_copies:
+        copy.start()
     tiles = 24
     info = jnp.concatenate([edge_info[0:8], near_info[1:9], near_info[11:19]], axis=0)
     scales = scale_of(info[:, WIDTH : WIDTH + 1])
@@ -398,16 +420,25 @@
     north[...] = columns_of(2.0 * scale_rows[:, 0:8] * y[:, 0:8])
 
     def number_of(t):
-        return words[t, LIVE]
-
-    spread_columns(8, number_of, east, north, columns, word_copy.wait)
-
-    def rows_for(word):
-        at, h = pl.ds(word & 1023, 1), (word >> 10) & 1
-        return [table[field, h, at, :] for field in (EAST, NORTH, ONE, PART)]
+        return words[0, t, LIVE]
+
+    def ready():
+        for copy in word_copies:
+            copy.wait()
+
+    spread_columns(8, number_of, east, north, columns, ready)
+
+    table[6:10] = turned(table[EAST : PART + 1])
+
+    plane = 2 * (NEAR_ROWS + EDGE_ROWS)
+    flat = table.reshape(10 * plane, LANES)
+
+    def rows_for(t, i):
+        row = words[0, t, i]
+        return [flat[pl.ds(row + field * plane, 1), :] for field in (EAST, NORTH, ONE, PART)]
 
     def each(t, carry, held, skip):
-        sweep_tile(t, t - skip, own[pl.ds(t, 1), :], held, sums, words, rows_for, steps)
+        sweep_tile(t, t - skip, own[pl.ds(t, 1), :], held, sums, words, steps, rows_for)
         return carry
 
     lax.fori_loop(0, 8, lambda t, c: each(t, c, columns, 0), 0)
@@ -468,24 +499,27 @@
     entries = []
     for e, (a, b) in enumerate(NEAR):
         at = slice(e * tiles, (e + 1) * tiles)
-        chunks = chunks_in(lives[at])
+        chunks = halves_in(lives[at])
         if e != 4:
             chunks = jnp.where(column_of(mine, REACH + e) > 0.5, chunks, 0)
-        source = blocks[at].astype(I32) * SLOTS + slots[at].astype(I32)
+        row = blocks[at].astype(I32) * (12 * SLOTS) + slots[at].astype(I32)
         n, spot = place_of(column + a, across + b, me, half)
-        entries.append((source + (e << 11) + (n << 15) + (spot << 20), chunks))
-    spare = cells + edge + (88 << 20)
-    words = list_chunks(entries, column_of(mine, COUNT), spare)
-    lane = lax.broadcasted_iota(I32, words.shape, 1)
+        entries.append((row, n * 64 + spot, jnp.float32(a), jnp.float32(b), chunks))
+    count = 2 * half
+    spare = (cells + edge) // SLOTS * (12 * SLOTS)
+    rows, givens, east, north = list_halves(
+        entries, column_of(mine, COUNT), spare, 6 * SLOTS, SLOTS, 24, (count * 64, 32)
+    )
+    lane = lax.broadcasted_iota(I32, rows.shape, 1)
     n, spot = place_of(column, across, me, half)
-    words = jnp.where(lane == HOLDER, n, words)
-    return jnp.where(lane == HELD_AT, spot, words)
+    givens = jnp.where(lane == HOLDER, n, givens)
+    return rows, jnp.where(lane == HELD_AT, spot, givens), east, north
 
 
 def second_kernel(
     own_block, mine, columns, same, other, same_b, other_b,
     betas, hats, residual,
-    table, results, own, scales, low, high, sums, listed,
+    table, given, own, scales, low, high, sums, listed, stepped,
     words, steps, sem, word_sem,
 ):
     copies = fetch(same, other, table, 3, sem)
@@ -493,20 +527,24 @@
     blocks = 2 * half
     for side, held in enumerate((same_b, other_b)):
         at = pl.ds(side * half, half)
-        copies.append(pltpu.make_async_copy(held, results.at[at, :, pl.ds(0, 88)], sem))
+        to = given.at[0, at, :, pl.ds(0, 24)]
+        copies.append(pltpu.make_async_copy(held.at[:, :, pl.ds(0, 24)], to, sem))
     for copy in copies:
         copy.start()
-    listed[...] = second_lists(mine, same, other, same_b, other_b)
-    word_copy = pltpu.make_async_copy(listed, words, word_sem)
-    word_copy.start()
-    set_steps(steps)
+    listed[0], listed[1], stepped[0], stepped[1] = second_lists(mine, same, other, same_b, other_b)
+    word_copies = [
+        pltpu.make_async_copy(listed, words, word_sem),
+        pltpu.make_async_copy(stepped, steps, word_sem),
+    ]
+    for copy in word_copies:
+        copy.start()
     scales[...] = scale_of(mine[:, WIDTH : WIDTH + 1])
     present = records(tiles) < column_of(mine, COUNT)[None]
     scale_rows = scales[...][None]
     x, y = own_block[EAST], own_block[NORTH]
 
     def number_of(t):
-        return words[t, LIVE]
+        return words[0, t, LIVE]
 
     for n in range(2 * half):
         held = (same_b if n < half else other_b).at[n % half]
@@ -516,22 +554,37 @@
             ]
     for field in range(3):
         table[blocks + half, field, :, 0:8, :] = jnp.zeros((2, 8, LANES), F32)
-    results[0, :, 88:96, :] = jnp.zeros((2, 8, LANES), F32)
+    given[0, :, :, 24:32, :] = jnp.zeros((2 * half, 2, 8, LANES), F32)
     for copy in copies:
         copy.wait()
-    word_copy.wait()
-
-    def rows_for(word):
-        n, slot = split(word & 1023, SLOTS)
-        h = (word >> 10) & 1
-        held = [table[n, field, h, pl.ds(slot, 1), :] for field in (EAST, NORTH, TWO)]
-        return [*held, results[(word >> 15) & 31, h, pl.ds(word >> 20, 1), :]]
+
+    def turn(n, carry):
+        table[n, 3:6] = turned(table[n, 0:3])
+        return carry
+
+    def turn_given(n, carry):
+        given[1, n] = turned(given[0, n])
+        return carry
+
+    lax.fori_loop(0, table.shape[0], turn, 0)
+    lax.fori_loop(0, 2 * half, turn_given, 0)
+    for copy in word_copies:
+        copy.wait()
+
+    flat = table.reshape(table.shape[0] * 12 * SLOTS, LANES)
+    flat_given = given.reshape(2 * 2 * half * 64, LANES)
+
+    def rows_for(t, i):
+        row = words[0, t, i]
+        held = [flat[pl.ds(row + field * 2 * SLOTS, 1), :] for field in (EAST, NORTH, TWO)]
+        return [*held, flat_given[pl.ds(words[1, t, i], 1), :]]
 
     def each(t, carry):
-        n, at = words[t, HOLDER], words[t, HELD_AT]
-        own[0, :, pl.ds(t, 1), :] = results[n, :, pl.ds(16 + at, 1), :]
-        own[1, :, pl.ds(t, 1), :] = results[n, :, pl.ds(32 + at, 1), :]
-        sweep_tile(t, t, scales[pl.ds(t, 1), :], columns, sums, words, rows_for, steps)
+        n, at = words[1, t, HOLDER], words[1, t, HELD_AT]
+        for k in range(2):
+            here = (n & (half - 1), slice(None), pl.ds(16 * (k + 1) + at, 1), slice(None))
+            own[k, :, pl.ds(t, 1), :] = jnp.where(n >= half, other_b[here], same_b[here])
+        sweep_tile(t, t, scales[pl.ds(t, 1), :], columns, sums, words, steps, rows_for)
         return carry
 
     lax.fori_loop(0, tiles, each, 0)
@@ -640,7 +693,7 @@
         in_specs=[VMEM, VMEM, VMEM],
         out_specs=VMEM,
         scratch_shapes=[
-            pltpu.VMEM((6, 2, NEAR_ROWS + EDGE_ROWS, LANES), F32),
+            pltpu.VMEM((10, 2, NEAR_ROWS + EDGE_ROWS, LANES), F32),
             pltpu.VMEM((24, LANES), F32),
             square,
             square,
@@ -648,9 +701,10 @@
             square,
             pltpu.VMEM((8, 2, TILE, LANES), F32),
             pltpu.VMEM((24, TILE, 2 * LANES), F32),
-            pltpu.VMEM((24, LANES), I32),
-            pltpu.SMEM((24, LANES), I32),
-            pltpu.SMEM((18,), F32),
+            pltpu.VMEM((1, 24, LANES), I32),
+            pltpu.VMEM((2, 24, LANES), F32),
+            pltpu.SMEM((1, 24, LANES), I32),
+            pltpu.SMEM((2, 24, LANES), F32),
             dma,
             dma,
         ],
@@ -667,16 +721,17 @@
         in_specs=[VMEM] * 7,
         out_specs=(VMEM, VMEM, VMEM),
         scratch_shapes=[
-            pltpu.VMEM((count + count // 2 + 1, 3, 2, tiles, LANES), F32),
-            pltpu.VMEM((count, 2, 96, LANES), F32),
+            pltpu.VMEM((count + count // 2 + 1, 6, 2, tiles, LANES), F32),
+            pltpu.VMEM((2, count, 2, 32, LANES), F32),
             pltpu.VMEM((2, 2, tiles, LANES), F32),
             pltpu.VMEM((tiles, LANES), F32),
             square,
             square,
             pltpu.VMEM((tiles, TILE, 2 * LANES), F32),
-            pltpu.VMEM((tiles, LANES), I32),
-            pltpu.SMEM((tiles, LANES), I32),
-            pltpu.SMEM((18,), F32),
+            pltpu.VMEM((2, tiles, LANES), I32),
+            pltpu.VMEM((2, tiles, LANES), F32),
+            pltpu.SMEM((2, tiles, LANES), I32),
+            pltpu.SMEM((2, tiles, LANES), F32),
             dma,
             dma,
         ],

time: 53 us -> 49.9 us (0.942)
  the two profiles are of different devices: /device:TPU:16 before, /device:TPU:25 now
where the time goes in v3:
time: 49.9 us
  Pallas kernels  23.3 us (47%)
  starting transfers between devices  16.8 us (34%)
  waiting for transfers between devices  9.01 us (18%)
  between operations  0.72 us (1%)
    ppermute x8, starting transfers between devices, swap(): return lax.ppermute(x, 'tile', [(i, i ^ k) for i in range(count)])  14.7 us
    ppermute x8, waiting for transfers between devices, swap(): return lax.ppermute(x, 'tile', [(i, i ^ k) for i in range(count)])  9.01 us
    pallas_call x1, Pallas kernels, body(): pl.pallas_call(first_kernel, out_shape=jax.ShapeDtypeStruct((2, 88, LANES...  8.96 us
    pallas_call x1, Pallas kernels, body(): pl.pallas_call(second_kernel, out_shape=(jax.ShapeDtypeStruct((2, wide),...  8.61 us
    pallas_call x1, Pallas kernels, body(): pl.pallas_call(near_kernel, out_shape=pltpu.VMEM((16, 2, TILE, LANES), F3...  2.31 us
    ppermute x1, starting transfers between devices, body(): border = lax.ppermute(edge, ('region', 'tile'), moves)  2.08 us
    pallas_call x1, Pallas kernels, body(): pl.pallas_call(own_columns_kernel, out_shape=pltpu.VMEM((tiles, 2, TILE,...  1.74 us
    pallas_call x1, Pallas kernels, body(): pl.pallas_call(prepare_kernel, out_shape=(pltpu.VMEM((7, 2, tiles, LANES)...  1.18 us
  transfers between devices with their start and end apart: 9, of which 5 were waited for; matrix products, arithmetic and copies ran while one was open for 0% of the time, Pallas kernels for 8%

profile of v3, /device:TPU:25, one launch (start us, length us, event | category | flops | bytes accessed | tf_op | source)
XLA Modules:
  0.0 49.9 jit_solution(14895787408384345194)
XLA Ops:
  0.6 1.2 %shard_map.103 = (f32[7,2,16,128]{3,2,1,0:T(8,128)S(1)}, f32[16,128]{1,0:T(8,128)S(1)}) custom-call(f32[2,4096]{1,0:T(2,128)} %refs_0_.1, f32[2,4096]{1,0:T(2,128)} %refs_1_.1, f32[1,4096]{1,0:T(1,128)} %bitcast.20, f32[1,4096]{1,0:T(1,128)} %bitcast.21, s32[16]{0:T(128)} %refs_4_.1, s32[2,16]{1,0:T(2,128)} %refs_5_.1, s32[9,2,16]{2,1,0:T(2,128)} %bitcast.22, ...), custom_call_target="tpu_custom_call" | custom-call | tf_op jit(solution)/shard_map/pallas_call | solution.py:633
  1.8 2.2 %collective-permute-start.2 = (f32[7,2,16,128]{3,2,1,0:T(8,128)S(1)}, f32[7,2,16,128]{3,2,1,0:T(8,128)S(1)}, u32[]{:S(2)}, u32[]{:S(2)}) collective-permute-start(f32[7,2,16,128]{3,2,1,0:T(8,128)S(1)} %get-tuple-element.10.block.own_block), channel_id=1, source_target_pairs={{0,6},{1,7},{2,4},{3,5},{4,2},{5,3},{6,0},{7,1},{8,14},{9,15},{10,... | collective-permute-start | bytes 344072 | tf_op jit(solution)/shard_map/ppermute | solution.py:612
  4.0 0.2 collective-permute-start.1
  4.3 0.3 collective-permute-start
  4.5 2.3 %collective-permute-done.2 = f32[7,2,16,128]{3,2,1,0:T(8,128)S(1)} collective-permute-done((f32[7,2,16,128]{3,2,1,0:T(8,128)S(1)}, f32[7,2,16,128]{3,2,1,0:T(8,128)S(1)}, u32[]{:S(2)}, u32[]{:S(2)}) %collective-permute-start.2) | collective-permute-done | bytes 114720 | tf_op jit(solution)/shard_map/ppermute | solution.py:612
  6.8 3.4 %collective-permute-done.1 = f32[7,2,16,128]{3,2,1,0:T(8,128)S(1)} collective-permute-done((f32[7,2,16,128]{3,2,1,0:T(8,128)S(1)}, f32[7,2,16,128]{3,2,1,0:T(8,128)S(1)}, u32[]{:S(2)}, u32[]{:S(2)}) %collective-permute-start.1) | collective-permute-done | bytes 114720 | tf_op jit(solution)/shard_map/ppermute | solution.py:612
  10.2 0.0 collective-permute-done
  10.2 0.7 %collective-permute-start.3 = (f32[4,7,2,16,128]{4,3,2,1,0:T(8,128)S(1)}, f32[4,7,2,16,128]{4,3,2,1,0:T(8,128)S(1)}, u32[]{:S(2)}, u32[]{:S(2)}) collective-permute-start(f32[4,7,2,16,128]{4,3,2,1,0:T(8,128)S(1)} %pad_maximum_fusion.same), channel_id=1, source_target_pairs={{0,1},{1,0},{2,3},{3,2},{4,5},{5,4},{6,7},{7,6},{8,9},{9,8},{10,11... | collective-permute-start | bytes 1376264 | tf_op jit(solution)/shard_map/ppermute | solution.py:612
  11.0 1.4 %collective-permute-done.3.other = f32[4,7,2,16,128]{4,3,2,1,0:T(8,128)S(1)} collective-permute-done((f32[4,7,2,16,128]{4,3,2,1,0:T(8,128)S(1)}, f32[4,7,2,16,128]{4,3,2,1,0:T(8,128)S(1)}, u32[]{:S(2)}, u32[]{:S(2)}) %collective-permute-start.3) | collective-permute-done | bytes 458784 | tf_op jit(solution)/shard_map/ppermute | solution.py:612
  12.4 0.5 %shard_map.105 = (f32[2,136,128]{2,1,0:T(8,128)S(1)}, f32[7,2,32,128]{3,2,1,0:T(8,128)S(1)}) custom-call(f32[4,7,2,16,128]{4,3,2,1,0:T(8,128)S(1)} %pad_maximum_fusion.same, f32[4,7,2,16,128]{4,3,2,1,0:T(8,128)S(1)} %collective-permute-done.3.other), custom_call_target="tpu_custom_call" | custom-call | tf_op jit(solution)/shard_map/pallas_call | solution.py:664
  12.9 2.1 %collective-permute-start.4 = (f32[2,136,128]{2,1,0:T(8,128)S(1)}, f32[2,136,128]{2,1,0:T(8,128)S(1)}, u32[]{:S(2)}, u32[]{:S(2)}) collective-permute-start(f32[2,136,128]{2,1,0:T(8,128)S(1)} %get-tuple-element.13), channel_id=1, source_target_pairs={{0,8},{2,10},{4,12},{6,14},{8,16},{9,1},{10,18},{11,3},{12,20},{13... | collective-permute-start | bytes 417800 | tf_op jit(solution)/shard_map/ppermute | solution.py:689
  15.0 2.3 %shard_map.106.near_columns = f32[16,2,256,128]{3,2,1,0:T(8,128)S(1)} custom-call(f32[7,2,32,128]{3,2,1,0:T(8,128)S(1)} %get-tuple-element.12.near), custom_call_target="tpu_custom_call" | custom-call | flops 4000000 | bytes 4000000 | tf_op jit(solution)/shard_map/pallas_call | solution.py:674
  17.3 0.0 collective-permute-done.4.border
  17.3 9.0 %shard_map.107 = f32[2,88,128]{2,1,0:T(8,128)S(1)} custom-call(f32[7,2,32,128]{3,2,1,0:T(8,128)S(1)} %get-tuple-element.12.near, f32[16,2,256,128]{3,2,1,0:T(8,128)S(1)} %shard_map.106.near_columns, f32[2,136,128]{2,1,0:T(8,128)S(1)} %collective-permute-done.4.border), custom_call_target="tpu_custom_call" | custom-call | tf_op jit(solution)/shard_map/pallas_call | solution.py:690
  26.3 0.1 collective-permute-start.7
  26.4 0.1 collective-permute-start.6
  26.5 2.6 %collective-permute-start.5 = (f32[2,88,128]{2,1,0:T(8,128)S(1)}, f32[2,88,128]{2,1,0:T(8,128)S(1)}, u32[]{:S(2)}, u32[]{:S(2)}) collective-permute-start(f32[2,88,128]{2,1,0:T(8,128)S(1)} %shard_map.107), channel_id=1, source_target_pairs={{0,2},{1,3},{2,0},{3,1},{4,6},{5,7},{6,4},{7,5},{8,10},{9,11},{10,... | collective-permute-start | bytes 270344 | tf_op jit(solution)/shard_map/ppermute | solution.py:612
  29.0 1.7 %collective-permute-done.7 = f32[2,88,128]{2,1,0:T(8,128)S(1)} collective-permute-done((f32[2,88,128]{2,1,0:T(8,128)S(1)}, f32[2,88,128]{2,1,0:T(8,128)S(1)}, u32[]{:S(2)}, u32[]{:S(2)}) %collective-permute-start.7) | collective-permute-done | bytes 90144 | tf_op jit(solution)/shard_map/ppermute | solution.py:612
  30.8 0.0 collective-permute-done.6
  30.8 0.1 collective-permute-done.5
  31.0 8.6 %collective-permute-start.8 = (f32[4,2,88,128]{3,2,1,0:T(8,128)S(1)}, f32[4,2,88,128]{3,2,1,0:T(8,128)S(1)}, u32[]{:S(2)}, u32[]{:S(2)}) collective-permute-start(f32[4,2,88,128]{3,2,1,0:T(8,128)S(1)} %pad_maximum_fusion.1.same_b), channel_id=1, source_target_pairs={{0,1},{1,0},{2,3},{3,2},{4,5},{5,4},{6,7},{7,6},{8,9},{9,8},{10,11... | collective-permute-start | bytes 1081352 | tf_op jit(solution)/shard_map/ppermute | solution.py:612
  39.5 1.7 %shard_map.104.columns = f32[16,2,256,128]{3,2,1,0:T(8,128)S(1)} custom-call(f32[7,2,16,128]{3,2,1,0:T(8,128)S(1)} %get-tuple-element.10.block.own_block, f32[16,128]{1,0:T(8,128)S(1)} %get-tuple-element.11.mine), custom_call_target="tpu_custom_call" | custom-call | flops 4000000 | bytes 4000000 | tf_op jit(solution)/shard_map/pallas_call | solution.py:654
  41.3 0.0 collective-permute-done.8.other_b
  41.3 8.6 %shard_map.108 = (f32[2,4096]{1,0:T(2,128)}, f32[2,4096]{1,0:T(2,128)}, f32[1,4096]{1,0:T(1,128)}) custom-call(f32[7,2,16,128]{3,2,1,0:T(8,128)S(1)} %get-tuple-element.10.block.own_block, f32[16,128]{1,0:T(8,128)S(1)} %get-tuple-element.11.mine, f32[16,2,256,128]{3,2,1,0:T(8,128)S(1)} %shard_map.104.columns, ...), custom_call_target="tpu_custom_call" | custom-call | tf_op jit(solution)/shard_map/pallas_call | solution.py:714
  (2 shorter events, 0.1 us)
Async XLA Ops:
  1.8 5.0 %collective-permute-start.2 = (f32[7,2,16,128]{3,2,1,0:T(8,128)S(1)}, f32[7,2,16,128]{3,2,1,0:T(8,128)S(1)}, u32[]{:S(2)}, u32[]{:S(2)}) collective-permute-start(f32[7,2,16,128]{3,2,1,0:T(8,128)S(1)} %get-tuple-element.10.block.own_block), channel_id=1, source_target_pairs={{0,6},{1,7},{2,4},{3,5},{4,2},{5,3},{6,0},{7,1},{8,14},{9,15},{10,... | collective-permute-start | bytes 344072 | tf_op jit(solution)/shard_map/ppermute | solution.py:612
  4.0 6.1 %collective-permute-start.1 = (f32[7,2,16,128]{3,2,1,0:T(8,128)S(1)}, f32[7,2,16,128]{3,2,1,0:T(8,128)S(1)}, u32[]{:S(2)}, u32[]{:S(2)}) collective-permute-start(f32[7,2,16,128]{3,2,1,0:T(8,128)S(1)} %get-tuple-element.10.block.own_block), channel_id=1, source_target_pairs={{0,4},{1,5},{2,6},{3,7},{4,0},{5,1},{6,2},{7,3},{8,12},{9,13},{10,... | collective-permute-start | bytes 344072 | tf_op jit(solution)/shard_map/ppermute | solution.py:612
  4.3 5.9 %collective-permute-start = (f32[7,2,16,128]{3,2,1,0:T(8,128)S(1)}, f32[7,2,16,128]{3,2,1,0:T(8,128)S(1)}, u32[]{:S(2)}, u32[]{:S(2)}) collective-permute-start(f32[7,2,16,128]{3,2,1,0:T(8,128)S(1)} %get-tuple-element.10.block.own_block), channel_id=1, source_target_pairs={{0,2},{1,3},{2,0},{3,1},{4,6},{5,7},{6,4},{7,5},{8,10},{9,11},{10,... | collective-permute-start | bytes 344072 | tf_op jit(solution)/shard_map/ppermute | solution.py:612
  10.2 2.2 %collective-permute-start.3 = (f32[4,7,2,16,128]{4,3,2,1,0:T(8,128)S(1)}, f32[4,7,2,16,128]{4,3,2,1,0:T(8,128)S(1)}, u32[]{:S(2)}, u32[]{:S(2)}) collective-permute-start(f32[4,7,2,16,128]{4,3,2,1,0:T(8,128)S(1)} %pad_maximum_fusion.same), channel_id=1, source_target_pairs={{0,1},{1,0},{2,3},{3,2},{4,5},{5,4},{6,7},{7,6},{8,9},{9,8},{10,11... | collective-permute-start | bytes 1376264 | tf_op jit(solution)/shard_map/ppermute | solution.py:612
  12.9 4.4 %collective-permute-start.4 = (f32[2,136,128]{2,1,0:T(8,128)S(1)}, f32[2,136,128]{2,1,0:T(8,128)S(1)}, u32[]{:S(2)}, u32[]{:S(2)}) collective-permute-start(f32[2,136,128]{2,1,0:T(8,128)S(1)} %get-tuple-element.13), channel_id=1, source_target_pairs={{0,8},{2,10},{4,12},{6,14},{8,16},{9,1},{10,18},{11,3},{12,20},{13... | collective-permute-start | bytes 417800 | tf_op jit(solution)/shard_map/ppermute | solution.py:689
  26.3 4.5 %collective-permute-start.7 = (f32[2,88,128]{2,1,0:T(8,128)S(1)}, f32[2,88,128]{2,1,0:T(8,128)S(1)}, u32[]{:S(2)}, u32[]{:S(2)}) collective-permute-start(f32[2,88,128]{2,1,0:T(8,128)S(1)} %shard_map.107), channel_id=1, source_target_pairs={{0,6},{1,7},{2,4},{3,5},{4,2},{5,3},{6,0},{7,1},{8,14},{9,15},{10,... | collective-permute-start | bytes 270344 | tf_op jit(solution)/shard_map/ppermute | solution.py:612
  26.4 4.4 %collective-permute-start.6 = (f32[2,88,128]{2,1,0:T(8,128)S(1)}, f32[2,88,128]{2,1,0:T(8,128)S(1)}, u32[]{:S(2)}, u32[]{:S(2)}) collective-permute-start(f32[2,88,128]{2,1,0:T(8,128)S(1)} %shard_map.107), channel_id=1, source_target_pairs={{0,4},{1,5},{2,6},{3,7},{4,0},{5,1},{6,2},{7,3},{8,12},{9,13},{10,... | collective-permute-start | bytes 270344 | tf_op jit(solution)/shard_map/ppermute | solution.py:612
  26.5 4.5 %collective-permute-start.5 = (f32[2,88,128]{2,1,0:T(8,128)S(1)}, f32[2,88,128]{2,1,0:T(8,128)S(1)}, u32[]{:S(2)}, u32[]{:S(2)}) collective-permute-start(f32[2,88,128]{2,1,0:T(8,128)S(1)} %shard_map.107), channel_id=1, source_target_pairs={{0,2},{1,3},{2,0},{3,1},{4,6},{5,7},{6,4},{7,5},{8,10},{9,11},{10,... | collective-permute-start | bytes 270344 | tf_op jit(solution)/shard_map/ppermute | solution.py:612
  31.0 10.3 %collective-permute-start.8 = (f32[4,2,88,128]{3,2,1,0:T(8,128)S(1)}, f32[4,2,88,128]{3,2,1,0:T(8,128)S(1)}, u32[]{:S(2)}, u32[]{:S(2)}) collective-permute-start(f32[4,2,88,128]{3,2,1,0:T(8,128)S(1)} %pad_maximum_fusion.1.same_b), channel_id=1, source_target_pairs={{0,1},{1,0},{2,3},{3,2},{4,5},{5,4},{6,7},{7,6},{8,9},{9,8},{10,11... | collective-permute-start | bytes 1081352 | tf_op jit(solution)/shard_map/ppermute | solution.py:612

commit v4 on v3

--- a/solution.py
+++ b/solution.py
@@ -134,18 +134,46 @@
     return jnp.concatenate([near[field, :, 1:9, :], near[field, :, 11:19, :]], axis=1)
 
 
-def near_kernel(near, columns, east, north, facts, sem):
+def near_kernel(
+    near, columns, sums,
+    table, own, east, north, listed, stepped, facts, words, steps, sem, word_sem,
+):
     copy = pltpu.make_async_copy(near.at[INFO, 0], facts, sem)
     copy.start()
+    rows = lax.axis_size("tile") * SLOTS // TX
+    near_info = near[INFO, 0]
+    listed[0], _, stepped[0], stepped[1] = first_lists(near_info, None, rows, (2,), 4, NEAR_ROWS)
+    word_copies = [
+        pltpu.make_async_copy(listed, words, word_sem),
+        pltpu.make_async_copy(stepped, steps, word_sem),
+    ]
+    for word_copy in word_copies:
+        word_copy.start()
     info = targets_of(near, INFO)[0]
-    scale = scale_of(info[:, WIDTH : WIDTH + 1])[None]
+    own[...] = scale_of(info[:, WIDTH : WIDTH + 1])
+    scale = own[...][None]
     east[...] = columns_of(2.0 * scale * targets_of(near, EAST))
     north[...] = columns_of(2.0 * scale * targets_of(near, NORTH))
+    table[0:4] = near[EAST : PART + 1]
+    table[4:8] = turned(near[EAST : PART + 1])
 
     def number_of(t):
         return facts[(t >> 3) * 10 + (t & 7) + 1, COUNT].astype(I32)
 
     spread_columns(16, number_of, east, north, columns, copy.wait)
+    for word_copy in word_copies:
+        word_copy.wait()
+    flat = table.reshape(16 * NEAR_ROWS, LANES)
+
+    def rows_for(t, i):
+        row = words[0, t, i]
+        return [flat[pl.ds(row + k * 2 * NEAR_ROWS, 1), :] for k in range(4)]
+
+    def each(t, carry):
+        sweep_tile(t, t + 8, own[pl.ds(t + 8, 1), :], columns, sums, words, steps, rows_for)
+        return carry
+
+    lax.fori_loop(0, 8, each, 0)
 
 
 USED, LIVE, HOLDER, HELD_AT = 100, 101, 102, 103
@@ -252,37 +280,57 @@
             lay(t, 3, (east[64:128, :], north[64:128, :]))
 
 
-def collect_sums(tiles, number_of, sums, low_ref, high_ref):
-    split_at = lax.broadcasted_iota(I32, (2 * LANES, LANES), 0) // LANES
-    sides = lax.broadcasted_iota(I32, (2 * LANES, LANES), 1) // 64
+SHARE = 3
+GROUP = 4
+
+
+def collect_sums(parts, number_of, low_ref, high_ref, large):
+    split_at = (lax.broadcasted_iota(I32, (4 * LANES, LANES), 0) // LANES) & 1
+    sides = lax.broadcasted_iota(I32, (4 * LANES, LANES), 1) // 64
     ones = (split_at == sides).astype(F32).astype(jnp.bfloat16)
-    lane = lax.broadcasted_iota(I32, (64, LANES), 1) & 63
+    place = lax.broadcasted_iota(I32, (64, LANES), 1)
+    lane = place & 63
 
     def total(values):
         high = values.astype(jnp.bfloat16)
         low = (values - high.astype(F32)).astype(jnp.bfloat16)
-        return jnp.dot(high, ones, preferred_element_type=F32) + jnp.dot(
-            low, ones, preferred_element_type=F32
-        )
+        return jnp.dot(jnp.concatenate([high, low], axis=1), ones, preferred_element_type=F32)
 
     for nb in range(2):
         result = jnp.zeros((64, LANES), F32)
-        for t in range(tiles):
-            x = total(sums[t, nb * 64 : nb * 64 + 64, :])
-            result = jnp.where(lane == t, x, result)
+        held = [(sums, t) for sums, tiles in parts for t in range(tiles)]
+        for i, (sums, t) in enumerate(held):
+            values = sums[t, nb * 64 : nb * 64 + 64, :]
+            if i % SHARE == SHARE - 1:
+                for k in range(2):
+                    x = jnp.sum(values[:, k * LANES : (k + 1) * LANES], axis=1, keepdims=True)
+                    result = jnp.where(place == k * 64 + i, x, result)
+            else:
+                result = jnp.where(lane == i, total(values), result)
         low_ref[nb * 64 : nb * 64 + 64, :] = result
     high_ref[...] = jnp.zeros_like(high_ref)
 
-    def rest(t, carry):
-        @pl.when(number_of(t) > 128)
-        def _():
-            x = total(sums[t, 128:256, :])
-            mine = lax.broadcasted_iota(I32, (128, LANES), 1) & 63
-            high_ref[...] = jnp.where(mine == t, x, high_ref[...])
-
-        return carry
-
-    lax.fori_loop(0, tiles, rest, 0)
+    start = 0
+    for sums, tiles in parts:
+        many = jnp.int32(0)
+        for t in range(tiles):
+            large[many] = jnp.int32(t)
+            many = many + (number_of(start + t) > 128).astype(I32)
+        last = large[jnp.maximum(many - 1, 0)]
+        for k in range(GROUP - 1):
+            large[many + k] = last
+
+        def some(g, carry, sums=sums, start=start):
+            result = high_ref[...]
+            for i in range(GROUP):
+                t = large[g * GROUP + i]
+                mine = (lax.broadcasted_iota(I32, (LANES, LANES), 1) & 63) == start + t
+                result = jnp.where(mine, total(sums[t, 128:256, :]), result)
+            high_ref[...] = result
+            return carry
+
+        lax.fori_loop(0, (many + GROUP - 1) // GROUP, some, 0)
+        start += tiles
 
 
 def sweep_tile(t, at_column, scale, columns, sums, words, steps, rows_for):
@@ -332,15 +380,20 @@
         block(whole, 32, 4)
 
 
-def first_lists(near_info, edge_info, rows):
+def first_lists(near_info, edge_info, rows, groups, fields, plane):
     me = lax.axis_index("tile")
     odd = me & 1
     first = (me >> 1) * 8
-    near_live, edge_live = column_of(near_info, COUNT), column_of(edge_info, COUNT)
+    near_live = column_of(near_info, COUNT)
+    if edge_info is not None:
+        edge_live = column_of(edge_info, COUNT)
     step = lax.broadcasted_iota(I32, (8, LANES), 0)
     on_map = [(first > 0).astype(F32), (first + 8 < rows).astype(F32)]
     lines = []
     for u in range(5):
+        if u < 2 and edge_info is None:
+            lines.append(None)
+            continue
         if u < 2:
             away = 1 - u
             parts = [edge_live[i : i + n] for i, n in ((16 + 2 * away, 1), (8 * away, 8), (17 + 2 * away, 1))]
@@ -359,9 +412,12 @@
         return jnp.where(step == (0 if b < 0 else 7), corner, at)
 
     result = []
-    for j, info in enumerate((edge_info[0:8], near_info[1:9], near_info[11:19])):
+    infos = (None if edge_info is None else edge_info[0:8], near_info[1:9], near_info[11:19])
+    for j, info in enumerate(infos):
+        if info is None or (edge_info is None and j not in groups):
+            continue
         entries = []
-        for du in (-1, 0, 1):
+        for du in (-1, 0, 1) if j in groups else ():
             for b in (-1, 0, 1):
                 here, there = 3 * (du + 1) + b + 1, 3 * (1 - du) + b + 1
                 a = jnp.where(odd == 1, -du, du).astype(F32)
@@ -370,15 +426,15 @@
                     taken = jnp.where(odd == 1, column_of(info, REACH + there), column_of(info, REACH + here))
                     chunks = jnp.where(taken > 0.5, chunks, 0)
                 entries.append((source(j + 1 + du, b), 0, a, jnp.float32(b), chunks))
-        plane = NEAR_ROWS + EDGE_ROWS
-        result.append(list_halves(entries, column_of(info, COUNT), SPARE, 10 * plane, plane))
+        moved = 2 * fields * plane
+        result.append(list_halves(entries, column_of(info, COUNT), SPARE, moved, plane))
     return [jnp.concatenate(parts, axis=0) for parts in zip(*result)]
 
 
 def first_kernel(
-    near, near_columns, border, out,
+    near, near_columns, near_sums, border, out,
     table, own, east, north, low, high, columns, sums, listed, stepped,
-    words, steps, sem, word_sem,
+    words, steps, large, sem, word_sem,
 ):
     rows = lax.axis_size("tile") * SLOTS // TX
     near_at, edge_at = pl.ds(0, NEAR_ROWS), pl.ds(NEAR_ROWS, EDGE_ROWS)
@@ -394,7 +450,9 @@
     for copy in copies:
         copy.start()
     near_info, edge_info = near[INFO, 0], border[0, 4 * 24 : 5 * 24, :]
-    listed[0], _, stepped[0], stepped[1] = first_lists(near_info, edge_info, rows)
+    listed[0], _, stepped[0], stepped[1] = first_lists(
+        near_info, edge_info, rows, (0, 1), 5, NEAR_ROWS + EDGE_ROWS
+    )
     word_copies = [
         pltpu.make_async_copy(listed, words, word_sem),
         pltpu.make_async_copy(stepped, steps, word_sem),
@@ -442,8 +500,8 @@
         return carry
 
     lax.fori_loop(0, 8, lambda t, c: each(t, c, columns, 0), 0)
-    lax.fori_loop(8, tiles, lambda t, c: each(t, c, near_columns, 8), 0)
-    collect_sums(tiles, number_of, sums, low, high)
+    lax.fori_loop(8, 16, lambda t, c: each(t, c, near_columns, 8), 0)
+    collect_sums([(sums, 16), (near_sums, 8)], number_of, low, high, large)
     shrink = jnp.exp2(-scale_rows * (x * x + y * y))
     den, num = rows_of(low[...], high[...], tiles)
     inv = 1.0 / (1.0 + shrink * den)
@@ -520,7 +578,7 @@
     own_block, mine, columns, same, other, same_b, other_b,
     betas, hats, residual,
     table, given, own, scales, low, high, sums, listed, stepped,
-    words, steps, sem, word_sem,
+    words, steps, large, sem, word_sem,
 ):
     copies = fetch(same, other, table, 3, sem)
     half, _, _, tiles, _ = same.shape
@@ -588,7 +646,7 @@
         return carry
 
     lax.fori_loop(0, tiles, each, 0)
-    collect_sums(tiles, number_of, sums, low, high)
+    collect_sums([(sums, tiles)], number_of, low, high, large)
     shrink = jnp.exp2(-scale_rows * (x * x + y * y))
     den, num = rows_of(low[...], high[...], tiles)
     inv = 1.0 / (1.0 + shrink * den)
@@ -671,12 +729,27 @@
         out_specs=(VMEM, VMEM),
         compiler_params=limit,
     )(same, other)
-    near_columns = pl.pallas_call(
+    near_columns, near_sums = pl.pallas_call(
         near_kernel,
-        out_shape=pltpu.VMEM((16, 2, TILE, LANES), F32),
+        out_shape=(
+            pltpu.VMEM((16, 2, TILE, LANES), F32),
+            pltpu.VMEM((8, TILE, 2 * LANES), F32),
+        ),
         in_specs=[VMEM],
-        out_specs=VMEM,
-        scratch_shapes=[square, square, pltpu.SMEM((NEAR_ROWS, LANES), F32), dma],
+        out_specs=(VMEM, VMEM),
+        scratch_shapes=[
+            pltpu.VMEM((8, 2, NEAR_ROWS, LANES), F32),
+            pltpu.VMEM((16, LANES), F32),
+            square,
+            square,
+            pltpu.VMEM((1, 8, LANES), I32),
+            pltpu.VMEM((2, 8, LANES), F32),
+            pltpu.SMEM((NEAR_ROWS, LANES), F32),
+            pltpu.SMEM((1, 8, LANES), I32),
+            pltpu.SMEM((2, 8, LANES), F32),
+            dma,
+            dma,
+        ],
         compiler_params=limit,
         cost_estimate=pl.CostEstimate(flops=4000000, bytes_accessed=4000000, transcendentals=0),
     )(near)
@@ -690,7 +763,7 @@
     first = pl.pallas_call(
         first_kernel,
         out_shape=jax.ShapeDtypeStruct((2, 88, LANES), F32),
-        in_specs=[VMEM, VMEM, VMEM],
+        in_specs=[VMEM] * 4,
         out_specs=VMEM,
         scratch_shapes=[
             pltpu.VMEM((10, 2, NEAR_ROWS + EDGE_ROWS, LANES), F32),
@@ -700,16 +773,17 @@
             square,
             square,
             pltpu.VMEM((8, 2, TILE, LANES), F32),
-            pltpu.VMEM((24, TILE, 2 * LANES), F32),
+            pltpu.VMEM((16, TILE, 2 * LANES), F32),
             pltpu.VMEM((1, 24, LANES), I32),
             pltpu.VMEM((2, 24, LANES), F32),
             pltpu.SMEM((1, 24, LANES), I32),
             pltpu.SMEM((2, 24, LANES), F32),
+            pltpu.SMEM((24,), I32),
             dma,
             dma,
         ],
         compiler_params=limit,
-    )(near, near_columns, border)
+    )(near, near_columns, near_sums, border)
     same_b, other_b = spread(first)
     betas, hats, residual = pl.pallas_call(
         second_kernel,
@@ -732,6 +806,7 @@
             pltpu.VMEM((2, tiles, LANES), F32),
             pltpu.SMEM((2, tiles, LANES), I32),
             pltpu.SMEM((2, tiles, LANES), F32),
+            pltpu.SMEM((24,), I32),
             dma,
             dma,
         ],

time: 49.9 us -> 46.1 us (0.924)
  Pallas kernels: 23.3 us -> 16.4 us
  starting transfers between devices: 16.8 us -> 18.3 us
  waiting for transfers between devices: 9.01 us -> 10.3 us
    pallas_call x1, Pallas kernels: 8.96 us -> 3.39 us  [body(): pl.pallas_call(first_kernel, out_shape=jax.ShapeDtypeStruct((2, 88, LANES...]
    ppermute x8, starting transfers between devices: 14.7 us -> 16.2 us  [swap(): return lax.ppermute(x, 'tile', [(i, i ^ k) for i in range(count)])]
    pallas_call x1, Pallas kernels: 8.61 us -> 7.17 us  [body(): pl.pallas_call(second_kernel, out_shape=(jax.ShapeDtypeStruct((2, wide),...]
    ppermute x8, waiting for transfers between devices: 9.01 us -> 10.3 us  [swap(): return lax.ppermute(x, 'tile', [(i, i ^ k) for i in range(count)])]
  transfers between devices with their start and end apart: 9 -> 9, of which waited for: 5 -> 6; matrix products, arithmetic and copies ran while one was open for 0% -> 0% of each run, Pallas kernels for 8% -> 9%
where the time goes in v4:
time: 46.1 us; the launch traced here: 45.7 us
  starting transfers between devices  18.3 us (40%)
  Pallas kernels  16.4 us (36%)
  waiting for transfers between devices  10.3 us (22%)
  between operations  0.7 us (2%)
    ppermute x8, starting transfers between devices, swap(): return lax.ppermute(x, 'tile', [(i, i ^ k) for i in range(count)])  16.2 us
    ppermute x8, waiting for transfers between devices, swap(): return lax.ppermute(x, 'tile', [(i, i ^ k) for i in range(count)])  10.3 us
    pallas_call x1, Pallas kernels, body(): pl.pallas_call(second_kernel, out_shape=(jax.ShapeDtypeStruct((2, wide),...  7.17 us
    pallas_call x1, Pallas kernels, body(): pl.pallas_call(first_kernel, out_shape=jax.ShapeDtypeStruct((2, 88, LANES...  3.39 us
    pallas_call x1, Pallas kernels, body(): pl.pallas_call(near_kernel, out_shape=(pltpu.VMEM((16, 2, TILE, LANES), F...  2.65 us
    ppermute x1, starting transfers between devices, body(): border = lax.ppermute(edge, ('region', 'tile'), moves)  2.08 us
    pallas_call x1, Pallas kernels, body(): pl.pallas_call(own_columns_kernel, out_shape=pltpu.VMEM((tiles, 2, TILE,...  1.51 us
    pallas_call x1, Pallas kernels, body(): pl.pallas_call(prepare_kernel, out_shape=(pltpu.VMEM((7, 2, tiles, LANES)...  1.18 us
  transfers between devices with their start and end apart: 9, of which 6 were waited for; matrix products, arithmetic and copies ran while one was open for 0% of the time, Pallas kernels for 9%

profile of v4, /device:TPU:25, one launch (start us, length us, event | category | flops | bytes accessed | tf_op | source)
XLA Modules:
  0.0 45.7 jit_solution(16151282285723307597)
XLA Ops:
  0.6 1.2 %shard_map.103 = (f32[7,2,16,128]{3,2,1,0:T(8,128)S(1)}, f32[16,128]{1,0:T(8,128)S(1)}) custom-call(f32[2,4096]{1,0:T(2,128)} %refs_0_.1, f32[2,4096]{1,0:T(2,128)} %refs_1_.1, f32[1,4096]{1,0:T(1,128)} %bitcast.20, f32[1,4096]{1,0:T(1,128)} %bitcast.21, s32[16]{0:T(128)} %refs_4_.1, s32[2,16]{1,0:T(2,128)} %refs_5_.1, s32[9,2,16]{2,1,0:T(2,128)} %bitcast.22, ...), custom_call_target="tpu_custom_call" | custom-call | tf_op jit(solution)/shard_map/pallas_call | solution.py:691
  1.8 1.3 %collective-permute-start = (f32[7,2,16,128]{3,2,1,0:T(8,128)S(1)}, f32[7,2,16,128]{3,2,1,0:T(8,128)S(1)}, u32[]{:S(2)}, u32[]{:S(2)}) collective-permute-start(f32[7,2,16,128]{3,2,1,0:T(8,128)S(1)} %get-tuple-element.12.block.own_block), channel_id=1, source_target_pairs={{0,2},{1,3},{2,0},{3,1},{4,6},{5,7},{6,4},{7,5},{8,10},{9,11},{10,... | collective-permute-start | bytes 344072 | tf_op jit(solution)/shard_map/ppermute | solution.py:670
  3.1 1.2 %collective-permute-start.1 = (f32[7,2,16,128]{3,2,1,0:T(8,128)S(1)}, f32[7,2,16,128]{3,2,1,0:T(8,128)S(1)}, u32[]{:S(2)}, u32[]{:S(2)}) collective-permute-start(f32[7,2,16,128]{3,2,1,0:T(8,128)S(1)} %get-tuple-element.12.block.own_block), channel_id=1, source_target_pairs={{0,4},{1,5},{2,6},{3,7},{4,0},{5,1},{6,2},{7,3},{8,12},{9,13},{10,... | collective-permute-start | bytes 344072 | tf_op jit(solution)/shard_map/ppermute | solution.py:670
  4.3 0.2 collective-permute-start.2
  4.5 1.4 %collective-permute-done = f32[7,2,16,128]{3,2,1,0:T(8,128)S(1)} collective-permute-done((f32[7,2,16,128]{3,2,1,0:T(8,128)S(1)}, f32[7,2,16,128]{3,2,1,0:T(8,128)S(1)}, u32[]{:S(2)}, u32[]{:S(2)}) %collective-permute-start) | collective-permute-done | bytes 114720 | tf_op jit(solution)/shard_map/ppermute | solution.py:670
  5.9 1.1 %collective-permute-done.1 = f32[7,2,16,128]{3,2,1,0:T(8,128)S(1)} collective-permute-done((f32[7,2,16,128]{3,2,1,0:T(8,128)S(1)}, f32[7,2,16,128]{3,2,1,0:T(8,128)S(1)}, u32[]{:S(2)}, u32[]{:S(2)}) %collective-permute-start.1) | collective-permute-done | bytes 114720 | tf_op jit(solution)/shard_map/ppermute | solution.py:670
  7.0 2.0 %collective-permute-done.2 = f32[7,2,16,128]{3,2,1,0:T(8,128)S(1)} collective-permute-done((f32[7,2,16,128]{3,2,1,0:T(8,128)S(1)}, f32[7,2,16,128]{3,2,1,0:T(8,128)S(1)}, u32[]{:S(2)}, u32[]{:S(2)}) %collective-permute-start.2) | collective-permute-done | bytes 114720 | tf_op jit(solution)/shard_map/ppermute | solution.py:670
  9.1 2.3 %collective-permute-start.3 = (f32[4,7,2,16,128]{4,3,2,1,0:T(8,128)S(1)}, f32[4,7,2,16,128]{4,3,2,1,0:T(8,128)S(1)}, u32[]{:S(2)}, u32[]{:S(2)}) collective-permute-start(f32[4,7,2,16,128]{4,3,2,1,0:T(8,128)S(1)} %pad_maximum_fusion.same), channel_id=1, source_target_pairs={{0,1},{1,0},{2,3},{3,2},{4,5},{5,4},{6,7},{7,6},{8,9},{9,8},{10,11... | collective-permute-start | bytes 1376264 | tf_op jit(solution)/shard_map/ppermute | solution.py:670
  11.4 1.4 %collective-permute-done.3.other = f32[4,7,2,16,128]{4,3,2,1,0:T(8,128)S(1)} collective-permute-done((f32[4,7,2,16,128]{4,3,2,1,0:T(8,128)S(1)}, f32[4,7,2,16,128]{4,3,2,1,0:T(8,128)S(1)}, u32[]{:S(2)}, u32[]{:S(2)}) %collective-permute-start.3) | collective-permute-done | bytes 458784 | tf_op jit(solution)/shard_map/ppermute | solution.py:670
  12.8 0.5 %shard_map.105 = (f32[2,136,128]{2,1,0:T(8,128)S(1)}, f32[7,2,32,128]{3,2,1,0:T(8,128)S(1)}) custom-call(f32[4,7,2,16,128]{4,3,2,1,0:T(8,128)S(1)} %pad_maximum_fusion.same, f32[4,7,2,16,128]{4,3,2,1,0:T(8,128)S(1)} %collective-permute-done.3.other), custom_call_target="tpu_custom_call" | custom-call | tf_op jit(solution)/shard_map/pallas_call | solution.py:722
  13.4 2.1 %collective-permute-start.4 = (f32[2,136,128]{2,1,0:T(8,128)S(1)}, f32[2,136,128]{2,1,0:T(8,128)S(1)}, u32[]{:S(2)}, u32[]{:S(2)}) collective-permute-start(f32[2,136,128]{2,1,0:T(8,128)S(1)} %get-tuple-element.17), channel_id=1, source_target_pairs={{0,8},{2,10},{4,12},{6,14},{8,16},{9,1},{10,18},{11,3},{12,20},{13... | collective-permute-start | bytes 417800 | tf_op jit(solution)/shard_map/ppermute | solution.py:762
  15.4 2.6 %shard_map.106 = (f32[16,2,256,128]{3,2,1,0:T(8,128)S(1)}, f32[8,256,256]{2,1,0:T(8,128)S(1)}) custom-call(f32[7,2,32,128]{3,2,1,0:T(8,128)S(1)} %get-tuple-element.14.near), custom_call_target="tpu_custom_call" | custom-call | flops 4000000 | bytes 4000000 | tf_op jit(solution)/shard_map/pallas_call | solution.py:732
  18.1 0.0 collective-permute-done.4.border
  18.1 3.4 %shard_map.107 = f32[2,88,128]{2,1,0:T(8,128)S(1)} custom-call(f32[7,2,32,128]{3,2,1,0:T(8,128)S(1)} %get-tuple-element.14.near, f32[16,2,256,128]{3,2,1,0:T(8,128)S(1)} %get-tuple-element.15.near_columns, f32[8,256,256]{2,1,0:T(8,128)S(1)} %get-tuple-element.16.near_sums, f32[2,136,128]{2,1,0:T(8,128)S(1)} %collective-permute-done.4.border), custom_call_target="tpu_custom_call" | custom-call | tf_op jit(solution)/shard_map/pallas_call | solution.py:763
  21.5 2.9 %collective-permute-start.7 = (f32[2,88,128]{2,1,0:T(8,128)S(1)}, f32[2,88,128]{2,1,0:T(8,128)S(1)}, u32[]{:S(2)}, u32[]{:S(2)}) collective-permute-start(f32[2,88,128]{2,1,0:T(8,128)S(1)} %shard_map.107), channel_id=1, source_target_pairs={{0,6},{1,7},{2,4},{3,5},{4,2},{5,3},{6,0},{7,1},{8,14},{9,15},{10,... | collective-permute-start | bytes 270344 | tf_op jit(solution)/shard_map/ppermute | solution.py:670
  24.5 3.6 %collective-permute-start.5 = (f32[2,88,128]{2,1,0:T(8,128)S(1)}, f32[2,88,128]{2,1,0:T(8,128)S(1)}, u32[]{:S(2)}, u32[]{:S(2)}) collective-permute-start(f32[2,88,128]{2,1,0:T(8,128)S(1)} %shard_map.107), channel_id=1, source_target_pairs={{0,2},{1,3},{2,0},{3,1},{4,6},{5,7},{6,4},{7,5},{8,10},{9,11},{10,... | collective-permute-start | bytes 270344 | tf_op jit(solution)/shard_map/ppermute | solution.py:670
  28.1 0.0 collective-permute-start.6
  28.1 0.0 collective-permute-done.7
  28.1 2.9 %collective-permute-done.5 = f32[2,88,128]{2,1,0:T(8,128)S(1)} collective-permute-done((f32[2,88,128]{2,1,0:T(8,128)S(1)}, f32[2,88,128]{2,1,0:T(8,128)S(1)}, u32[]{:S(2)}, u32[]{:S(2)}) %collective-permute-start.5) | collective-permute-done | bytes 90144 | tf_op jit(solution)/shard_map/ppermute | solution.py:670
  31.0 1.5 %collective-permute-done.6 = f32[2,88,128]{2,1,0:T(8,128)S(1)} collective-permute-done((f32[2,88,128]{2,1,0:T(8,128)S(1)}, f32[2,88,128]{2,1,0:T(8,128)S(1)}, u32[]{:S(2)}, u32[]{:S(2)}) %collective-permute-start.6) | collective-permute-done | bytes 90144 | tf_op jit(solution)/shard_map/ppermute | solution.py:670
  32.5 4.6 %collective-permute-start.8 = (f32[4,2,88,128]{3,2,1,0:T(8,128)S(1)}, f32[4,2,88,128]{3,2,1,0:T(8,128)S(1)}, u32[]{:S(2)}, u32[]{:S(2)}) collective-permute-start(f32[4,2,88,128]{3,2,1,0:T(8,128)S(1)} %pad_maximum_fusion.1.same_b), channel_id=1, source_target_pairs={{0,1},{1,0},{2,3},{3,2},{4,5},{5,4},{6,7},{7,6},{8,9},{9,8},{10,11... | collective-permute-start | bytes 1081352 | tf_op jit(solution)/shard_map/ppermute | solution.py:670
  37.0 1.5 %shard_map.104.columns = f32[16,2,256,128]{3,2,1,0:T(8,128)S(1)} custom-call(f32[7,2,16,128]{3,2,1,0:T(8,128)S(1)} %get-tuple-element.12.block.own_block, f32[16,128]{1,0:T(8,128)S(1)} %get-tuple-element.13.mine), custom_call_target="tpu_custom_call" | custom-call | flops 4000000 | bytes 4000000 | tf_op jit(solution)/shard_map/pallas_call | solution.py:712
  38.5 0.0 collective-permute-done.8.other_b
  38.5 7.2 %shard_map.108 = (f32[2,4096]{1,0:T(2,128)}, f32[2,4096]{1,0:T(2,128)}, f32[1,4096]{1,0:T(1,128)}) custom-call(f32[7,2,16,128]{3,2,1,0:T(8,128)S(1)} %get-tuple-element.12.block.own_block, f32[16,128]{1,0:T(8,128)S(1)} %get-tuple-element.13.mine, f32[16,2,256,128]{3,2,1,0:T(8,128)S(1)} %shard_map.104.columns, ...), custom_call_target="tpu_custom_call" | custom-call | tf_op jit(solution)/shard_map/pallas_call | solution.py:788
  (2 shorter events, 0.1 us)
Async XLA Ops:
  1.8 4.1 %collective-permute-start = (f32[7,2,16,128]{3,2,1,0:T(8,128)S(1)}, f32[7,2,16,128]{3,2,1,0:T(8,128)S(1)}, u32[]{:S(2)}, u32[]{:S(2)}) collective-permute-start(f32[7,2,16,128]{3,2,1,0:T(8,128)S(1)} %get-tuple-element.12.block.own_block), channel_id=1, source_target_pairs={{0,2},{1,3},{2,0},{3,1},{4,6},{5,7},{6,4},{7,5},{8,10},{9,11},{10,... | collective-permute-start | bytes 344072 | tf_op jit(solution)/shard_map/ppermute | solution.py:670
  3.1 3.9 %collective-permute-start.1 = (f32[7,2,16,128]{3,2,1,0:T(8,128)S(1)}, f32[7,2,16,128]{3,2,1,0:T(8,128)S(1)}, u32[]{:S(2)}, u32[]{:S(2)}) collective-permute-start(f32[7,2,16,128]{3,2,1,0:T(8,128)S(1)} %get-tuple-element.12.block.own_block), channel_id=1, source_target_pairs={{0,4},{1,5},{2,6},{3,7},{4,0},{5,1},{6,2},{7,3},{8,12},{9,13},{10,... | collective-permute-start | bytes 344072 | tf_op jit(solution)/shard_map/ppermute | solution.py:670
  4.3 4.7 %collective-permute-start.2 = (f32[7,2,16,128]{3,2,1,0:T(8,128)S(1)}, f32[7,2,16,128]{3,2,1,0:T(8,128)S(1)}, u32[]{:S(2)}, u32[]{:S(2)}) collective-permute-start(f32[7,2,16,128]{3,2,1,0:T(8,128)S(1)} %get-tuple-element.12.block.own_block), channel_id=1, source_target_pairs={{0,6},{1,7},{2,4},{3,5},{4,2},{5,3},{6,0},{7,1},{8,14},{9,15},{10,... | collective-permute-start | bytes 344072 | tf_op jit(solution)/shard_map/ppermute | solution.py:670
  9.1 3.8 %collective-permute-start.3 = (f32[4,7,2,16,128]{4,3,2,1,0:T(8,128)S(1)}, f32[4,7,2,16,128]{4,3,2,1,0:T(8,128)S(1)}, u32[]{:S(2)}, u32[]{:S(2)}) collective-permute-start(f32[4,7,2,16,128]{4,3,2,1,0:T(8,128)S(1)} %pad_maximum_fusion.same), channel_id=1, source_target_pairs={{0,1},{1,0},{2,3},{3,2},{4,5},{5,4},{6,7},{7,6},{8,9},{9,8},{10,11... | collective-permute-start | bytes 1376264 | tf_op jit(solution)/shard_map/ppermute | solution.py:670
  13.4 4.7 %collective-permute-start.4 = (f32[2,136,128]{2,1,0:T(8,128)S(1)}, f32[2,136,128]{2,1,0:T(8,128)S(1)}, u32[]{:S(2)}, u32[]{:S(2)}) collective-permute-start(f32[2,136,128]{2,1,0:T(8,128)S(1)} %get-tuple-element.17), channel_id=1, source_target_pairs={{0,8},{2,10},{4,12},{6,14},{8,16},{9,1},{10,18},{11,3},{12,20},{13... | collective-permute-start | bytes 417800 | tf_op jit(solution)/shard_map/ppermute | solution.py:762
  21.5 6.6 %collective-permute-start.7 = (f32[2,88,128]{2,1,0:T(8,128)S(1)}, f32[2,88,128]{2,1,0:T(8,128)S(1)}, u32[]{:S(2)}, u32[]{:S(2)}) collective-permute-start(f32[2,88,128]{2,1,0:T(8,128)S(1)} %shard_map.107), channel_id=1, source_target_pairs={{0,6},{1,7},{2,4},{3,5},{4,2},{5,3},{6,0},{7,1},{8,14},{9,15},{10,... | collective-permute-start | bytes 270344 | tf_op jit(solution)/shard_map/ppermute | solution.py:670
  24.5 6.5 %collective-permute-start.5 = (f32[2,88,128]{2,1,0:T(8,128)S(1)}, f32[2,88,128]{2,1,0:T(8,128)S(1)}, u32[]{:S(2)}, u32[]{:S(2)}) collective-permute-start(f32[2,88,128]{2,1,0:T(8,128)S(1)} %shard_map.107), channel_id=1, source_target_pairs={{0,2},{1,3},{2,0},{3,1},{4,6},{5,7},{6,4},{7,5},{8,10},{9,11},{10,... | collective-permute-start | bytes 270344 | tf_op jit(solution)/shard_map/ppermute | solution.py:670
  28.1 4.3 %collective-permute-start.6 = (f32[2,88,128]{2,1,0:T(8,128)S(1)}, f32[2,88,128]{2,1,0:T(8,128)S(1)}, u32[]{:S(2)}, u32[]{:S(2)}) collective-permute-start(f32[2,88,128]{2,1,0:T(8,128)S(1)} %shard_map.107), channel_id=1, source_target_pairs={{0,4},{1,5},{2,6},{3,7},{4,0},{5,1},{6,2},{7,3},{8,12},{9,13},{10,... | collective-permute-start | bytes 270344 | tf_op jit(solution)/shard_map/ppermute | solution.py:670
  32.5 6.1 %collective-permute-start.8 = (f32[4,2,88,128]{3,2,1,0:T(8,128)S(1)}, f32[4,2,88,128]{3,2,1,0:T(8,128)S(1)}, u32[]{:S(2)}, u32[]{:S(2)}) collective-permute-start(f32[4,2,88,128]{3,2,1,0:T(8,128)S(1)} %pad_maximum_fusion.1.same_b), channel_id=1, source_target_pairs={{0,1},{1,0},{2,3},{3,2},{4,5},{5,4},{6,7},{7,6},{8,9},{9,8},{10,11... | collective-permute-start | bytes 1081352 | tf_op jit(solution)/shard_map/ppermute | solution.py:670
